TPU v7x, 32 devices: a whole 2x2x4 slice. The times are simulated.
32 devices in a mesh: groups: 2 (over y), seq: 4 (over z), head: 4 (over x, core).
Axes of the slice: x: 2, y: 2, z: 4, core: 2. Of those that a mesh axis runs over, the one named last changes fastest.
Arguments:
- doc_start: int32 [1024], P(('groups', 'seq')), parts along dimension 0, may hold values from 0 to 511, as said below
- q_gdn: bfloat16 [1024, 2048], P(('groups', 'seq'), 'head'), parts along dimension 0, may hold values from -6 to 6
- k_gdn: bfloat16 [1024, 2048], P(('groups', 'seq'), 'head'), parts along dimension 0, may hold values from -6 to 6
- v_gdn: bfloat16 [1024, 4096], P(('groups', 'seq'), 'head'), parts along dimension 0, may hold values from -6 to 6
- z_gdn: bfloat16 [1024, 4096], P(('groups', 'seq'), 'head'), parts along dimension 0, may hold values from -6 to 6
- beta_logit: float32 [32, 1024], P('head', ('groups', 'seq')), parts along dimension 1, may hold values from -8 to 3
- log_decay: float32 [32, 1024], P('head', ('groups', 'seq')), parts along dimension 1, may hold values from -1 to 0
- norm_weight: float32 [128], replicated, may hold values from 0.1 to 1.9
- q_attn: bfloat16 [1024, 4096], P(('groups', 'seq'), 'head'), parts along dimension 0, may hold values from -6 to 6
- k_attn: bfloat16 [1024, 512], P(('groups', 'seq')), parts along dimension 0, may hold values from -6 to 6
- v_attn: bfloat16 [1024, 512], P(('groups', 'seq')), parts along dimension 0, may hold values from -6 to 6
- gate_attn: bfloat16 [1024, 4096], P(('groups', 'seq'), 'head'), parts along dimension 0, may hold values from -6 to 6
Outputs:
- gdn_out: bfloat16 [1024, 4096], P(('groups', 'seq'), 'head'), parts along dimension 0
- attn_out: bfloat16 [1024, 4096], P(('groups', 'seq'), 'head'), parts along dimension 0
There are 2 independent parts, one for each index of `groups`. A program takes and returns all parts, laid end to end along the dimension named above; an argument that names none is the same for every part. Nothing has to cross between parts.
Inputs may be any that keep to these rules, and one draw needn't show every extreme that they name: Nondecreasing; doc_start[i] <= i, with equality exactly at the first token of each of the 3 documents; the first document starts at 0.
All inputs are finite; a program needn't handle non-finite values.
Results may differ from a plain program's by a relative error of at most 0.0095.
Values may be sent and summed in bfloat16 or wider, within the bound.
No kernel may reach another device: no remote copies, remote signals or barrier semaphores. Data moves between devices by JAX's collectives and lax.ppermute only.
A program may use at most 128 MiB of HBM per device.

v0:
```python
import jax
import jax.numpy as jnp
from jax import lax
from jax.sharding import PartitionSpec as P

DK = 128
DV = 128
QH = 16
KVH = 2
HD_A = 256
BLOCK = 64


HIGH = lax.Precision.HIGHEST


def shifted(shard, axis, by):
    length = lax.axis_size(axis)
    pairs = [(i, i + by) for i in range(length) if 0 <= i + by < length]
    return lax.ppermute(shard, axis, pairs)


def unit_rows(values):
    return values * lax.rsqrt(jnp.sum(values * values, axis=-1, keepdims=True) + 1e-06)


def blocked(values, count):
    length, heads, width = values.shape
    return values.reshape(count, length // count, heads, width).transpose(0, 2, 1, 3)


def block_terms(anchor, doc_block, query, keys, values, beta, log_gate):
    width = query.shape[1]
    running = jnp.cumsum(log_gate, axis=1)
    place = anchor + jnp.arange(width, dtype=jnp.int32)
    causal = place[None, :] <= place[:, None]
    same = causal & (doc_block[:, None] <= place[None, :])
    strict = same & (place[None, :] < place[:, None])
    spread = jnp.where(same[None], running[:, :, None] - running[:, None, :], 0.0)
    decay = jnp.where(same[None], jnp.exp(spread), 0.0)
    alive = (doc_block < anchor).astype(jnp.float32)
    entry = jnp.exp(running) * alive[None, :]
    gram = jnp.einsum("hik,hjk->hij", keys, keys, precision=HIGH)
    lower_part = jnp.where(strict[None], decay * gram, 0.0)
    system = jnp.eye(width, dtype=jnp.float32)[None] + beta[:, :, None] * lower_part
    right = jnp.concatenate([beta[:, :, None] * values, (beta * entry)[:, :, None] * keys], axis=2)
    solved = lax.linalg.triangular_solve(
        system, right, left_side=True, lower=True, unit_diagonal=True
    )
    fresh = solved[:, :, : values.shape[2]]
    erased = solved[:, :, values.shape[2] :]
    scores = jnp.einsum("hik,hjk->hij", query, keys, precision=HIGH) * decay
    local_out = jnp.einsum("hij,hjv->hiv", scores, fresh, precision=HIGH)
    reach = entry[:, :, None] * query - jnp.einsum("hij,hjk->hik", scores, erased, precision=HIGH)
    tail_keys = decay[:, -1, :, None] * keys
    identity = jnp.eye(keys.shape[2], dtype=jnp.float32)
    carry_map = entry[:, -1, None, None] * identity[None] - jnp.einsum(
        "hjk,hjl->hkl", erased, tail_keys, precision=HIGH
    )
    carry_add = jnp.einsum("hjv,hjk->hvk", fresh, tail_keys, precision=HIGH)
    return (local_out, reach, carry_map, carry_add)


def compose(earlier, later):
    joined_map = jnp.einsum("hkl,hlm->hkm", earlier[0], later[0], precision=HIGH)
    joined_add = jnp.einsum("hvl,hlm->hvm", earlier[1], later[0], precision=HIGH) + later[1]
    return (joined_map, joined_add)


def entering_state(device_map, device_add):

    def relay(turn, pair):
        incoming, state = pair
        incoming = shifted(state.astype(jnp.bfloat16), "seq", 1).astype(state.dtype)
        state = jnp.einsum("hvk,hkl->hvl", incoming, device_map, precision=HIGH) + device_add
        return (incoming, state)

    start_state, _ = lax.fori_loop(
        0, lax.axis_size("seq") - 1, relay, (jnp.zeros_like(device_add), device_add)
    )
    return start_state


def delta_layer(doc_start, q_gdn, k_gdn, v_gdn, z_gdn, beta_logit, log_decay, norm_weight, anchor):
    length = q_gdn.shape[0]
    key_heads = q_gdn.shape[1] // DK
    value_heads = v_gdn.shape[1] // DV
    repeat = value_heads // key_heads
    count = length // BLOCK
    query = jnp.repeat(
        unit_rows(q_gdn.astype(jnp.float32).reshape(length, key_heads, DK)), repeat, axis=1
    )
    keys = jnp.repeat(
        unit_rows(k_gdn.astype(jnp.float32).reshape(length, key_heads, DK)), repeat, axis=1
    )
    values = v_gdn.astype(jnp.float32).reshape(length, value_heads, DV)
    beta = jax.nn.sigmoid(beta_logit).reshape(value_heads, count, BLOCK).transpose(1, 0, 2)
    log_gate = log_decay.reshape(value_heads, count, BLOCK).transpose(1, 0, 2)
    docs = doc_start.reshape(count, BLOCK)
    anchors = anchor + BLOCK * jnp.arange(count, dtype=jnp.int32)
    identity = jnp.broadcast_to(jnp.eye(DK, dtype=jnp.float32), (value_heads, DK, DK))

    def sweep(totals, inputs):
        total_map, total_add = totals
        block_anchor, doc_block, q_block, k_block, v_block, b_block, g_block = inputs
        local_out, reach, carry_map, carry_add = block_terms(
            block_anchor, doc_block, q_block, k_block, v_block, b_block, g_block
        )
        joined = compose((total_map, total_add), (carry_map, carry_add))
        return (joined, (local_out, reach, total_map, total_add))

    start_totals = (identity, jnp.zeros((value_heads, DV, DK), jnp.float32))
    scanned = (
        anchors,
        docs,
        blocked(query, count),
        blocked(keys, count),
        blocked(values, count),
        beta,
        log_gate,
    )
    (device_map, device_add), (local_out, reach, prefix_map, prefix_add) = lax.scan(
        sweep, start_totals, scanned
    )
    start_state = entering_state(device_map, device_add)
    block_state = jnp.einsum("hvk,chkl->chvl", start_state, prefix_map, precision=HIGH) + prefix_add
    mixed = local_out + jnp.einsum("chik,chvk->chiv", reach, block_state, precision=HIGH)
    mixed = mixed.transpose(0, 2, 1, 3).reshape(length, value_heads, DV)
    gate = z_gdn.astype(jnp.float32).reshape(length, value_heads, DV)
    factor = lax.rsqrt(jnp.mean(mixed * mixed, axis=-1, keepdims=True) + 1e-06)
    normed = mixed * factor * norm_weight * jax.nn.silu(gate)
    return normed.reshape(length, value_heads * DV).astype(jnp.bfloat16)


def attend(doc_start, q_attn, k_attn, v_attn, gate_attn, anchor):
    length = q_attn.shape[0]
    local_heads = q_attn.shape[1] // HD_A
    group = QH // KVH
    shards_seen = lax.axis_size("seq") // 2 + 1
    window_size = shards_seen * length
    kv_head = lax.axis_index("head") * local_heads // group
    keys_own = lax.dynamic_slice_in_dim(k_attn, kv_head * HD_A, HD_A, 1)
    values_own = lax.dynamic_slice_in_dim(v_attn, kv_head * HD_A, HD_A, 1)
    query = q_attn.reshape(length, local_heads, HD_A)
    q_place = anchor + jnp.arange(length, dtype=jnp.int32)
    lower = jnp.maximum(doc_start, q_place - window_size + 1)
    lowest = jnp.min(lower)
    highest = anchor + length - 1
    factor = HD_A ** (-0.5)
    initial = (
        jnp.full((local_heads, length), -1e30, jnp.float32),
        jnp.zeros((local_heads, length), jnp.float32),
        jnp.zeros((local_heads, length, HD_A), jnp.float32),
    )
    key_piece = lax.all_gather(keys_own, "seq", axis=0, tiled=True)
    value_piece = lax.all_gather(values_own, "seq", axis=0, tiled=True)
    count = key_piece.shape[0]
    width = count
    while width > 1024 and width % 2 == 0:
        width = width // 2

    def one(index, inner):
        begin = index * width
        key_part = lax.dynamic_slice_in_dim(key_piece, begin, width, 0)
        value_part = lax.dynamic_slice_in_dim(value_piece, begin, width, 0)
        k_place = begin + jnp.arange(width, dtype=jnp.int32)

        def compute(state):
            peak, total, accum = state
            scores = (
                jnp.einsum("qhd,kd->hqk", query, key_part, preferred_element_type=jnp.float32)
                * factor
            )
            visible = (k_place[None, :] >= lower[:, None]) & (k_place[None, :] <= q_place[:, None])
            masked = jnp.where(visible[None], scores, -jnp.inf)
            new_peak = jnp.maximum(peak, jnp.max(masked, axis=-1))
            weights = jnp.exp(masked - new_peak[:, :, None])
            shrink = jnp.exp(peak - new_peak)
            total = total * shrink + jnp.sum(weights, axis=-1)
            update = jnp.einsum(
                "hqk,kd->hqd",
                weights.astype(jnp.bfloat16),
                value_part,
                preferred_element_type=jnp.float32,
            )
            accum = accum * shrink[:, :, None] + update
            return (new_peak, total, accum)

        def unchanged(state):
            return state

        busy = (begin <= highest) & (begin + width - 1 >= lowest)
        return lax.cond(busy, compute, unchanged, inner)

    peak, total, accum = lax.fori_loop(0, count // width, one, initial)
    mixed = (accum / total[:, :, None]).transpose(1, 0, 2).reshape(length, local_heads * HD_A)
    return (mixed * jax.nn.sigmoid(gate_attn.astype(jnp.float32))).astype(jnp.bfloat16)


def shards(
    doc_start,
    q_gdn,
    k_gdn,
    v_gdn,
    z_gdn,
    beta_logit,
    log_decay,
    norm_weight,
    q_attn,
    k_attn,
    v_attn,
    gate_attn,
):
    anchor = lax.axis_index("seq") * q_gdn.shape[0]
    gdn_out = delta_layer(
        doc_start, q_gdn, k_gdn, v_gdn, z_gdn, beta_logit, log_decay, norm_weight, anchor
    )
    attn_out = attend(doc_start, q_attn, k_attn, v_attn, gate_attn, anchor)
    return (gdn_out, attn_out)


def solution(mesh):
    return jax.shard_map(
        shards,
        mesh=mesh,
        in_specs=(
            P(("groups", "seq")),
            P(("groups", "seq"), "head"),
            P(("groups", "seq"), "head"),
            P(("groups", "seq"), "head"),
            P(("groups", "seq"), "head"),
            P("head", ("groups", "seq")),
            P("head", ("groups", "seq")),
            P(),
            P(("groups", "seq"), "head"),
            P(("groups", "seq"), None),
            P(("groups", "seq"), None),
            P(("groups", "seq"), "head"),
        ),
        out_specs=(P(("groups", "seq"), "head"), P(("groups", "seq"), "head")),
        check_vma=False,
    )
```

profile of v0, /device:TPU:26, one launch (start us, length us, event | category | flops | bytes accessed | tf_op | source)
XLA Modules:
  0.0 187.5 jit_solution(7092509554987152704)
XLA Ops:
  0.7 1.0 reshape.347
  2.2 0.9 copy-done.16
  3.7 0.9 copy-done.13
  4.7 0.8 bitcast_bitcast_fusion
  5.7 0.6 copy-done.19
  7.1 0.7 copy-done.21
  7.8 105.6 %while.13 = (s32[]{:T(128)}, f32[8,128,128]{1,2,0:T(8,128)S(1)}, f32[8,128,128]{1,2,0:T(8,128)S(1)}, f32[2,8,64,128]{3,2,1,0:T(8,128)}, f32[2,8,64,128]{3,2,1,0:...) while((s32[]{:T(128)}, f32[8,128,128]{1,2,0:T(8,128)S(1)}, ...), condition=%wide.region_4.5_spmd.clone, body=%wide.region_2.4_spmd.clone.sunk | while | flops 907780864 | bytes 40192524 | solution.py:122
  8.4 0.6 iota_add_fusion.5
  10.1 39.3 %custom-call.11 = f32[8,1,64,64]{2,3,1,0:T(8,128)S(1)} custom-call(f32[8,1,64,64]{3,2,1,0:T(8,128)S(1)} %fusion.124), custom_call_target="InvertDiagBlocksLowerTriangular" | custom-call | tf_op jit(solution)/shard_map/while/body/eval_jaxpr/triangular_solve | solution.py:47
  49.4 0.7 fusion.120
  50.3 1.0 constant_dynamic-slice_fusion.9
  51.4 0.6 fusion.125
  52.4 1.1 convolution_subtract_fusion.3
  53.5 1.0 convolution_bitcast_fusion.7
  55.2 1.1 convolution_add_fusion.7
  56.3 1.0 convolution_bitcast_fusion.6
  59.8 0.8 copy-done.8
  61.2 0.6 iota_add_fusion.5
  62.9 39.3 %custom-call.11 = f32[8,1,64,64]{2,3,1,0:T(8,128)S(1)} custom-call(f32[8,1,64,64]{3,2,1,0:T(8,128)S(1)} %fusion.124), custom_call_target="InvertDiagBlocksLowerTriangular" | custom-call | tf_op jit(solution)/shard_map/while/body/eval_jaxpr/triangular_solve | solution.py:47
  102.2 0.7 fusion.120
  103.1 1.0 constant_dynamic-slice_fusion.9
  105.2 1.1 convolution_subtract_fusion.3
  106.3 1.0 convolution_bitcast_fusion.7
  108.0 1.1 convolution_add_fusion.7
  109.1 1.0 convolution_bitcast_fusion.6
  112.7 0.8 copy-done.8
  113.6 0.7 convert.19
  114.6 33.9 %while.12 = (s32[]{:T(128)}, f32[8,128,128]{2,1,0:T(8,128)}, bf16[8,128,128]{2,1,0:T(8,128)(2,1)}, f32[8,128,128]{2,1,0:T(8,128)S(1)}, f32[8,128,128]{2,1,0:T(8,128)S(1)}, /*index=5*/s32[]{:T(128)}) while((s32[]{:T(128)}, f32[8,128,128]{2,1,0:T(8,128)}, bf16[8,128,128]{2,1,0:T(8,128)(2,1)}, f32[8,128,128]{2,1,0:T(8,128)S(1)}, ...), condition=%wide.region_6.7_spmd, body=%wide.region_5.6_spmd.sunk | while | flops 201719808 | bytes 3407981 | solution.py:78
  114.6 1.4 collective-permute-start
  116.1 8.9 %collective-permute-done = bf16[8,128,128]{2,1,0:T(8,128)(2,1)S(1)} collective-permute-done((bf16[8,128,128]{2,1,0:T(8,128)(2,1)}, bf16[8,128,128]{2,1,0:T(8,128)(2,1)S(1)}, u32[]{:S(2)}, u32[]{:S(2)}) %collective-permute-start) | collective-permute-done | bytes 262176 | tf_op jit(solution)/shard_map/while/body/eval_jaxpr/ppermute | solution.py:20
  124.9 0.8 convert_element_type.81
  125.8 1.1 convolution_add_fusion.6
  126.9 1.3 collective-permute-start
  128.2 8.0 %collective-permute-done = bf16[8,128,128]{2,1,0:T(8,128)(2,1)S(1)} collective-permute-done((bf16[8,128,128]{2,1,0:T(8,128)(2,1)}, bf16[8,128,128]{2,1,0:T(8,128)(2,1)S(1)}, u32[]{:S(2)}, u32[]{:S(2)}) %collective-permute-start) | collective-permute-done | bytes 262176 | tf_op jit(solution)/shard_map/while/body/eval_jaxpr/ppermute | solution.py:20
  136.1 0.8 convert_element_type.81
  137.0 1.1 convolution_add_fusion.6
  138.1 1.3 collective-permute-start
  139.4 7.2 %collective-permute-done = bf16[8,128,128]{2,1,0:T(8,128)(2,1)S(1)} collective-permute-done((bf16[8,128,128]{2,1,0:T(8,128)(2,1)}, bf16[8,128,128]{2,1,0:T(8,128)(2,1)S(1)}, u32[]{:S(2)}, u32[]{:S(2)}) %collective-permute-start) | collective-permute-done | bytes 262176 | tf_op jit(solution)/shard_map/while/body/eval_jaxpr/ppermute | solution.py:20
  146.5 0.8 convert_element_type.81
  147.4 1.1 convolution_add_fusion.6
  148.5 2.2 %fusion.53 = f32[2,8,128,128]{2,3,1,0:T(8,128)S(1)} fusion(f32[2,8,128,128]{2,3,1,0:T(8,128)S(1)} %copy-done.6, f32[2,8,128,128]{2,3,1,0:T(8,128)S(1)} %copy-done.3, f32[8,128,128]{2,1,0:T(8,128)} %get-tuple-element.215), kind=kOutput, calls=%fused_computation.91 | convolution fusion | flops 402915328 | bytes 3670016 | tf_op jit(solution)/shard_map/hvk,chkl->chvl/dot_general | solution.py:126
  150.7 1.1 multiply_reduce_fusion
  153.2 1.0 fusion.61
  154.2 14.0 %all_gather.6 = bf16[512,256]{1,0:T(8,128)(2,1)S(1)} all-gather(bf16[128,256]{1,0:T(8,128)(2,1)S(1)} %constant_dynamic-slice_fusion.5), channel_id=1, replica_groups=mesh['groups'=2,'seq'=4,'head'=4] {'seq'}, dimensions={0}, use_global_device_ids=true | all-gather | bytes 327680 | tf_op jit(solution)/shard_map/all_gather | solution.py:155
  168.2 14.6 %all_gather.7 = bf16[512,256]{1,0:T(8,128)(2,1)S(1)} all-gather(bf16[128,256]{1,0:T(8,128)(2,1)S(1)} %constant_dynamic-slice_fusion.4), channel_id=1, replica_groups=mesh['groups'=2,'seq'=4,'head'=4] {'seq'}, dimensions={0}, use_global_device_ids=true | all-gather | bytes 327680 | tf_op jit(solution)/shard_map/all_gather | solution.py:156
  184.4 1.2 conditional.1
  185.8 0.9 copy-done.15
  186.7 0.8 multiply_convert_fusion
  (143 shorter events, 17.2 us)
Async XLA Ops:
  0.6 153.5 %copy-start = (bf16[128,512]{1,0:T(8,128)(2,1)S(1)}, bf16[128,512]{1,0:T(8,128)(2,1)}, u32[]{:S(2)}) copy-start(bf16[128,512]{1,0:T(8,128)(2,1)} %param.27) | copy-start | bytes 393220
  2.2 0.9 copy-start.16
  3.6 1.0 copy-start.13
  5.6 0.7 copy-start.19
  6.3 0.7 copy-start.18
  7.1 0.7 copy-start.21
  53.5 1.2 copy-start.1
  53.5 1.5 copy-start.4
  55.2 2.2 %copy-start.2 = (f32[2,8,128,128]{2,3,1,0:T(8,128)}, f32[2,8,128,128]{2,3,1,0:T(8,128)S(1)}, u32[]{:S(2)}) copy-start(f32[2,8,128,128]{2,3,1,0:T(8,128)S(1)} %get-tuple-element.561) | copy-start | bytes 3145732 | tf_op jit(solution)/shard_map/while
  55.2 2.2 %copy-start.5 = (f32[2,8,128,128]{2,3,1,0:T(8,128)}, f32[2,8,128,128]{2,3,1,0:T(8,128)S(1)}, u32[]{:S(2)}) copy-start(f32[2,8,128,128]{2,3,1,0:T(8,128)S(1)} %get-tuple-element.562) | copy-start | bytes 3145732 | tf_op jit(solution)/shard_map/while
  57.3 1.0 copy-start.10
  58.4 1.0 copy-start.7
  58.8 1.0 copy-start.11
  59.8 0.8 copy-start.8
  106.3 1.2 copy-start.1
  106.3 1.5 copy-start.4
  108.0 2.2 %copy-start.2 = (f32[2,8,128,128]{2,3,1,0:T(8,128)}, f32[2,8,128,128]{2,3,1,0:T(8,128)S(1)}, u32[]{:S(2)}) copy-start(f32[2,8,128,128]{2,3,1,0:T(8,128)S(1)} %get-tuple-element.561) | copy-start | bytes 3145732 | tf_op jit(solution)/shard_map/while
  108.0 2.2 %copy-start.5 = (f32[2,8,128,128]{2,3,1,0:T(8,128)}, f32[2,8,128,128]{2,3,1,0:T(8,128)S(1)}, u32[]{:S(2)}) copy-start(f32[2,8,128,128]{2,3,1,0:T(8,128)S(1)} %get-tuple-element.562) | copy-start | bytes 3145732 | tf_op jit(solution)/shard_map/while
  110.2 1.0 copy-start.10
  111.2 1.0 copy-start.7
  111.6 1.0 copy-start.11
  112.6 0.8 copy-start.8
  114.6 33.9 %copy-start.3 = (f32[2,8,128,128]{2,3,1,0:T(8,128)S(1)}, f32[2,8,128,128]{2,3,1,0:T(8,128)}, u32[]{:S(2)}) copy-start(f32[2,8,128,128]{2,3,1,0:T(8,128)} %get-tuple-element.212) | copy-start | bytes 3145732
  114.6 33.9 %copy-start.6 = (f32[2,8,128,128]{2,3,1,0:T(8,128)S(1)}, f32[2,8,128,128]{2,3,1,0:T(8,128)}, u32[]{:S(2)}) copy-start(f32[2,8,128,128]{2,3,1,0:T(8,128)} %get-tuple-element.216) | copy-start | bytes 3145732
  114.6 10.3 %collective-permute-start = (bf16[8,128,128]{2,1,0:T(8,128)(2,1)}, bf16[8,128,128]{2,1,0:T(8,128)(2,1)S(1)}, u32[]{:S(2)}, u32[]{:S(2)}) collective-permute-start(bf16[8,128,128]{2,1,0:T(8,128)(2,1)} %get-tuple-element.581), channel_id=1, source_target_pairs={{0,4},{4,8},{8,12},{1,5},{5,9},{9,13},{2,6},{6,10},{10,14},{3,7},{... | collective-permute-start | bytes 786440 | tf_op jit(solution)/shard_map/while/body/eval_jaxpr/ppermute | solution.py:20
  126.9 9.3 %collective-permute-start = (bf16[8,128,128]{2,1,0:T(8,128)(2,1)}, bf16[8,128,128]{2,1,0:T(8,128)(2,1)S(1)}, u32[]{:S(2)}, u32[]{:S(2)}) collective-permute-start(bf16[8,128,128]{2,1,0:T(8,128)(2,1)} %get-tuple-element.581), channel_id=1, source_target_pairs={{0,4},{4,8},{8,12},{1,5},{5,9},{9,13},{2,6},{6,10},{10,14},{3,7},{... | collective-permute-start | bytes 786440 | tf_op jit(solution)/shard_map/while/body/eval_jaxpr/ppermute | solution.py:20
  138.1 8.5 %collective-permute-start = (bf16[8,128,128]{2,1,0:T(8,128)(2,1)}, bf16[8,128,128]{2,1,0:T(8,128)(2,1)S(1)}, u32[]{:S(2)}, u32[]{:S(2)}) collective-permute-start(bf16[8,128,128]{2,1,0:T(8,128)(2,1)} %get-tuple-element.581), channel_id=1, source_target_pairs={{0,4},{4,8},{8,12},{1,5},{5,9},{9,13},{2,6},{6,10},{10,14},{3,7},{... | collective-permute-start | bytes 786440 | tf_op jit(solution)/shard_map/while/body/eval_jaxpr/ppermute | solution.py:20
  148.5 2.2 %copy-start.9 = (f32[2,8,64,128]{3,2,1,0:T(8,128)S(1)}, f32[2,8,64,128]{3,2,1,0:T(8,128)}, u32[]{:S(2)}) copy-start(f32[2,8,64,128]{3,2,1,0:T(8,128)} %get-tuple-element.210) | copy-start | bytes 1572868
  148.5 2.2 %copy-start.12 = (f32[2,8,64,128]{3,2,1,0:T(8,128)S(1)}, f32[2,8,64,128]{3,2,1,0:T(8,128)}, u32[]{:S(2)}) copy-start(f32[2,8,64,128]{3,2,1,0:T(8,128)} %get-tuple-element.211) | copy-start | bytes 1572868
  152.2 1.0 copy-start.14
  152.5 0.7 copy-start.20
  154.2 14.0 %copy-start.17 = (bf16[128,512]{1,0:T(8,128)(2,1)S(1)}, bf16[128,512]{1,0:T(8,128)(2,1)}, u32[]{:S(2)}) copy-start(bf16[128,512]{1,0:T(8,128)(2,1)} %param.28) | copy-start | bytes 393220
  183.4 0.9 copy-start.22
  185.7 1.0 copy-start.15
where the time goes:
time: 190 us; the launch traced here: 188 us
  other arithmetic  90.3 us (48%)
  blocking collectives  28.6 us (15%)
  waiting for transfers between devices  24 us (13%)
  matrix products  21.1 us (11%)
  local copies, waits for them, and re-layouts  17.3 us (9%)
  starting transfers between devices  3.98 us (2%)
    another operation x6, other arithmetic, block_terms(): lax.linalg.triangular_solve(system, right, left_side=True, lower=True, un...  78.8 us
    ppermute x3, waiting for transfers between devices, shifted(): return lax.ppermute(shard, axis, pairs)  24 us
    all_gather x1, blocking collectives, attend(): value_piece = lax.all_gather(values_own, 'seq', axis=0, tiled=True)  14.6 us
    all_gather x1, blocking collectives, attend(): key_piece = lax.all_gather(keys_own, 'seq', axis=0, tiled=True)  14 us
    unnamed x31, local copies, waits for them, and re-layouts  5.57 us
    while x34, local copies, waits for them, and re-layouts  4.79 us
    ppermute x3, starting transfers between devices, shifted(): return lax.ppermute(shard, axis, pairs)  3.98 us
  transfers between devices with their start and end apart: 3, of which 3 were waited for; matrix products, arithmetic and copies ran while one was open for 0% of the time, Pallas kernels for 0%

commit v1 on v0

v1 whole, which is shorter than its diff:
```python
import functools

import jax
import jax.numpy as jnp
from jax import lax
from jax.experimental import pallas as pl
from jax.experimental.pallas import tpu as pltpu
from jax.sharding import PartitionSpec as P

DK = 128
DV = 128
QH = 16
KVH = 2
HD_A = 256
EPS = 1e-06
VMEM_LIMIT = 48 * 1024 * 1024

F32 = jnp.float32
BF16 = jnp.bfloat16


def dot(a, b):
    return jnp.dot(a, b, preferred_element_type=F32)


def dot_t(a, b):
    return lax.dot_general(a, b, (((1,), (1,)), ((), ())), preferred_element_type=F32)


def prefix_sums(rows):
    count, length = rows.shape
    first = rows.astype(BF16)
    rest = rows - first.astype(F32)
    second = rest.astype(BF16)
    third = (rest - second.astype(F32)).astype(BF16)
    t_at = lax.broadcasted_iota(jnp.int32, (length, length), 0)
    i_at = lax.broadcasted_iota(jnp.int32, (length, length), 1)
    ones = (t_at <= i_at).astype(F32).astype(BF16)
    return dot(first, ones) + dot(second, ones) + dot(third, ones)


def columns_of(rows):
    count, length = rows.shape
    padded = jnp.concatenate([rows, jnp.zeros((length - count, length), F32)], axis=0)
    return padded.T


def diagonal_row(square, same_place):
    return jnp.sum(jnp.where(same_place, square, 0.0), axis=0, keepdims=True)


def places(length):
    row = lax.broadcasted_iota(jnp.int32, (length, length), 0)
    col = lax.broadcasted_iota(jnp.int32, (length, length), 1)
    return row, col


def state_kernel(anchor_ref, doc_ref, beta_ref, gate_ref, k_ref, v_ref, x_ref, u_ref, a_ref, send_ref):
    length = k_ref.shape[0]
    heads = beta_ref.shape[0]
    key_heads = k_ref.shape[1] // DK
    repeat = heads // key_heads
    anchor = anchor_ref[0]
    row, col = places(length)
    beta = jax.nn.sigmoid(beta_ref[...])
    running = prefix_sums(gate_ref[...])
    doc = doc_ref[...]
    keys = [k_ref[:, g * DK : (g + 1) * DK] for g in range(key_heads)]
    grams = [dot_t(k, k) for k in keys]
    squares = [diagonal_row(g, row == col) + EPS for g in grams]
    log_inv = [-0.5 * jnp.log(s) for s in squares]
    inv = [lax.rsqrt(s) for s in squares]
    log_rows = jnp.concatenate([log_inv[h // repeat] for h in range(heads)], axis=0)
    cols = columns_of(
        jnp.concatenate([running + log_rows, jnp.broadcast_to(doc.astype(F32), (8, length))], axis=0)
    )
    doc_col = cols[:, heads : heads + 1]
    place = (anchor + col).astype(F32)
    strict = (doc_col <= place) & (col < row)
    tail_same = doc[:, length - 1 : length] <= (anchor + col[:1, :])
    systems = []
    for h in range(heads):
        spread = cols[:, h : h + 1] - running[h : h + 1, :]
        decay = jnp.where(strict, jnp.exp(spread), 0.0)
        weight = beta[h : h + 1, :] * inv[h // repeat]
        systems.append((decay * grams[h // repeat] * weight).astype(F32))
    differ = row ^ col
    inverse = [jnp.where(row == col, 1.0, 0.0) - jnp.where(differ == 1, n, 0.0) for n in systems]
    level = 1
    while (1 << level) < length:
        mask = (differ >> level) == 1
        short = [x.astype(BF16) for x in inverse]
        inner = [
            dot(jnp.where(mask, n, 0.0).astype(BF16), x).astype(BF16) for n, x in zip(systems, short)
        ]
        inverse = [x - dot(s, y) for x, s, y in zip(inverse, short, inner)]
        level += 1
    keys_t = [k.astype(F32).T for k in keys]
    for h in range(heads):
        x = inverse[h].astype(BF16)
        x_ref[h] = x
        u = dot(x, v_ref[:, h * DV : (h + 1) * DV]).astype(BF16)
        u_ref[h] = u
        tail = jnp.exp(running[h : h + 1, length - 1 : length] - running[h : h + 1, :])
        tail = jnp.where(tail_same, tail, 0.0) * beta[h : h + 1, :] * inv[h // repeat]
        a = dot((keys_t[h // repeat] * tail).astype(BF16), u)
        a_ref[h] = a
        send_ref[h] = a.astype(BF16)


def query_kernel(
    anchor_ref, doc_ref, beta_ref, gate_ref, q_ref, k_ref, z_ref, w_ref, x_ref, u_ref, m_ref, local_ref, reach_ref, gz_ref
):
    length = k_ref.shape[0]
    heads = beta_ref.shape[0]
    key_heads = k_ref.shape[1] // DK
    repeat = heads // key_heads
    anchor = anchor_ref[0]
    row, col = places(length)
    beta = jax.nn.sigmoid(beta_ref[...])
    running = prefix_sums(gate_ref[...])
    doc = doc_ref[...]
    keys = [k_ref[:, g * DK : (g + 1) * DK] for g in range(key_heads)]
    queries = [q_ref[:, g * DK : (g + 1) * DK] for g in range(key_heads)]
    inv = [lax.rsqrt(diagonal_row(dot_t(k, k), row == col) + EPS) for k in keys]
    log_q = [-0.5 * jnp.log(diagonal_row(dot_t(q, q), row == col) + EPS) for q in queries]
    log_rows = jnp.concatenate([log_q[h // repeat] for h in range(heads)], axis=0)
    alive = doc < (anchor + col[:1, :])
    alive = doc < anchor
    cols = columns_of(
        jnp.concatenate([running + log_rows, jnp.broadcast_to(doc.astype(F32), (8, length))], axis=0)
    )
    doc_col = cols[:, heads : heads + 1]
    place = (anchor + col).astype(F32)
    same = (doc_col <= place) & (col <= row)
    alive_col = doc_col < anchor.astype(F32)
    tail_same = doc[:, length - 1 : length] <= (anchor + col[:1, :])
    cross = [dot_t(q, k) for q, k in zip(queries, keys)]
    keys_t = [k.astype(F32).T for k in keys]
    for h in range(heads):
        g = h // repeat
        run = running[h : h + 1, :]
        entry = jnp.where(alive, jnp.exp(run), 0.0)
        w = dot((x_ref[h].astype(F32) * (entry * inv[g])).astype(BF16), keys[g]).astype(BF16)
        weight = beta[h : h + 1, :] * inv[g]
        decay = jnp.where(same, jnp.exp(cols[:, h : h + 1] - run), 0.0)
        scores = (decay * cross[g] * weight).astype(BF16)
        local_ref[h] = dot(scores, u_ref[h])
        lead = jnp.where(alive_col, jnp.exp(cols[:, h : h + 1]), 0.0)
        reach_ref[h] = (lead * queries[g].astype(F32) - dot(scores, w)).astype(BF16)
        tail = jnp.exp(run[:, length - 1 : length] - run)
        tail = jnp.where(tail_same, tail, 0.0) * weight
        carried = dot((keys_t[g] * tail).astype(BF16), w)
        m_ref[h] = (jnp.where(row == col, entry[:, length - 1 : length], 0.0) - carried).astype(BF16)
    z = z_ref[...].astype(F32)
    gain = z / (1.0 + jnp.exp(-z))
    for h in range(heads):
        gz_ref[h] = gain[:, h * DV : (h + 1) * DV] * w_ref[...]


def combine_kernel(s_ref, m_ref, a_ref, out_ref):
    for h in range(s_ref.shape[0]):
        out_ref[h] = (dot(m_ref[h], s_ref[h]) + a_ref[h]).astype(BF16)


def output_kernel(count, *refs):
    states = refs[:count]
    local_ref, reach_ref, gz_ref, out_ref = refs[count:]
    for h in range(local_ref.shape[0]):
        state = states[0][h]
        for other in states[1:]:
            state = state + other[h]
        mixed = local_ref[h] + dot(reach_ref[h], state)
        factor = lax.rsqrt(jnp.mean(mixed * mixed, axis=-1, keepdims=True) + EPS)
        out_ref[:, h * DV : (h + 1) * DV] = (mixed * factor * gz_ref[h]).astype(BF16)


def attention_kernel(span, window, anchor_ref, doc_ref, q_ref, gate_ref, k_ref, v_ref, out_ref):
    length = q_ref.shape[0]
    heads = q_ref.shape[1] // HD_A
    anchor = anchor_ref[0]
    total_keys = k_ref.shape[0]
    begin = jnp.clip(anchor + length - span, 0, total_keys - span)
    begin = pl.multiple_of(begin, length)
    keys = k_ref[pl.ds(begin, span), :]
    values = v_ref[pl.ds(begin, span), :]
    docs = jnp.broadcast_to(doc_ref[...].astype(F32), (length, length)).T[:, :1].astype(jnp.int32)
    q_place = anchor + lax.broadcasted_iota(jnp.int32, (length, 1), 0)
    lower = jnp.maximum(docs, q_place - window + 1)
    k_place = begin + lax.broadcasted_iota(jnp.int32, (length, span), 1)
    visible = (k_place >= lower) & (k_place <= q_place)
    for h in range(heads):
        part = slice(h * HD_A, (h + 1) * HD_A)
        scores = dot_t(q_ref[:, part], keys) * (HD_A**-0.5)
        scores = jnp.where(visible, scores, -jnp.inf)
        peak = jnp.max(scores, axis=-1, keepdims=True)
        weights = jnp.exp(scores - peak)
        total = jnp.sum(weights, axis=-1, keepdims=True)
        mixed = dot(weights.astype(BF16), values) / total
        out_ref[:, part] = (mixed * jax.nn.sigmoid(gate_ref[:, part].astype(F32))).astype(BF16)


def call(kernel, out_shape, operands, flops, scalars=1):
    moved = sum(o.size * o.dtype.itemsize for o in operands)
    specs = [pl.BlockSpec(memory_space=pltpu.SMEM)] * scalars
    specs += [pl.BlockSpec(memory_space=pltpu.VMEM)] * (len(operands) - scalars)
    return pl.pallas_call(
        kernel,
        out_shape=out_shape,
        in_specs=specs,
        out_specs=jax.tree.map(lambda _: pl.BlockSpec(memory_space=pltpu.VMEM), out_shape),
        compiler_params=pltpu.CompilerParams(vmem_limit_bytes=VMEM_LIMIT),
        cost_estimate=pl.CostEstimate(flops=flops, bytes_accessed=moved, transcendentals=0),
    )(*operands)


def shards(
    doc_start,
    q_gdn,
    k_gdn,
    v_gdn,
    z_gdn,
    beta_logit,
    log_decay,
    norm_weight,
    q_attn,
    k_attn,
    v_attn,
    gate_attn,
):
    devices = lax.axis_size("seq")
    length = q_gdn.shape[0]
    heads = v_gdn.shape[1] // DV
    place = lax.axis_index("seq").astype(jnp.int32)
    anchor = (place * length).reshape(1)
    docs = doc_start.reshape(1, length)
    shape = jax.ShapeDtypeStruct

    local_heads = q_attn.shape[1] // HD_A
    group = QH // KVH
    kv_head = lax.axis_index("head") * local_heads // group
    keys_own = lax.dynamic_slice_in_dim(k_attn, kv_head * HD_A, HD_A, 1)
    values_own = lax.dynamic_slice_in_dim(v_attn, kv_head * HD_A, HD_A, 1)
    keys_all = lax.all_gather(keys_own, "seq", axis=0, tiled=True)
    values_all = lax.all_gather(values_own, "seq", axis=0, tiled=True)

    square = (heads, length, length)
    inverse, fresh, added, leaving = call(
        state_kernel,
        (
            shape(square, BF16),
            shape((heads, length, DV), BF16),
            shape((heads, DK, DV), F32),
            shape((heads, DK, DV), BF16),
        ),
        (anchor, docs, beta_logit, log_decay, k_gdn, v_gdn),
        100 * heads * length * DK * DV,
    )
    carry, local_out, reach, gain = call(
        query_kernel,
        (
            shape((heads, DK, DK), BF16),
            shape((heads, length, DV), F32),
            shape((heads, length, DK), BF16),
            shape((heads, length, DV), F32),
        ),
        (anchor, docs, beta_logit, log_decay, q_gdn, k_gdn, z_gdn, norm_weight.reshape(1, DV), inverse, fresh),
        100 * heads * length * DK * DV,
    )
    arrived = []
    for hop in range(devices - 1):
        if hop > 0:
            leaving = call(
                combine_kernel, shape((heads, DK, DV), BF16), (arrived[-1], carry, added), 2 * heads * DK * DK * DV, 0
            )
        arrived.append(lax.ppermute(leaving, "seq", [(hop, hop + 1)]))

    shards_seen = devices // 2 + 1
    span = min(devices, shards_seen + 1) * length
    attn_out = call(
        functools.partial(attention_kernel, span, shards_seen * length),
        shape(q_attn.shape, BF16),
        (anchor, docs, q_attn, gate_attn, keys_all, values_all),
        4 * local_heads * length * span * HD_A,
    )
    gdn_out = call(
        functools.partial(output_kernel, len(arrived)),
        shape(v_gdn.shape, BF16),
        (*arrived, local_out, reach, gain),
        2 * heads * length * DK * DV,
        0,
    )
    return (gdn_out, attn_out)


def solution(mesh):
    tokens = P(("groups", "seq"))
    both = P(("groups", "seq"), "head")
    return jax.shard_map(
        shards,
        mesh=mesh,
        in_specs=(
            tokens,
            both,
            both,
            both,
            both,
            P("head", ("groups", "seq")),
            P("head", ("groups", "seq")),
            P(),
            both,
            P(("groups", "seq"), None),
            P(("groups", "seq"), None),
            both,
        ),
        out_specs=(both, both),
        check_vma=False,
    )
```

time: 190 us -> 59.1 us (0.31)
  the two profiles are of different devices: /device:TPU:26 before, /device:TPU:0 now
where the time goes in v1:
time: 59.1 us; the launch traced here: 58.9 us
  blocking collectives  37.2 us (63%)
  Pallas kernels  8.27 us (14%)
  starting transfers between devices  6.43 us (11%)
  local copies, waits for them, and re-layouts  3.25 us (5%)
  waiting for transfers between devices  2.9 us (5%)
  between operations  0.82 us (1%)
    all_gather x1, blocking collectives, shards(): keys_all = lax.all_gather(keys_own, 'seq', axis=0, tiled=True)  22.2 us
    all_gather x1, blocking collectives, shards(): values_all = lax.all_gather(values_own, 'seq', axis=0, tiled=True)  15 us
    pallas_call x6, Pallas kernels, call(): pl.pallas_call(kernel, out_shape=out_shape, in_specs=specs, out_specs=jax...  8.27 us
    ppermute x3, starting transfers between devices, shards(): arrived.append(lax.ppermute(leaving, 'seq', [(hop, hop + 1)]))  6.43 us
    unnamed x24, local copies, waits for them, and re-layouts  3.23 us
    ppermute x3, waiting for transfers between devices, shards(): arrived.append(lax.ppermute(leaving, 'seq', [(hop, hop + 1)]))  2.9 us
  transfers between devices with their start and end apart: 3, of which 1 were waited for; matrix products, arithmetic and copies ran while one was open for 0% of the time, Pallas kernels for 7%

profile of v1, /device:TPU:0, one launch (start us, length us, event | category | flops | bytes accessed | tf_op | source)
XLA Modules:
  0.0 58.9 jit_solution(10503195138837709144)
XLA Ops:
  0.6 0.0 copy-start
  0.7 0.0 copy-start.9
  0.7 0.0 copy-start.8
  0.7 0.0 copy-start.3
  0.7 0.7 %copy-done.9 = f32[8,128]{1,0:T(8,128)S(1)} copy-done((f32[8,128]{1,0:T(8,128)S(1)}, f32[8,128]{1,0:T(8,128)}, u32[]{:S(2)}) %copy-start.9) | copy-done | bytes 4120
  1.4 0.0 copy-done.8
  1.4 0.0 copy-done.3
  1.4 0.0 copy-start.4
  1.4 0.9 %copy-done.4 = bf16[128,1024]{1,0:T(8,128)(2,1)S(1)} copy-done((bf16[128,1024]{1,0:T(8,128)(2,1)S(1)}, bf16[128,1024]{1,0:T(8,128)(2,1)}, u32[]{:S(2)}) %copy-start.4) | copy-done | bytes 262168
  2.3 0.0 copy-start.6
  2.3 0.9 %copy-done.6 = bf16[128,512]{1,0:T(8,128)(2,1)S(1)} copy-done((bf16[128,512]{1,0:T(8,128)(2,1)S(1)}, bf16[128,512]{1,0:T(8,128)(2,1)}, u32[]{:S(2)}) %copy-start.6) | copy-done | bytes 131096
  3.2 0.0 copy-start.5
  3.3 0.0 copy-start.7
  3.3 2.6 %shard_map.131 = (bf16[8,128,128]{2,1,0:T(8,128)(2,1)S(1)}, bf16[8,128,128]{2,1,0:T(8,128)(2,1)S(1)}, f32[8,128,128]{2,1,0:T(8,128)S(1)}, bf16[8,128,128]{2,1,0:T(8,128)(2,1)S(1)}) custom-call(s32[1]{0:T(128)} %bitcast.anchor_ref, s32[1,128]{1,0:T(1,128)S(1)} %bitcast.3, f32[8,128]{1,0:T(8,128)S(1)} %copy-done.8, f32[8,128]{1,0:T(8,128)S(1)} %copy-done.9, ...), custom_call_target="tpu_custom_call" | custom-call | flops 1677721600 | bytes 401924 | tf_op jit(solution)/shard_map/pallas_call | solution.py:207
  5.9 4.9 %collective-permute-start = (bf16[8,128,128]{2,1,0:T(8,128)(2,1)S(1)}, bf16[8,128,128]{2,1,0:T(8,128)(2,1)S(1)}, u32[]{:S(2)}, u32[]{:S(2)}) collective-permute-start(bf16[8,128,128]{2,1,0:T(8,128)(2,1)S(1)} %get-tuple-element.10), channel_id=1, source_target_pairs={{0,4},{1,5},{2,6},{3,7},{16,20},{17,21},{18,22},{19,23}} | collective-permute-start | bytes 786440 | tf_op jit(solution)/shard_map/ppermute | solution.py:276
  10.8 0.0 copy-start.10
  10.8 0.0 copy-done.5
  10.9 0.0 copy-done.7
  10.9 0.6 %copy-done.10 = f32[128]{0:T(128)S(1)} copy-done((f32[128]{0:T(128)S(1)}, f32[128]{0:T(128)}, u32[]{:S(2)}) %copy-start.10) | copy-done | bytes 536
  11.5 2.0 %shard_map.132 = (bf16[8,128,128]{2,1,0:T(8,128)(2,1)S(1)}, f32[8,128,128]{2,1,0:T(8,128)S(1)}, bf16[8,128,128]{2,1,0:T(8,128)(2,1)S(1)}, f32[8,128,128]{2,1,0:T(8,128)S(1)}) custom-call(s32[1]{0:T(128)} %bitcast.anchor_ref, s32[1,128]{1,0:T(1,128)S(1)} %bitcast.4, f32[8,128]{1,0:T(8,128)S(1)} %copy-done.8, f32[8,128]{1,0:T(8,128)S(1)} %copy-done.9, ...), custom_call_target="tpu_custom_call" | custom-call | flops 1677721600 | bytes 1057796 | tf_op jit(solution)/shard_map/pallas_call | solution.py:207
  13.5 2.9 %collective-permute-done.s_ref.refs_0_ = bf16[8,128,128]{2,1,0:T(8,128)(2,1)S(1)} collective-permute-done((bf16[8,128,128]{2,1,0:T(8,128)(2,1)S(1)}, bf16[8,128,128]{2,1,0:T(8,128)(2,1)S(1)}, u32[]{:S(2)}, u32[]{:S(2)}) %collective-permute-start) | collective-permute-done | bytes 262176 | tf_op jit(solution)/shard_map/ppermute | solution.py:276
  16.4 0.2 shard_map.133
  16.6 0.7 %collective-permute-start.1 = (bf16[8,128,128]{2,1,0:T(8,128)(2,1)S(1)}, bf16[8,128,128]{2,1,0:T(8,128)(2,1)S(1)}, u32[]{:S(2)}, u32[]{:S(2)}) collective-permute-start(bf16[8,128,128]{2,1,0:T(8,128)(2,1)S(1)} %shard_map.133), channel_id=1, source_target_pairs={{4,8},{5,9},{6,10},{7,11},{20,24},{21,25},{22,26},{23,27}} | collective-permute-start | bytes 786440 | tf_op jit(solution)/shard_map/ppermute | solution.py:276
  17.3 0.0 copy-done
  17.3 0.0 collective-permute-done.1.s_ref.refs_1_
  17.3 0.2 shard_map.134
  17.6 0.0 copy-start.11
  17.6 0.8 %collective-permute-start.2 = (bf16[8,128,128]{2,1,0:T(8,128)(2,1)S(1)}, bf16[8,128,128]{2,1,0:T(8,128)(2,1)S(1)}, u32[]{:S(2)}, u32[]{:S(2)}) collective-permute-start(bf16[8,128,128]{2,1,0:T(8,128)(2,1)S(1)} %shard_map.134), channel_id=1, source_target_pairs={{8,12},{9,13},{10,14},{11,15},{24,28},{25,29},{26,30},{27,31}} | collective-permute-start | bytes 786440 | tf_op jit(solution)/shard_map/ppermute | solution.py:276
  18.4 0.0 copy-start.2
  18.4 22.2 %all_gather.6.k_ref = bf16[512,256]{1,0:T(8,128)(2,1)S(1)} all-gather(bf16[128,256]{1,0:T(8,128)(2,1)S(1)} %constant_dynamic-slice_fusion.1), channel_id=1, replica_groups=mesh['groups'=2,'seq'=4,'head'=4] {'seq'}, dimensions={0}, use_global_device_ids=true | all-gather | bytes 327680 | tf_op jit(solution)/shard_map/all_gather | solution.py:244
  40.6 0.0 copy-done.11
  40.6 0.0 copy-start.1
  40.6 15.0 %all_gather.7.v_ref = bf16[512,256]{1,0:T(8,128)(2,1)S(1)} all-gather(bf16[128,256]{1,0:T(8,128)(2,1)S(1)} %constant_dynamic-slice_fusion), channel_id=1, replica_groups=mesh['groups'=2,'seq'=4,'head'=4] {'seq'}, dimensions={0}, use_global_device_ids=true | all-gather | bytes 327680 | tf_op jit(solution)/shard_map/all_gather | solution.py:245
  55.6 0.0 copy-done.2
  55.6 0.0 copy-done.1
  55.6 2.2 %shard_map.136 = bf16[128,1024]{1,0:T(8,128)(2,1)} custom-call(s32[1]{0:T(128)} %bitcast.anchor_ref, s32[1,128]{1,0:T(1,128)S(1)} %bitcast.5, bf16[128,1024]{1,0:T(8,128)(2,1)S(1)} %copy-done.1, bf16[128,1024]{1,0:T(8,128)(2,1)S(1)} %copy-done.2, bf16[512,256]{1,0:T(8,128)(2,1)S(1)} %all_gather.6.k_ref, bf16[512,256]{1,0:T(8,128)(2,1)S(1)} %all_gather.7.v_ref), custom_call_target="tpu_custom_call" | custom-call | flops 268435456 | bytes 1049092 | tf_op jit(solution)/shard_map/pallas_call | solution.py:207
  57.8 0.0 collective-permute-done.2.refs_2_
  57.8 1.1 %shard_map.135 = bf16[128,1024]{1,0:T(8,128)(2,1)} custom-call(bf16[8,128,128]{2,1,0:T(8,128)(2,1)S(1)} %collective-permute-done.s_ref.refs_0_, bf16[8,128,128]{2,1,0:T(8,128)(2,1)S(1)} %collective-permute-done.1.s_ref.refs_1_, bf16[8,128,128]{2,1,0:T(8,128)(2,1)S(1)} %collective-permute-done.2.refs_2_, f32[8,128,128]{2,1,0:T(8,128)S(1)} %get-tuple-element.15.refs_3_, ...), custom_call_target="tpu_custom_call" | custom-call | flops 33554432 | bytes 2097152 | tf_op jit(solution)/shard_map/pallas_call | solution.py:207
  (2 shorter events, 0.0 us)
Async XLA Ops:
  0.6 16.7 %copy-start = (bf16[128,512]{1,0:T(8,128)(2,1)S(1)}, bf16[128,512]{1,0:T(8,128)(2,1)}, u32[]{:S(2)}) copy-start(bf16[128,512]{1,0:T(8,128)(2,1)} %param.21) | copy-start | bytes 393220
  0.7 0.7 %copy-start.9 = (f32[8,128]{1,0:T(8,128)S(1)}, f32[8,128]{1,0:T(8,128)}, u32[]{:S(2)}) copy-start(f32[8,128]{1,0:T(8,128)} %gate_ref.4) | copy-start | bytes 12292
  0.7 0.7 %copy-start.8 = (f32[8,128]{1,0:T(8,128)S(1)}, f32[8,128]{1,0:T(8,128)}, u32[]{:S(2)}) copy-start(f32[8,128]{1,0:T(8,128)} %beta_ref.3) | copy-start | bytes 12292
  0.7 0.7 %copy-start.3 = (s32[128]{0:T(128)S(1)}, s32[128]{0:T(128)}, u32[]{:S(2)}) copy-start(s32[128]{0:T(128)} %param.12) | copy-start | bytes 1540
  1.4 1.0 %copy-start.4 = (bf16[128,1024]{1,0:T(8,128)(2,1)S(1)}, bf16[128,1024]{1,0:T(8,128)(2,1)}, u32[]{:S(2)}) copy-start(bf16[128,1024]{1,0:T(8,128)(2,1)} %v_ref.1) | copy-start | bytes 786436
  2.3 0.9 %copy-start.6 = (bf16[128,512]{1,0:T(8,128)(2,1)S(1)}, bf16[128,512]{1,0:T(8,128)(2,1)}, u32[]{:S(2)}) copy-start(bf16[128,512]{1,0:T(8,128)(2,1)} %k_ref.3) | copy-start | bytes 393220
  3.2 7.6 %copy-start.5 = (bf16[128,1024]{1,0:T(8,128)(2,1)S(1)}, bf16[128,1024]{1,0:T(8,128)(2,1)}, u32[]{:S(2)}) copy-start(bf16[128,1024]{1,0:T(8,128)(2,1)} %z_ref.1) | copy-start | bytes 786436
  3.3 7.6 %copy-start.7 = (bf16[128,512]{1,0:T(8,128)(2,1)S(1)}, bf16[128,512]{1,0:T(8,128)(2,1)}, u32[]{:S(2)}) copy-start(bf16[128,512]{1,0:T(8,128)(2,1)} %q_ref.2) | copy-start | bytes 393220
  5.9 10.5 %collective-permute-start = (bf16[8,128,128]{2,1,0:T(8,128)(2,1)S(1)}, bf16[8,128,128]{2,1,0:T(8,128)(2,1)S(1)}, u32[]{:S(2)}, u32[]{:S(2)}) collective-permute-start(bf16[8,128,128]{2,1,0:T(8,128)(2,1)S(1)} %get-tuple-element.10), channel_id=1, source_target_pairs={{0,4},{1,5},{2,6},{3,7},{16,20},{17,21},{18,22},{19,23}} | collective-permute-start | bytes 786440 | tf_op jit(solution)/shard_map/ppermute | solution.py:276
  10.8 0.7 %copy-start.10 = (f32[128]{0:T(128)S(1)}, f32[128]{0:T(128)}, u32[]{:S(2)}) copy-start(f32[128]{0:T(128)} %param.19) | copy-start | bytes 1540
  16.6 0.7 %collective-permute-start.1 = (bf16[8,128,128]{2,1,0:T(8,128)(2,1)S(1)}, bf16[8,128,128]{2,1,0:T(8,128)(2,1)S(1)}, u32[]{:S(2)}, u32[]{:S(2)}) collective-permute-start(bf16[8,128,128]{2,1,0:T(8,128)(2,1)S(1)} %shard_map.133), channel_id=1, source_target_pairs={{4,8},{5,9},{6,10},{7,11},{20,24},{21,25},{22,26},{23,27}} | collective-permute-start | bytes 786440 | tf_op jit(solution)/shard_map/ppermute | solution.py:276
  17.6 23.0 %copy-start.11 = (bf16[128,512]{1,0:T(8,128)(2,1)S(1)}, bf16[128,512]{1,0:T(8,128)(2,1)}, u32[]{:S(2)}) copy-start(bf16[128,512]{1,0:T(8,128)(2,1)} %param.22) | copy-start | bytes 393220
  17.6 40.2 %collective-permute-start.2 = (bf16[8,128,128]{2,1,0:T(8,128)(2,1)S(1)}, bf16[8,128,128]{2,1,0:T(8,128)(2,1)S(1)}, u32[]{:S(2)}, u32[]{:S(2)}) collective-permute-start(bf16[8,128,128]{2,1,0:T(8,128)(2,1)S(1)} %shard_map.134), channel_id=1, source_target_pairs={{8,12},{9,13},{10,14},{11,15},{24,28},{25,29},{26,30},{27,31}} | collective-permute-start | bytes 786440 | tf_op jit(solution)/shard_map/ppermute | solution.py:276
  18.4 37.2 %copy-start.2 = (bf16[128,1024]{1,0:T(8,128)(2,1)S(1)}, bf16[128,1024]{1,0:T(8,128)(2,1)}, u32[]{:S(2)}) copy-start(bf16[128,1024]{1,0:T(8,128)(2,1)} %gate_ref.5) | copy-start | bytes 786436
  40.6 15.0 %copy-start.1 = (bf16[128,1024]{1,0:T(8,128)(2,1)S(1)}, bf16[128,1024]{1,0:T(8,128)(2,1)}, u32[]{:S(2)}) copy-start(bf16[128,1024]{1,0:T(8,128)(2,1)} %q_ref.3) | copy-start | bytes 786436

commit v2 on v1

v2 whole, which is shorter than its diff:
```python
import functools

import jax
import jax.numpy as jnp
from jax import lax
from jax.experimental import pallas as pl
from jax.experimental.pallas import tpu as pltpu
from jax.sharding import PartitionSpec as P

DK = 128
DV = 128
QH = 16
KVH = 2
HD_A = 256
EPS = 1e-06
VMEM_LIMIT = 48 * 1024 * 1024
PIECES = 2

F32 = jnp.float32
BF16 = jnp.bfloat16


def dot(a, b):
    return jnp.dot(a, b, preferred_element_type=F32)


def dot_t(a, b):
    return lax.dot_general(a, b, (((1,), (1,)), ((), ())), preferred_element_type=F32)


def prefix_sums(rows):
    count, length = rows.shape
    first = rows.astype(BF16)
    rest = rows - first.astype(F32)
    second = rest.astype(BF16)
    third = (rest - second.astype(F32)).astype(BF16)
    t_at = lax.broadcasted_iota(jnp.int32, (length, length), 0)
    i_at = lax.broadcasted_iota(jnp.int32, (length, length), 1)
    ones = (t_at <= i_at).astype(F32).astype(BF16)
    return dot(first, ones) + dot(second, ones) + dot(third, ones)


def columns_of(rows):
    count, length = rows.shape
    padded = jnp.concatenate([rows, jnp.zeros((length - count, length), F32)], axis=0)
    return padded.T


def diagonal_row(square, same_place):
    return jnp.sum(jnp.where(same_place, square, 0.0), axis=0, keepdims=True)


def places(length):
    row = lax.broadcasted_iota(jnp.int32, (length, length), 0)
    col = lax.broadcasted_iota(jnp.int32, (length, length), 1)
    return row, col


def pack_kernel(scalar_ref, k_hbm, v_hbm, own_ref, part_ref, sems):
    rows = part_ref.shape[0]
    column = pl.multiple_of(scalar_ref[1], HD_A)
    begin = pl.multiple_of(scalar_ref[2], rows)
    copies = []
    for side, source in enumerate((k_hbm, v_hbm)):
        lanes = pl.ds(side * HD_A, HD_A)
        wanted = pl.ds(column, HD_A)
        copies += [
            pltpu.make_async_copy(source.at[pl.ds(begin, rows), wanted], part_ref.at[:, lanes], sems.at[2 * side]),
            pltpu.make_async_copy(source.at[:, wanted], own_ref.at[:, lanes], sems.at[2 * side + 1]),
        ]
    for copy in copies:
        copy.start()
    for copy in copies:
        copy.wait()


def state_kernel(
    scalar_ref, doc_hbm, beta_hbm, gate_hbm, k_hbm, v_hbm, u_ref, w_ref, a_ref, m_ref, *rest
):
    send_refs = rest[:-6]
    doc_ref, beta_ref, gate_ref, k_ref, v_ref, sems = rest[-6:]
    sources = [(k_hbm, k_ref), (gate_hbm, gate_ref), (beta_hbm, beta_ref), (doc_hbm, doc_ref), (v_hbm, v_ref)]
    copies = [pltpu.make_async_copy(a, b, sems.at[i]) for i, (a, b) in enumerate(sources)]
    for copy in copies:
        copy.start()
    for copy in copies[:4]:
        copy.wait()
    length = k_ref.shape[0]
    heads = beta_ref.shape[0]
    key_heads = k_ref.shape[1] // DK
    repeat = heads // key_heads
    anchor = scalar_ref[0]
    row, col = places(length)
    beta = jax.nn.sigmoid(beta_ref[...])
    running = prefix_sums(gate_ref[...])
    doc = doc_ref[...]
    keys = [k_ref[:, g * DK : (g + 1) * DK] for g in range(key_heads)]
    grams = [dot_t(k, k) for k in keys]
    squares = [diagonal_row(g, row == col) + EPS for g in grams]
    log_inv = [-0.5 * jnp.log(s) for s in squares]
    inv = [lax.rsqrt(s) for s in squares]
    log_rows = jnp.concatenate([log_inv[h // repeat] for h in range(heads)], axis=0)
    cols = columns_of(
        jnp.concatenate([running + log_rows, jnp.broadcast_to(doc.astype(F32), (8, length))], axis=0)
    )
    doc_col = cols[:, heads : heads + 1]
    place = (anchor + col).astype(F32)
    strict = (doc_col <= place) & (col < row)
    tail_same = doc[:, length - 1 : length] <= (anchor + col[:1, :])
    systems = []
    for h in range(heads):
        spread = cols[:, h : h + 1] - running[h : h + 1, :]
        decay = jnp.where(strict, jnp.exp(spread), 0.0)
        weight = beta[h : h + 1, :] * inv[h // repeat]
        systems.append(decay * grams[h // repeat] * weight)
    differ = row ^ col
    inverse = [jnp.where(row == col, 1.0, 0.0) - jnp.where(differ == 1, n, 0.0) for n in systems]
    level = 1
    while (1 << level) < length:
        mask = (differ >> level) == 1
        short = [x.astype(BF16) for x in inverse]
        inner = [
            dot(jnp.where(mask, n, 0.0).astype(BF16), x).astype(BF16) for n, x in zip(systems, short)
        ]
        inverse = [x - dot(s, y) for x, s, y in zip(inverse, short, inner)]
        level += 1
    keys_t = [k.astype(F32).T for k in keys]
    for copy in copies[4:]:
        copy.wait()
    piece = heads // len(send_refs)
    for h in range(heads):
        g = h // repeat
        run = running[h : h + 1, :]
        u = dot(inverse[h].astype(BF16), v_ref[:, h * DV : (h + 1) * DV]).astype(BF16)
        u_ref[h] = u
        tail = jnp.exp(run[:, length - 1 : length] - run)
        tail = jnp.where(tail_same, tail, 0.0) * beta[h : h + 1, :] * inv[g]
        tail_keys = (keys_t[g] * tail).astype(BF16)
        a = dot(tail_keys, u)
        a_ref[h] = a
        send_refs[h // piece][h % piece] = a.astype(BF16)
        entry = jnp.where(doc < anchor, jnp.exp(run), 0.0)
        w = dot((inverse[h] * (entry * inv[g])).astype(BF16), keys[g]).astype(BF16)
        w_ref[h] = w
        m_ref[h] = (jnp.where(row == col, entry[:, length - 1 : length], 0.0) - dot(tail_keys, w)).astype(BF16)


def query_kernel(
    scalar_ref, doc_ref, beta_ref, gate_ref, q_ref, k_ref, z_ref, gain_ref, u_ref, w_ref, local_ref, reach_ref, gz_ref
):
    length = k_ref.shape[0]
    heads = beta_ref.shape[0]
    key_heads = k_ref.shape[1] // DK
    repeat = heads // key_heads
    anchor = scalar_ref[0]
    row, col = places(length)
    beta = jax.nn.sigmoid(beta_ref[...])
    running = prefix_sums(gate_ref[...])
    doc = doc_ref[...]
    keys = [k_ref[:, g * DK : (g + 1) * DK] for g in range(key_heads)]
    queries = [q_ref[:, g * DK : (g + 1) * DK] for g in range(key_heads)]
    inv = [lax.rsqrt(diagonal_row(dot_t(k, k), row == col) + EPS) for k in keys]
    log_q = [-0.5 * jnp.log(diagonal_row(dot_t(q, q), row == col) + EPS) for q in queries]
    log_rows = jnp.concatenate([log_q[h // repeat] for h in range(heads)], axis=0)
    cols = columns_of(
        jnp.concatenate([running + log_rows, jnp.broadcast_to(doc.astype(F32), (8, length))], axis=0)
    )
    doc_col = cols[:, heads : heads + 1]
    place = (anchor + col).astype(F32)
    same = (doc_col <= place) & (col <= row)
    alive_col = doc_col < anchor.astype(F32)
    cross = [dot_t(q, k) for q, k in zip(queries, keys)]
    for h in range(heads):
        g = h // repeat
        weight = beta[h : h + 1, :] * inv[g]
        decay = jnp.where(same, jnp.exp(cols[:, h : h + 1] - running[h : h + 1, :]), 0.0)
        scores = (decay * cross[g] * weight).astype(BF16)
        local_ref[h] = dot(scores, u_ref[h])
        lead = jnp.where(alive_col, jnp.exp(cols[:, h : h + 1]), 0.0)
        reach_ref[h] = (lead * queries[g].astype(F32) - dot(scores, w_ref[h])).astype(BF16)
    z = z_ref[...].astype(F32)
    gate = z / (1.0 + jnp.exp(-z))
    for h in range(heads):
        gz_ref[h] = gate[:, h * DV : (h + 1) * DV] * gain_ref[...]


def combine_kernel(begin, s_ref, m_ref, a_ref, out_ref):
    for h in range(s_ref.shape[0]):
        out_ref[h] = (dot(m_ref[begin + h], s_ref[h]) + a_ref[begin + h]).astype(BF16)


def output_kernel(hops, pieces, *refs):
    states = refs[: hops * pieces]
    local_ref, reach_ref, gz_ref, out_ref = refs[hops * pieces :]
    heads = local_ref.shape[0]
    piece = heads // pieces
    for h in range(heads):
        parts = [states[hop * pieces + h // piece][h % piece] for hop in range(hops)]
        state = parts[0]
        for other in parts[1:]:
            state = state + other
        mixed = local_ref[h] + dot(reach_ref[h], state)
        factor = lax.rsqrt(jnp.mean(mixed * mixed, axis=-1, keepdims=True) + EPS)
        out_ref[:, h * DV : (h + 1) * DV] = (mixed * factor * gz_ref[h]).astype(BF16)


def attention_kernel(window, layout, scalar_ref, doc_ref, q_ref, gate_ref, own_ref, *refs):
    sections, out_ref = refs[:-1], refs[-1]
    length = q_ref.shape[0]
    heads = q_ref.shape[1] // HD_A
    anchor = scalar_ref[0]
    docs = columns_of(jnp.broadcast_to(doc_ref[...].astype(F32), (8, length)))[:, :1].astype(jnp.int32)
    q_place = anchor + lax.broadcasted_iota(jnp.int32, (length, 1), 0)
    lower = jnp.maximum(jnp.maximum(docs, q_place - window + 1), 0)
    spots = [anchor + lax.broadcasted_iota(jnp.int32, (length, length), 1)]
    for distance, turn, rows in layout:
        start = anchor - distance * length + scalar_ref[2 + turn]
        spots.append(start + lax.broadcasted_iota(jnp.int32, (length, rows), 1))
    k_place = jnp.concatenate(spots, axis=1)
    visible = (k_place >= lower) & (k_place <= q_place)
    blocks = [own_ref, *sections]
    keys = jnp.concatenate([b[:, :HD_A] for b in blocks], axis=0)
    values = jnp.concatenate([b[:, HD_A:] for b in blocks], axis=0)
    for h in range(heads):
        part = slice(h * HD_A, (h + 1) * HD_A)
        scores = dot_t(q_ref[:, part], keys) * (HD_A**-0.5)
        scores = jnp.where(visible, scores, -jnp.inf)
        peak = jnp.max(scores, axis=-1, keepdims=True)
        weights = jnp.exp(scores - peak)
        total = jnp.sum(weights, axis=-1, keepdims=True)
        mixed = dot(weights.astype(BF16), values) / total
        out_ref[:, part] = (mixed * jax.nn.sigmoid(gate_ref[:, part].astype(F32))).astype(BF16)


def call(kernel, out_shape, operands, flops, scalars=1, outside=0, scratch=()):
    moved = sum(o.size * o.dtype.itemsize for o in operands)
    specs = [pl.BlockSpec(memory_space=pltpu.SMEM)] * scalars
    specs += [pl.BlockSpec(memory_space=pltpu.HBM)] * outside
    specs += [pl.BlockSpec(memory_space=pltpu.VMEM)] * (len(operands) - scalars - outside)
    return pl.pallas_call(
        kernel,
        out_shape=out_shape,
        in_specs=specs,
        out_specs=jax.tree.map(lambda _: pl.BlockSpec(memory_space=pltpu.VMEM), out_shape),
        scratch_shapes=scratch,
        compiler_params=pltpu.CompilerParams(vmem_limit_bytes=VMEM_LIMIT),
        cost_estimate=pl.CostEstimate(flops=flops, bytes_accessed=moved, transcendentals=0),
    )(*operands)


def after(value, *others):
    return lax.optimization_barrier((value, *others))[0]


def shards(
    doc_start,
    q_gdn,
    k_gdn,
    v_gdn,
    z_gdn,
    beta_logit,
    log_decay,
    norm_weight,
    q_attn,
    k_attn,
    v_attn,
    gate_attn,
):
    devices = lax.axis_size("seq")
    length = q_gdn.shape[0]
    heads = v_gdn.shape[1] // DV
    local_heads = q_attn.shape[1] // HD_A
    group = QH // KVH
    head_devices = lax.axis_size("head")
    sharers = max(1, min(group // local_heads, head_devices))
    rows = length // sharers
    place = lax.axis_index("seq").astype(jnp.int32)
    head_at = lax.axis_index("head").astype(jnp.int32)
    kv_head = head_at * local_heads // group
    share = head_at % sharers
    scalars = jnp.stack(
        [place * length, kv_head * HD_A] + [(share + sharers - t) % sharers * rows for t in range(sharers)]
    )
    docs = doc_start.reshape(1, length)
    shape = jax.ShapeDtypeStruct
    pieces = PIECES if heads % PIECES == 0 else 1

    own, part = call(
        pack_kernel,
        (shape((length, 2 * HD_A), BF16), shape((rows, 2 * HD_A), BF16)),
        (scalars, k_attn, v_attn),
        0,
        outside=2,
        scratch=[pltpu.SemaphoreType.DMA((4,))],
    )
    fresh, erased, added, carry, *leaving = call(
        state_kernel,
        (
            shape((heads, length, DV), BF16),
            shape((heads, length, DK), BF16),
            shape((heads, DK, DV), F32),
            shape((heads, DK, DK), BF16),
            *[shape((heads // pieces, DK, DV), BF16)] * pieces,
        ),
        (scalars, docs, beta_logit, log_decay, k_gdn, v_gdn),
        100 * heads * length * DK * DV,
        outside=5,
        scratch=[
            pltpu.VMEM(docs.shape, jnp.int32),
            pltpu.VMEM(beta_logit.shape, F32),
            pltpu.VMEM(log_decay.shape, F32),
            pltpu.VMEM(k_gdn.shape, BF16),
            pltpu.VMEM(v_gdn.shape, BF16),
            pltpu.SemaphoreType.DMA((5,)),
        ],
    )

    wanted = min(devices // 2 + 1, devices - 1)
    units = [part]
    layout = []
    sections = []
    have = 1
    while have < wanted + 1:
        take = min(have, wanted + 1 - have)
        block = units[0] if take == 1 else jnp.concatenate(units[:take], axis=0)
        got = lax.ppermute(block, "seq", [(i, i + have) for i in range(devices - have)])
        for turn in range(sharers):
            if turn == 0:
                swapped = got
            else:
                swapped = lax.ppermute(
                    got, "head", [(i, i // sharers * sharers + (i + turn) % sharers) for i in range(head_devices)]
                )
            for step in range(take):
                layout.append((have + step, turn, rows))
                sections.append(swapped[step * rows : (step + 1) * rows])
        units += [got[step * rows : (step + 1) * rows] for step in range(take)]
        have += take

    arrived = [[lax.ppermute(s, "seq", [(0, 1)]) for s in leaving]]
    local_out, reach, gain = call(
        query_kernel,
        (
            shape((heads, length, DV), F32),
            shape((heads, length, DK), BF16),
            shape((heads, length, DV), F32),
        ),
        (scalars, docs, beta_logit, log_decay, q_gdn, k_gdn, z_gdn, norm_weight.reshape(1, DV), fresh, erased),
        100 * heads * length * DK * DV,
    )
    piece = heads // pieces
    for hop in range(1, devices - 1):
        leaving = [
            call(
                functools.partial(combine_kernel, at * piece),
                shape((piece, DK, DV), BF16),
                (arrived[-1][at], carry, added),
                2 * piece * DK * DK * DV,
                0,
            )
            for at in range(pieces)
        ]
        arrived.append([lax.ppermute(s, "seq", [(hop, hop + 1)]) for s in leaving])

    attn_out = call(
        functools.partial(attention_kernel, (devices // 2 + 1) * length, layout),
        shape(q_attn.shape, BF16),
        (scalars, docs, q_attn, gate_attn, own, *sections),
        4 * local_heads * length * length * (wanted + 1) * HD_A,
    )
    gdn_out = call(
        functools.partial(output_kernel, len(arrived), pieces),
        shape(v_gdn.shape, BF16),
        (*[s for hop in arrived for s in hop], local_out, reach, gain),
        2 * heads * length * DK * DV,
        0,
    )
    return (gdn_out, attn_out)


def solution(mesh):
    tokens = P(("groups", "seq"))
    both = P(("groups", "seq"), "head")
    return jax.shard_map(
        shards,
        mesh=mesh,
        in_specs=(
            tokens,
            both,
            both,
            both,
            both,
            P("head", ("groups", "seq")),
            P("head", ("groups", "seq")),
            P(),
            both,
            P(("groups", "seq"), None),
            P(("groups", "seq"), None),
            both,
        ),
        out_specs=(both, both),
        check_vma=False,
    )
```

time: 59.1 us -> 35.8 us (0.61)
  the two profiles are of different devices: /device:TPU:0 before, /device:TPU:26 now
where the time goes in v2:
time: 35.8 us; the launch traced here: 35.5 us
  waiting for transfers between devices  12.4 us (35%)
  Pallas kernels  10.5 us (29%)
  starting transfers between devices  8.18 us (23%)
  local copies, waits for them, and re-layouts  3.39 us (9%)
  between operations  1.01 us (3%)
    pallas_call x9, Pallas kernels, call(): pl.pallas_call(kernel, out_shape=out_shape, in_specs=specs, out_specs=jax...  10.5 us
    ppermute x4, waiting for transfers between devices, shards(): arrived.append([lax.ppermute(s, 'seq', [(hop, hop + 1)]) for s in leaving])  9.59 us
    ppermute x4, starting transfers between devices, shards(): arrived.append([lax.ppermute(s, 'seq', [(hop, hop + 1)]) for s in leaving])  4.05 us
    unnamed x26, local copies, waits for them, and re-layouts  3.37 us
    ppermute x2, waiting for transfers between devices, shards(): lax.ppermute(block, 'seq', [(i, i + have) for i in range(devices - have)])  2.77 us
    ppermute x2, starting transfers between devices, shards(): lax.ppermute(block, 'seq', [(i, i + have) for i in range(devices - have)])  2.58 us
    ppermute x2, starting transfers between devices, shards(): arrived = [[lax.ppermute(s, 'seq', [(0, 1)]) for s in leaving]]  1.47 us
  transfers between devices with their start and end apart: 10, of which 3 were waited for; matrix products, arithmetic and copies ran while one was open for 0% of the time, Pallas kernels for 25%

profile of v2, /device:TPU:26, one launch (start us, length us, event | category | flops | bytes accessed | tf_op | source)
XLA Modules:
  0.0 35.5 jit_solution(15663578427871129241)
XLA Ops:
  0.7 0.0 copy-start.11
  0.7 0.0 copy-start.10
  0.7 0.1 pad_add_fusion.scalar_ref
  0.8 0.9 %copy-done.2 = bf16[128,512]{1,0:T(8,128)(2,1)S(1)} copy-done((bf16[128,512]{1,0:T(8,128)(2,1)S(1)}, bf16[128,512]{1,0:T(8,128)(2,1)}, u32[]{:S(2)}) %copy-start.2) | copy-done | bytes 131096
  1.7 0.9 %copy-done.3 = bf16[128,512]{1,0:T(8,128)(2,1)S(1)} copy-done((bf16[128,512]{1,0:T(8,128)(2,1)S(1)}, bf16[128,512]{1,0:T(8,128)(2,1)}, u32[]{:S(2)}) %copy-start.3) | copy-done | bytes 131096
  2.6 0.6 %shard_map.138 = (bf16[128,512]{1,0:T(8,128)(2,1)S(1)}, bf16[64,512]{1,0:T(8,128)(2,1)S(1)}) custom-call(s32[4]{0:T(128)S(1)} %pad_add_fusion.scalar_ref, bf16[128,512]{1,0:T(8,128)(2,1)S(1)} %copy-done.2, bf16[128,512]{1,0:T(8,128)(2,1)S(1)} %copy-done.3), custom_call_target="tpu_custom_call" | custom-call | bytes 262160 | tf_op jit(solution)/shard_map/pallas_call | solution.py:240
  3.2 0.0 copy-start.4
  3.2 1.3 %collective-permute-start.6 = (bf16[64,512]{1,0:T(8,128)(2,1)S(1)}, bf16[64,512]{1,0:T(8,128)(2,1)S(1)}, u32[]{:S(2)}, u32[]{:S(2)}) collective-permute-start(bf16[64,512]{1,0:T(8,128)(2,1)S(1)} %get-tuple-element.23), channel_id=1, source_target_pairs={{0,4},{4,8},{8,12},{1,5},{5,9},{9,13},{2,6},{6,10},{10,14},{3,7},{... | collective-permute-start | bytes 196616 | tf_op jit(solution)/shard_map/ppermute | solution.py:326
  4.5 0.0 copy-done.11
  4.5 0.0 copy-done.10
  4.5 0.0 copy-done.5
  4.5 0.0 copy-done.4
  4.5 0.0 copy-start.7
  4.6 0.9 %copy-done.7 = bf16[128,512]{1,0:T(8,128)(2,1)S(1)} copy-done((bf16[128,512]{1,0:T(8,128)(2,1)S(1)}, bf16[128,512]{1,0:T(8,128)(2,1)}, u32[]{:S(2)}) %copy-start.7) | copy-done | bytes 131096
  5.5 3.6 %shard_map.131 = (bf16[8,128,128]{2,1,0:T(8,128)(2,1)S(1)}, bf16[8,128,128]{2,1,0:T(8,128)(2,1)S(1)}, f32[8,128,128]{2,1,0:T(8,128)S(1)}, bf16[8,128,128]{2,1,0:...) custom-call(s32[4]{0:T(128)S(1)} %pad_add_fusion.scalar_ref, s32[1,128]{1,0:T(1,128)S(1)} %bitcast.6, ...), custom_call_target="tpu_custom_call" | custom-call | flops 1677721600 | bytes 401936 | tf_op jit(solution)/shard_map/pallas_call | solution.py:240
  9.1 0.0 copy-start.6
  9.1 0.8 %collective-permute-start = (bf16[4,128,128]{2,1,0:T(8,128)(2,1)S(1)}, bf16[4,128,128]{2,1,0:T(8,128)(2,1)S(1)}, u32[]{:S(2)}, u32[]{:S(2)}) collective-permute-start(bf16[4,128,128]{2,1,0:T(8,128)(2,1)S(1)} %get-tuple-element.13), channel_id=1, source_target_pairs={{0,4},{1,5},{2,6},{3,7},{16,20},{17,21},{18,22},{19,23}} | collective-permute-start | bytes 393224 | tf_op jit(solution)/shard_map/ppermute | solution.py:340
  9.9 0.7 %collective-permute-start.1 = (bf16[4,128,128]{2,1,0:T(8,128)(2,1)S(1)}, bf16[4,128,128]{2,1,0:T(8,128)(2,1)S(1)}, u32[]{:S(2)}, u32[]{:S(2)}) collective-permute-start(bf16[4,128,128]{2,1,0:T(8,128)(2,1)S(1)} %get-tuple-element.14), channel_id=1, source_target_pairs={{0,4},{1,5},{2,6},{3,7},{16,20},{17,21},{18,22},{19,23}} | collective-permute-start | bytes 393224 | tf_op jit(solution)/shard_map/ppermute | solution.py:340
  10.6 0.0 collective-permute-done.6.refs_0_
  10.6 1.3 %collective-permute-start.8 = (bf16[128,512]{1,0:T(8,128)(2,1)S(1)}, bf16[128,512]{1,0:T(8,128)(2,1)S(1)}, u32[]{:S(2)}, u32[]{:S(2)}) collective-permute-start(bf16[128,512]{1,0:T(8,128)(2,1)S(1)} %pad_maximum_fusion), channel_id=1, source_target_pairs={{0,8},{4,12},{1,9},{5,13},{2,10},{6,14},{3,11},{7,15},{16,24},{20,... | collective-permute-start | bytes 393224 | tf_op jit(solution)/shard_map/ppermute | solution.py:326
  11.9 0.0 copy-start.12
  11.9 0.0 copy-done.8
  12.0 0.0 copy-done.9
  12.0 0.6 %copy-done.12 = f32[128]{0:T(128)S(1)} copy-done((f32[128]{0:T(128)S(1)}, f32[128]{0:T(128)}, u32[]{:S(2)}) %copy-start.12) | copy-done | bytes 536
  12.6 1.7 %shard_map.136 = (f32[8,128,128]{2,1,0:T(8,128)S(1)}, bf16[8,128,128]{2,1,0:T(8,128)(2,1)S(1)}, f32[8,128,128]{2,1,0:T(8,128)S(1)}) custom-call(s32[4]{0:T(128)S(1)} %pad_add_fusion.scalar_ref, s32[1,128]{1,0:T(1,128)S(1)} %bitcast.7, f32[8,128]{1,0:T(8,128)S(1)} %copy-done.10, f32[8,128]{1,0:T(8,128)S(1)} %copy-done.11, bf16[128,512]{1,0:T(8,128)(2,1)S(1)} %copy-done.9, ...), custom_call_target="tpu_custom_call" | custom-call | flops 1677721600 | bytes 1057808 | tf_op jit(solution)/shard_map/pallas_call | solution.py:240
  14.3 0.1 collective-permute-start.7
  14.4 0.0 collective-permute-done.s_ref.refs_0_
  14.4 0.2 shard_map.132
  14.6 0.7 %collective-permute-start.2 = (bf16[4,128,128]{2,1,0:T(8,128)(2,1)S(1)}, bf16[4,128,128]{2,1,0:T(8,128)(2,1)S(1)}, u32[]{:S(2)}, u32[]{:S(2)}) collective-permute-start(bf16[4,128,128]{2,1,0:T(8,128)(2,1)S(1)} %shard_map.132), channel_id=1, source_target_pairs={{4,8},{5,9},{6,10},{7,11},{20,24},{21,25},{22,26},{23,27}} | collective-permute-start | bytes 393224 | tf_op jit(solution)/shard_map/ppermute | solution.py:363
  15.3 0.0 collective-permute-done.1.s_ref.refs_1_
  15.3 0.2 shard_map.133
  15.5 0.7 %collective-permute-start.3 = (bf16[4,128,128]{2,1,0:T(8,128)(2,1)S(1)}, bf16[4,128,128]{2,1,0:T(8,128)(2,1)S(1)}, u32[]{:S(2)}, u32[]{:S(2)}) collective-permute-start(bf16[4,128,128]{2,1,0:T(8,128)(2,1)S(1)} %shard_map.133), channel_id=1, source_target_pairs={{4,8},{5,9},{6,10},{7,11},{20,24},{21,25},{22,26},{23,27}} | collective-permute-start | bytes 393224 | tf_op jit(solution)/shard_map/ppermute | solution.py:363
  16.1 2.8 %collective-permute-done.8 = bf16[128,512]{1,0:T(8,128)(2,1)S(1)} collective-permute-done((bf16[128,512]{1,0:T(8,128)(2,1)S(1)}, bf16[128,512]{1,0:T(8,128)(2,1)S(1)}, u32[]{:S(2)}, u32[]{:S(2)}) %collective-permute-start.8) | collective-permute-done | bytes 131104 | tf_op jit(solution)/shard_map/ppermute | solution.py:326
  18.9 0.0 collective-permute-start.9
  18.9 0.0 collective-permute-done.2.s_ref.refs_2_
  18.9 0.2 shard_map.134
  19.1 1.3 %collective-permute-start.4 = (bf16[4,128,128]{2,1,0:T(8,128)(2,1)S(1)}, bf16[4,128,128]{2,1,0:T(8,128)(2,1)S(1)}, u32[]{:S(2)}, u32[]{:S(2)}) collective-permute-start(bf16[4,128,128]{2,1,0:T(8,128)(2,1)S(1)} %shard_map.134), channel_id=1, source_target_pairs={{8,12},{9,13},{10,14},{11,15},{24,28},{25,29},{26,30},{27,31}} | collective-permute-start | bytes 393224 | tf_op jit(solution)/shard_map/ppermute | solution.py:363
  20.4 0.0 collective-permute-done.3.s_ref.refs_3_
  20.4 0.0 copy-start.1
  20.4 0.2 shard_map.135
  20.6 0.0 copy-start
  20.6 1.4 %collective-permute-start.5 = (bf16[4,128,128]{2,1,0:T(8,128)(2,1)S(1)}, bf16[4,128,128]{2,1,0:T(8,128)(2,1)S(1)}, u32[]{:S(2)}, u32[]{:S(2)}) collective-permute-start(bf16[4,128,128]{2,1,0:T(8,128)(2,1)S(1)} %shard_map.135), channel_id=1, source_target_pairs={{8,12},{9,13},{10,14},{11,15},{24,28},{25,29},{26,30},{27,31}} | collective-permute-start | bytes 393224 | tf_op jit(solution)/shard_map/ppermute | solution.py:363
  22.1 0.0 collective-permute-done.9
  22.1 0.0 collective-permute-done.7.refs_1_
  22.1 2.7 %shard_map.139 = bf16[128,1024]{1,0:T(8,128)(2,1)} custom-call(s32[4]{0:T(128)S(1)} %pad_add_fusion.scalar_ref, s32[1,128]{1,0:T(1,128)S(1)} %bitcast.8, bf16[128,1024]{1,0:T(8,128)(2,1)S(1)} %copy-done, bf16[128,1024]{1,0:T(8,128)(2,1)S(1)} %copy-done.1, bf16[128,512]{1,0:T(8,128)(2,1)S(1)} %get-tuple-element.22.own_ref, ...), custom_call_target="tpu_custom_call" | custom-call | flops 268435456 | bytes 1049104 | tf_op jit(solution)/shard_map/pallas_call | solution.py:240
  24.9 6.8 %collective-permute-done.4.refs_4_ = bf16[4,128,128]{2,1,0:T(8,128)(2,1)S(1)} collective-permute-done((bf16[4,128,128]{2,1,0:T(8,128)(2,1)S(1)}, bf16[4,128,128]{2,1,0:T(8,128)(2,1)S(1)}, u32[]{:S(2)}, u32[]{:S(2)}) %collective-permute-start.4) | collective-permute-done | bytes 131104 | tf_op jit(solution)/shard_map/ppermute | solution.py:363
  31.6 2.8 %collective-permute-done.5.refs_5_ = bf16[4,128,128]{2,1,0:T(8,128)(2,1)S(1)} collective-permute-done((bf16[4,128,128]{2,1,0:T(8,128)(2,1)S(1)}, bf16[4,128,128]{2,1,0:T(8,128)(2,1)S(1)}, u32[]{:S(2)}, u32[]{:S(2)}) %collective-permute-start.5) | collective-permute-done | bytes 131104 | tf_op jit(solution)/shard_map/ppermute | solution.py:363
  34.4 1.1 %shard_map.137 = bf16[128,1024]{1,0:T(8,128)(2,1)} custom-call(bf16[4,128,128]{2,1,0:T(8,128)(2,1)S(1)} %collective-permute-done.s_ref.refs_0_, bf16[4,128,128]{2,1,0:T(8,128)(2,1)S(1)} %collective-permute-done.1.s_ref.refs_1_, bf16[4,128,128]{2,1,0:T(8,128)(2,1)S(1)} %collective-permute-done.2.s_ref.refs_2_, ...), custom_call_target="tpu_custom_call" | custom-call | flops 33554432 | bytes 2097152 | tf_op jit(solution)/shard_map/pallas_call | solution.py:240
  (11 shorter events, 0.0 us)
Async XLA Ops:
  0.7 3.8 %copy-start.11 = (f32[8,128]{1,0:T(8,128)S(1)}, f32[8,128]{1,0:T(8,128)}, u32[]{:S(2)}) copy-start(f32[8,128]{1,0:T(8,128)} %gate_ref.2) | copy-start | bytes 12292
  0.7 3.8 %copy-start.10 = (f32[8,128]{1,0:T(8,128)S(1)}, f32[8,128]{1,0:T(8,128)}, u32[]{:S(2)}) copy-start(f32[8,128]{1,0:T(8,128)} %beta_ref.1) | copy-start | bytes 12292
  0.8 0.9 %copy-start.2 = (bf16[128,512]{1,0:T(8,128)(2,1)S(1)}, bf16[128,512]{1,0:T(8,128)(2,1)}, u32[]{:S(2)}) copy-start(bf16[128,512]{1,0:T(8,128)(2,1)} %k_hbm.3) | copy-start | bytes 393220
  1.7 0.9 %copy-start.3 = (bf16[128,512]{1,0:T(8,128)(2,1)S(1)}, bf16[128,512]{1,0:T(8,128)(2,1)}, u32[]{:S(2)}) copy-start(bf16[128,512]{1,0:T(8,128)(2,1)} %v_hbm.3) | copy-start | bytes 393220
  2.6 2.0 %copy-start.5 = (bf16[128,1024]{1,0:T(8,128)(2,1)S(1)}, bf16[128,1024]{1,0:T(8,128)(2,1)}, u32[]{:S(2)}) copy-start(bf16[128,1024]{1,0:T(8,128)(2,1)} %v_hbm.2) | copy-start | bytes 786436
  3.2 1.3 %copy-start.4 = (s32[128]{0:T(128)S(1)}, s32[128]{0:T(128)}, u32[]{:S(2)}) copy-start(s32[128]{0:T(128)} %param.12) | copy-start | bytes 1540
  3.2 7.4 %collective-permute-start.6 = (bf16[64,512]{1,0:T(8,128)(2,1)S(1)}, bf16[64,512]{1,0:T(8,128)(2,1)S(1)}, u32[]{:S(2)}, u32[]{:S(2)}) collective-permute-start(bf16[64,512]{1,0:T(8,128)(2,1)S(1)} %get-tuple-element.23), channel_id=1, source_target_pairs={{0,4},{4,8},{8,12},{1,5},{5,9},{9,13},{2,6},{6,10},{10,14},{3,7},{... | collective-permute-start | bytes 196616 | tf_op jit(solution)/shard_map/ppermute | solution.py:326
  4.5 0.9 %copy-start.7 = (bf16[128,512]{1,0:T(8,128)(2,1)S(1)}, bf16[128,512]{1,0:T(8,128)(2,1)}, u32[]{:S(2)}) copy-start(bf16[128,512]{1,0:T(8,128)(2,1)} %k_ref.1) | copy-start | bytes 393220
  5.5 6.5 %copy-start.8 = (bf16[128,512]{1,0:T(8,128)(2,1)S(1)}, bf16[128,512]{1,0:T(8,128)(2,1)}, u32[]{:S(2)}) copy-start(bf16[128,512]{1,0:T(8,128)(2,1)} %k_ref.1) | copy-start | bytes 393220
  5.5 6.5 %copy-start.9 = (bf16[128,512]{1,0:T(8,128)(2,1)S(1)}, bf16[128,512]{1,0:T(8,128)(2,1)}, u32[]{:S(2)}) copy-start(bf16[128,512]{1,0:T(8,128)(2,1)} %q_ref.2) | copy-start | bytes 393220
  9.1 2.9 %copy-start.6 = (bf16[128,1024]{1,0:T(8,128)(2,1)S(1)}, bf16[128,1024]{1,0:T(8,128)(2,1)}, u32[]{:S(2)}) copy-start(bf16[128,1024]{1,0:T(8,128)(2,1)} %z_ref.1) | copy-start | bytes 786436
  9.1 5.3 %collective-permute-start = (bf16[4,128,128]{2,1,0:T(8,128)(2,1)S(1)}, bf16[4,128,128]{2,1,0:T(8,128)(2,1)S(1)}, u32[]{:S(2)}, u32[]{:S(2)}) collective-permute-start(bf16[4,128,128]{2,1,0:T(8,128)(2,1)S(1)} %get-tuple-element.13), channel_id=1, source_target_pairs={{0,4},{1,5},{2,6},{3,7},{16,20},{17,21},{18,22},{19,23}} | collective-permute-start | bytes 393224 | tf_op jit(solution)/shard_map/ppermute | solution.py:340
  9.9 5.3 %collective-permute-start.1 = (bf16[4,128,128]{2,1,0:T(8,128)(2,1)S(1)}, bf16[4,128,128]{2,1,0:T(8,128)(2,1)S(1)}, u32[]{:S(2)}, u32[]{:S(2)}) collective-permute-start(bf16[4,128,128]{2,1,0:T(8,128)(2,1)S(1)} %get-tuple-element.14), channel_id=1, source_target_pairs={{0,4},{1,5},{2,6},{3,7},{16,20},{17,21},{18,22},{19,23}} | collective-permute-start | bytes 393224 | tf_op jit(solution)/shard_map/ppermute | solution.py:340
  10.6 8.3 %collective-permute-start.8 = (bf16[128,512]{1,0:T(8,128)(2,1)S(1)}, bf16[128,512]{1,0:T(8,128)(2,1)S(1)}, u32[]{:S(2)}, u32[]{:S(2)}) collective-permute-start(bf16[128,512]{1,0:T(8,128)(2,1)S(1)} %pad_maximum_fusion), channel_id=1, source_target_pairs={{0,8},{4,12},{1,9},{5,13},{2,10},{6,14},{3,11},{7,15},{16,24},{20,... | collective-permute-start | bytes 393224 | tf_op jit(solution)/shard_map/ppermute | solution.py:326
  11.9 0.7 %copy-start.12 = (f32[128]{0:T(128)S(1)}, f32[128]{0:T(128)}, u32[]{:S(2)}) copy-start(f32[128]{0:T(128)} %param.19) | copy-start | bytes 1540
  14.3 7.8 %collective-permute-start.7 = (bf16[64,512]{1,0:T(8,128)(2,1)S(1)}, bf16[64,512]{1,0:T(8,128)(2,1)S(1)}, u32[]{:S(2)}, u32[]{:S(2)}) collective-permute-start(bf16[64,512]{1,0:T(8,128)(2,1)S(1)} %collective-permute-done.6.refs_0_), channel_id=1, source_target_pairs={{0,1},{1,0},{2,3},{3,2},{4,5},{5,4},{6,7},{7,6},{8,9},{9,8},{10,11... | collective-permute-start | bytes 196616 | tf_op jit(solution)/shard_map/ppermute | solution.py:331
  14.6 4.3 %collective-permute-start.2 = (bf16[4,128,128]{2,1,0:T(8,128)(2,1)S(1)}, bf16[4,128,128]{2,1,0:T(8,128)(2,1)S(1)}, u32[]{:S(2)}, u32[]{:S(2)}) collective-permute-start(bf16[4,128,128]{2,1,0:T(8,128)(2,1)S(1)} %shard_map.132), channel_id=1, source_target_pairs={{4,8},{5,9},{6,10},{7,11},{20,24},{21,25},{22,26},{23,27}} | collective-permute-start | bytes 393224 | tf_op jit(solution)/shard_map/ppermute | solution.py:363
  15.5 5.0 %collective-permute-start.3 = (bf16[4,128,128]{2,1,0:T(8,128)(2,1)S(1)}, bf16[4,128,128]{2,1,0:T(8,128)(2,1)S(1)}, u32[]{:S(2)}, u32[]{:S(2)}) collective-permute-start(bf16[4,128,128]{2,1,0:T(8,128)(2,1)S(1)} %shard_map.133), channel_id=1, source_target_pairs={{4,8},{5,9},{6,10},{7,11},{20,24},{21,25},{22,26},{23,27}} | collective-permute-start | bytes 393224 | tf_op jit(solution)/shard_map/ppermute | solution.py:363
  18.9 3.2 %collective-permute-start.9 = (bf16[128,512]{1,0:T(8,128)(2,1)S(1)}, bf16[128,512]{1,0:T(8,128)(2,1)S(1)}, u32[]{:S(2)}, u32[]{:S(2)}) collective-permute-start(bf16[128,512]{1,0:T(8,128)(2,1)S(1)} %collective-permute-done.8), channel_id=1, source_target_pairs={{0,1},{1,0},{2,3},{3,2},{4,5},{5,4},{6,7},{7,6},{8,9},{9,8},{10,11... | collective-permute-start | bytes 393224 | tf_op jit(solution)/shard_map/ppermute | solution.py:331
  19.1 12.5 %collective-permute-start.4 = (bf16[4,128,128]{2,1,0:T(8,128)(2,1)S(1)}, bf16[4,128,128]{2,1,0:T(8,128)(2,1)S(1)}, u32[]{:S(2)}, u32[]{:S(2)}) collective-permute-start(bf16[4,128,128]{2,1,0:T(8,128)(2,1)S(1)} %shard_map.134), channel_id=1, source_target_pairs={{8,12},{9,13},{10,14},{11,15},{24,28},{25,29},{26,30},{27,31}} | collective-permute-start | bytes 393224 | tf_op jit(solution)/shard_map/ppermute | solution.py:363
  20.4 1.7 %copy-start.1 = (bf16[128,1024]{1,0:T(8,128)(2,1)S(1)}, bf16[128,1024]{1,0:T(8,128)(2,1)}, u32[]{:S(2)}) copy-start(bf16[128,1024]{1,0:T(8,128)(2,1)} %gate_ref.3) | copy-start | bytes 786436
  20.6 1.5 %copy-start = (bf16[128,1024]{1,0:T(8,128)(2,1)S(1)}, bf16[128,1024]{1,0:T(8,128)(2,1)}, u32[]{:S(2)}) copy-start(bf16[128,1024]{1,0:T(8,128)(2,1)} %q_ref.3) | copy-start | bytes 786436
  20.6 13.8 %collective-permute-start.5 = (bf16[4,128,128]{2,1,0:T(8,128)(2,1)S(1)}, bf16[4,128,128]{2,1,0:T(8,128)(2,1)S(1)}, u32[]{:S(2)}, u32[]{:S(2)}) collective-permute-start(bf16[4,128,128]{2,1,0:T(8,128)(2,1)S(1)} %shard_map.135), channel_id=1, source_target_pairs={{8,12},{9,13},{10,14},{11,15},{24,28},{25,29},{26,30},{27,31}} | collective-permute-start | bytes 393224 | tf_op jit(solution)/shard_map/ppermute | solution.py:363

commit v3 on v2

v3 whole, which is shorter than its diff:
```python
import functools

import jax
import jax.numpy as jnp
from jax import lax
from jax.experimental import pallas as pl
from jax.experimental.pallas import tpu as pltpu
from jax.sharding import PartitionSpec as P

DK = 128
DV = 128
QH = 16
KVH = 2
HD_A = 256
EPS = 1e-06
VMEM_LIMIT = 48 * 1024 * 1024
PIECES = 2

F32 = jnp.float32
BF16 = jnp.bfloat16


def dot(a, b):
    return jnp.dot(a, b, preferred_element_type=F32)


def dot_t(a, b):
    return lax.dot_general(a, b, (((1,), (1,)), ((), ())), preferred_element_type=F32)


def prefix_sums(rows):
    count, length = rows.shape
    first = rows.astype(BF16)
    rest = rows - first.astype(F32)
    second = rest.astype(BF16)
    third = (rest - second.astype(F32)).astype(BF16)
    t_at = lax.broadcasted_iota(jnp.int32, (length, length), 0)
    i_at = lax.broadcasted_iota(jnp.int32, (length, length), 1)
    ones = (t_at <= i_at).astype(F32).astype(BF16)
    return dot(first, ones) + dot(second, ones) + dot(third, ones)


def columns_of(rows):
    count, length = rows.shape
    padded = jnp.concatenate([rows, jnp.zeros((length - count, length), F32)], axis=0)
    return padded.T


def diagonal_row(square, same_place):
    return jnp.sum(jnp.where(same_place, square, 0.0), axis=0, keepdims=True)


def places(length):
    row = lax.broadcasted_iota(jnp.int32, (length, length), 0)
    col = lax.broadcasted_iota(jnp.int32, (length, length), 1)
    return row, col


def state_terms(scalar_ref, inputs, u_ref, w_ref=None, a_ref=None, m_ref=None, send_refs=()):
    k_ref, gate_ref, beta_ref, doc_ref, v_ref = inputs
    doc = doc_ref[...]
    anchor = scalar_ref[0]
    length = k_ref.shape[0]
    heads = beta_ref.shape[0]
    key_heads = k_ref.shape[1] // DK
    repeat = heads // key_heads
    row, col = places(length)
    beta = jax.nn.sigmoid(beta_ref[...])
    running = prefix_sums(gate_ref[...])
    keys = [k_ref[:, g * DK : (g + 1) * DK] for g in range(key_heads)]
    grams = [dot_t(k, k) for k in keys]
    squares = [diagonal_row(g, row == col) + EPS for g in grams]
    log_inv = [-0.5 * jnp.log(s) for s in squares]
    inv = [lax.rsqrt(s) for s in squares]
    log_rows = jnp.concatenate([log_inv[h // repeat] for h in range(heads)], axis=0)
    cols = columns_of(
        jnp.concatenate([running + log_rows, jnp.broadcast_to(doc.astype(F32), (8, length))], axis=0)
    )
    doc_col = cols[:, heads : heads + 1]
    place = (anchor + col).astype(F32)
    strict = (doc_col <= place) & (col < row)
    tail_same = doc[:, length - 1 : length] <= (anchor + col[:1, :])
    systems = []
    for h in range(heads):
        spread = cols[:, h : h + 1] - running[h : h + 1, :]
        decay = jnp.where(strict, jnp.exp(spread), 0.0)
        weight = beta[h : h + 1, :] * inv[h // repeat]
        systems.append(decay * grams[h // repeat] * weight)
    differ = row ^ col
    inverse = [jnp.where(row == col, 1.0, 0.0) - jnp.where(differ == 1, n, 0.0) for n in systems]
    level = 1
    while (1 << level) < length:
        mask = (differ >> level) == 1
        short = [x.astype(BF16) for x in inverse]
        inner = [
            dot(jnp.where(mask, n, 0.0).astype(BF16), x).astype(BF16) for n, x in zip(systems, short)
        ]
        inverse = [x - dot(s, y) for x, s, y in zip(inverse, short, inner)]
        level += 1
    keys_t = [k.astype(F32).T for k in keys]
    for h in range(heads):
        g = h // repeat
        run = running[h : h + 1, :]
        u = dot(inverse[h].astype(BF16), v_ref[:, h * DV : (h + 1) * DV]).astype(BF16)
        u_ref[h] = u
        tail = jnp.exp(run[:, length - 1 : length] - run)
        tail = jnp.where(tail_same, tail, 0.0) * beta[h : h + 1, :] * inv[g]
        tail_keys = (keys_t[g] * tail).astype(BF16)
        a = dot(tail_keys, u)
        if send_refs:
            piece = heads // len(send_refs)
            send_refs[h // piece][h % piece] = a.astype(BF16)
            continue
        a_ref[h] = a
        entry = jnp.where(doc < anchor, jnp.exp(run), 0.0)
        w = dot((inverse[h] * (entry * inv[g])).astype(BF16), keys[g]).astype(BF16)
        w_ref[h] = w
        m_ref[h] = (jnp.where(row == col, entry[:, length - 1 : length], 0.0) - dot(tail_keys, w)).astype(BF16)


def opening_kernel(scalar_ref, *refs):
    sources, (ka_hbm, va_hbm) = refs[:6], refs[6:8]
    inputs, (unit_ref, u_ref), send_refs, sems = refs[8:14], refs[14:16], refs[16:-1], refs[-1]
    groups = HD_A // DK
    rows = unit_ref.shape[0] // (2 * groups)
    column = pl.multiple_of(scalar_ref[1], HD_A)
    begin = pl.multiple_of(scalar_ref[2], rows)
    pairs = list(zip(sources, inputs))
    for at in range(2 * groups):
        source = (ka_hbm, va_hbm)[at // groups].at[pl.ds(begin, rows), pl.ds(column + at % groups * DK, DK)]
        pairs.append((source, unit_ref.at[pl.ds(at * rows, rows)]))
    copies = [pltpu.make_async_copy(a, b, sems.at[i]) for i, (a, b) in enumerate(pairs)]
    for copy in copies:
        copy.start()
    for copy in copies:
        copy.wait()

    @pl.when(scalar_ref[0] == 0)
    def _():
        state_terms(scalar_ref, inputs[:5], u_ref, send_refs=send_refs)


def second_kernel(scalar_ref, *refs):
    inputs, (_, u_ref, w_ref, a_ref, m_ref) = refs[:5], refs[5:]
    length = u_ref.shape[1]

    @pl.when(scalar_ref[0] == 0)
    def _():
        w_ref[...] = jnp.zeros(w_ref.shape, BF16)

    @pl.when(scalar_ref[0] == length)
    def _():
        state_terms(scalar_ref, inputs, u_ref, w_ref, a_ref, m_ref)


def later_kernel(scalar_ref, *refs):
    inputs, outs = refs[:5], refs[9:]
    length = outs[0].shape[1]

    @pl.when(scalar_ref[0] > length)
    def _():
        state_terms(scalar_ref, inputs, *outs)


def query_kernel(
    scalar_ref, doc_ref, beta_ref, gate_ref, q_ref, k_ref, z_ref, gain_ref, u_ref, w_ref, local_ref, reach_ref, gz_ref
):
    length = k_ref.shape[0]
    heads = beta_ref.shape[0]
    key_heads = k_ref.shape[1] // DK
    repeat = heads // key_heads
    anchor = scalar_ref[0]
    row, col = places(length)
    beta = jax.nn.sigmoid(beta_ref[...])
    running = prefix_sums(gate_ref[...])
    doc = doc_ref[...]
    keys = [k_ref[:, g * DK : (g + 1) * DK] for g in range(key_heads)]
    queries = [q_ref[:, g * DK : (g + 1) * DK] for g in range(key_heads)]
    inv = [lax.rsqrt(diagonal_row(dot_t(k, k), row == col) + EPS) for k in keys]
    log_q = [-0.5 * jnp.log(diagonal_row(dot_t(q, q), row == col) + EPS) for q in queries]
    log_rows = jnp.concatenate([log_q[h // repeat] for h in range(heads)], axis=0)
    cols = columns_of(
        jnp.concatenate([running + log_rows, jnp.broadcast_to(doc.astype(F32), (8, length))], axis=0)
    )
    doc_col = cols[:, heads : heads + 1]
    place = (anchor + col).astype(F32)
    same = (doc_col <= place) & (col <= row)
    alive_col = doc_col < anchor.astype(F32)
    cross = [dot_t(q, k) for q, k in zip(queries, keys)]
    for h in range(heads):
        g = h // repeat
        weight = beta[h : h + 1, :] * inv[g]
        decay = jnp.where(same, jnp.exp(cols[:, h : h + 1] - running[h : h + 1, :]), 0.0)
        scores = (decay * cross[g] * weight).astype(BF16)
        local_ref[h] = dot(scores, u_ref[h])
        lead = jnp.where(alive_col, jnp.exp(cols[:, h : h + 1]), 0.0)
        reach_ref[h] = (lead * queries[g].astype(F32) - dot(scores, w_ref[h])).astype(BF16)
    z = z_ref[...].astype(F32)
    gate = z / (1.0 + jnp.exp(-z))
    for h in range(heads):
        gz_ref[h] = gate[:, h * DV : (h + 1) * DV] * gain_ref[...]


def combine_kernel(begin, s_ref, m_ref, a_ref, out_ref):
    for h in range(s_ref.shape[0]):
        out_ref[h] = (dot(m_ref[begin + h], s_ref[h]) + a_ref[begin + h]).astype(BF16)


def normed_piece(begin, states, local_ref, reach_ref, gz_ref, out_ref, columns):
    for at in range(states[0].shape[0]):
        state = states[0][at]
        for other in states[1:]:
            state = state + other[at]
        h = begin + at
        mixed = local_ref[h] + dot(reach_ref[h], state)
        factor = lax.rsqrt(jnp.mean(mixed * mixed, axis=-1, keepdims=True) + EPS)
        spot = columns + at * DV
        out_ref[:, spot : spot + DV] = (mixed * factor * gz_ref[h]).astype(BF16)


def piece_kernel(begin, hops, *refs):
    normed_piece(begin, refs[:hops], *refs[hops:], 0)


def output_kernel(begin, hops, *refs):
    states, terms, ready = refs[:hops], refs[hops : hops + 3], refs[hops + 3 : -3]
    out_hbm, held_ref, sems = refs[-3:]
    copies = []
    spot = 0
    for at, part in enumerate((*ready, held_ref)):
        if part is held_ref:
            normed_piece(begin, states, *terms, held_ref, 0)
        width = part.shape[1]
        copies.append(pltpu.make_async_copy(part, out_hbm.at[:, spot : spot + width], sems.at[at]))
        copies[-1].start()
        spot += width
    for copy in copies:
        copy.wait()


def attention_kernel(window, layout, scalar_ref, doc_ref, q_ref, gate_ref, k_ref, v_ref, *refs):
    units, (out_hbm, held_ref, sems) = refs[:-3], refs[-3:]
    length = q_ref.shape[0]
    heads = q_ref.shape[1] // HD_A
    groups = HD_A // DK
    anchor = scalar_ref[0]
    docs = columns_of(jnp.broadcast_to(doc_ref[...].astype(F32), (8, length)))[:, :1].astype(jnp.int32)
    q_place = anchor + lax.broadcasted_iota(jnp.int32, (length, 1), 0)
    lower = jnp.maximum(jnp.maximum(docs, q_place - window + 1), 0)
    spots = [anchor + lax.broadcasted_iota(jnp.int32, (length, length), 1)]
    wanted = pl.ds(pl.multiple_of(scalar_ref[1], HD_A), HD_A)
    keys, values = [k_ref[:, wanted]], [v_ref[:, wanted]]
    for (distance, turn), unit in zip(layout, units):
        rows = unit.shape[0] // (2 * groups)
        start = anchor - distance * length + scalar_ref[2 + turn]
        spots.append(start + lax.broadcasted_iota(jnp.int32, (length, rows), 1))
        blocks = [unit[at * rows : (at + 1) * rows] for at in range(2 * groups)]
        keys.append(jnp.concatenate(blocks[:groups], axis=1))
        values.append(jnp.concatenate(blocks[groups:], axis=1))
    k_place = jnp.concatenate(spots, axis=1)
    visible = (k_place >= lower) & (k_place <= q_place)
    keys = jnp.concatenate(keys, axis=0)
    values = jnp.concatenate(values, axis=0)
    step = 2
    copies = []
    for first in range(0, heads, step):
        names = range(first, min(first + step, heads))
        queries = jnp.concatenate([q_ref[:, h * HD_A : (h + 1) * HD_A] for h in names], axis=0)
        scores = dot_t(queries * BF16(HD_A**-0.5), keys)
        scores = jnp.where(jnp.concatenate([visible] * len(names), axis=0), scores, -jnp.inf)
        peak = jnp.max(scores, axis=-1, keepdims=True)
        weights = jnp.exp(scores - peak)
        total = jnp.sum(weights, axis=-1, keepdims=True)
        mixed = dot(weights.astype(BF16), values)
        for at, h in enumerate(names):
            part = slice(h * HD_A, (h + 1) * HD_A)
            rows = slice(at * length, (at + 1) * length)
            gate = 1.0 + jnp.exp(-gate_ref[:, part].astype(F32))
            held_ref[:, part] = (mixed[rows] / (total[rows] * gate)).astype(BF16)
            copy = pltpu.make_async_copy(held_ref.at[:, part], out_hbm.at[:, part], sems.at[h])
            copy.start()
            copies.append(copy)
    for copy in copies:
        copy.wait()


def call(kernel, out_shape, operands, flops, scalars=1, outside=0, scratch=(), aliases=None, held=pltpu.VMEM):
    moved = sum(o.size * o.dtype.itemsize for o in operands)
    inside = len(operands) - scalars - outside
    operands = [
        pltpu.with_memory_space_constraint(o, pltpu.HBM) if scalars <= i < scalars + outside else o
        for i, o in enumerate(operands)
    ]
    specs = [pl.BlockSpec(memory_space=pltpu.SMEM)] * scalars
    specs += [pl.BlockSpec(memory_space=pltpu.HBM)] * outside
    specs += [pl.BlockSpec(memory_space=pltpu.VMEM)] * inside
    if held is not pltpu.VMEM and aliases:
        specs[-1] = pl.BlockSpec(memory_space=held)
    return pl.pallas_call(
        kernel,
        out_shape=out_shape,
        in_specs=specs,
        out_specs=jax.tree.map(lambda _: pl.BlockSpec(memory_space=held), out_shape),
        scratch_shapes=scratch,
        input_output_aliases=aliases or {},
        compiler_params=pltpu.CompilerParams(vmem_limit_bytes=VMEM_LIMIT),
        cost_estimate=pl.CostEstimate(flops=flops, bytes_accessed=moved, transcendentals=0),
    )(*operands)


def after(value, *others):
    return lax.optimization_barrier((value, *others))[0]


def shards(
    doc_start,
    q_gdn,
    k_gdn,
    v_gdn,
    z_gdn,
    beta_logit,
    log_decay,
    norm_weight,
    q_attn,
    k_attn,
    v_attn,
    gate_attn,
):
    devices = lax.axis_size("seq")
    length = q_gdn.shape[0]
    heads = v_gdn.shape[1] // DV
    local_heads = q_attn.shape[1] // HD_A
    group = QH // KVH
    head_devices = lax.axis_size("head")
    sharers = max(1, min(group // local_heads, head_devices))
    rows = length // sharers
    place = lax.axis_index("seq").astype(jnp.int32)
    head_at = lax.axis_index("head").astype(jnp.int32)
    kv_head = head_at * local_heads // group
    share = head_at % sharers
    scalars = jnp.stack(
        [place * length, kv_head * HD_A] + [(share + sharers - t) % sharers * rows for t in range(sharers)]
    )
    docs = doc_start.reshape(1, length)
    shape = jax.ShapeDtypeStruct
    pieces = PIECES if heads % PIECES == 0 else 1

    sources = (k_gdn, log_decay, beta_logit, docs, v_gdn, norm_weight.reshape(1, DV))
    terms = (
        shape((heads, length, DV), BF16),
        shape((heads, length, DK), BF16),
        shape((heads, DK, DV), F32),
        shape((heads, DK, DK), BF16),
    )
    work = 100 * heads * length * DK * DV
    piece = heads // pieces
    groups = HD_A // DK
    opened = call(
        opening_kernel,
        (
            *[shape(a.shape, a.dtype) for a in sources],
            shape((2 * groups * rows, DK), BF16),
            terms[0],
            *[shape((piece, DK, DV), BF16)] * pieces,
        ),
        (scalars, *sources, k_attn, v_attn),
        work,
        outside=len(sources) + 2,
        scratch=[pltpu.SemaphoreType.DMA((len(sources) + 2 * groups,))],
    )
    inputs, (gain_in, unit, fresh), leaving = opened[:5], opened[5:8], opened[8:]

    def hand_on(hop, pieces_out):
        return [lax.ppermute(s, "seq", [(hop, hop + 1)]) for s in pieces_out]

    def combined(got, carry, added, between=None):
        done = []
        for at, state in enumerate(got):
            if at == 1 and between:
                state = after(state, *between(done[0]))
            elif done:
                state = after(state, done[-1])
            done.append(
                call(
                    functools.partial(combine_kernel, at * piece),
                    shape((piece, DK, DV), BF16),
                    (state, carry, added),
                    2 * piece * DK * DK * DV,
                    0,
                )
            )
        return done

    def swapped(got, turn):
        pairs = [(i, i // sharers * sharers + (i + turn) % sharers) for i in range(head_devices)]
        return lax.ppermute(got, "head", pairs)

    wanted = min(devices // 2 + 1, devices - 1)
    arrived = [hand_on(0, leaving)]
    fresh, erased, added, carry = call(
        second_kernel, terms, (scalars, *inputs, fresh), work, aliases={6: 0}
    )
    unit = after(unit, fresh)
    units = [lax.ppermute(unit, "seq", [(i, i + 1) for i in range(devices - 1)])]
    direct = wanted == devices - 1 and wanted > 1
    farthest = [lax.ppermute(unit, "seq", [(0, wanted)])] if direct else []
    leaving = combined(arrived[-1], carry, added)
    arrived.append(hand_on(1, leaving))
    block = after(units[0], leaving[-1])
    for distance in range(2, wanted + 1 - direct):
        block = lax.ppermute(block, "seq", [(i, i + 1) for i in range(distance - 1, devices - 1)])
        units.append(block)
    units += farthest
    fresh, erased, added, carry = call(
        later_kernel,
        terms,
        (scalars, *inputs, after(fresh, leaving[-1]), erased, added, carry),
        work,
        aliases={6: 0, 7: 1, 8: 2, 9: 3},
    )
    def queries(first):
        mixing.extend(call(
            query_kernel,
            (
                shape((heads, length, DV), F32),
                shape((heads, length, DK), BF16),
                shape((heads, length, DV), F32),
            ),
            (
                *(scalars, inputs[3], inputs[2], inputs[1], q_gdn, inputs[0], z_gdn, gain_in),
                *(after(fresh, first), erased),
            ),
            work,
        ))
        return mixing[:1]

    mixing = []
    for hop in range(2, devices - 1):
        leaving = combined(arrived[-1], carry, added, queries if hop == 2 else None)
        arrived.append(hand_on(hop, leaving))
    local_out, reach, gain = mixing

    layout, sections = [], []
    for distance, got in enumerate(units, 1):
        for turn in range(sharers):
            layout.append((distance, turn))
            sections.append(swapped(after(got, leaving[-1]), turn) if turn else got)
    attn_out = call(
        functools.partial(attention_kernel, (devices // 2 + 1) * length, layout),
        shape(q_attn.shape, BF16),
        (scalars, inputs[3], q_attn, gate_attn, k_attn, v_attn, *sections),
        4 * local_heads * length * length * (wanted + 1) * HD_A,
        scratch=[pltpu.VMEM(q_attn.shape, BF16), pltpu.SemaphoreType.DMA((local_heads,))],
        held=pltpu.HBM,
    )
    ready = []
    for at in range(pieces):
        states = [got[at] for got in arrived]
        operands = (*states, after(local_out, attn_out), reach, gain)
        cost = 2 * piece * length * DK * DV
        if at < pieces - 1:
            ready.append(
                call(
                    functools.partial(piece_kernel, at * piece, len(states)),
                    shape((length, piece * DV), BF16),
                    operands,
                    cost,
                    0,
                )
            )
    gdn_out = call(
        functools.partial(output_kernel, at * piece, len(states)),
        shape(v_gdn.shape, BF16),
        (*operands, *ready),
        cost,
        0,
        scratch=[pltpu.VMEM((length, piece * DV), BF16), pltpu.SemaphoreType.DMA((pieces,))],
        held=pltpu.HBM,
    )
    return (gdn_out, attn_out)


def solution(mesh):
    tokens = P(("groups", "seq"))
    both = P(("groups", "seq"), "head")
    return jax.shard_map(
        shards,
        mesh=mesh,
        in_specs=(
            tokens,
            both,
            both,
            both,
            both,
            P("head", ("groups", "seq")),
            P("head", ("groups", "seq")),
            P(),
            both,
            P(("groups", "seq"), None),
            P(("groups", "seq"), None),
            both,
        ),
        out_specs=(both, both),
        check_vma=False,
    )
```

time: 35.8 us -> 29.1 us (0.81)
  the two profiles are of different devices: /device:TPU:26 before, /device:TPU:19 now
where the time goes in v3:
time: 29.1 us; the launch traced here: 28.8 us
  starting transfers between devices  14.6 us (50%)
  Pallas kernels  11.3 us (39%)
  waiting for transfers between devices  1.82 us (6%)
  between operations  0.92 us (3%)
    pallas_call x11, Pallas kernels, call(): pl.pallas_call(kernel, out_shape=out_shape, in_specs=specs, out_specs=jax...  11.3 us
    ppermute x6, starting transfers between devices, hand_on(): return [lax.ppermute(s, 'seq', [(hop, hop + 1)]) for s in pieces_out]  6.52 us
    ppermute x1, starting transfers between devices, shards(): lax.ppermute(unit, 'seq', [(i, i + 1) for i in range(devices - 1)])  3.2 us
    ppermute x3, starting transfers between devices, swapped(): return lax.ppermute(got, 'head', pairs)  2.35 us
    ppermute x1, starting transfers between devices, shards(): lax.ppermute(block, 'seq', [(i, i + 1) for i in range(distance - 1, devic...  1.91 us
    ppermute x3, waiting for transfers between devices, swapped(): return lax.ppermute(got, 'head', pairs)  0.9 us
    ppermute x1, waiting for transfers between devices, shards(): lax.ppermute(unit, 'seq', [(i, i + 1) for i in range(devices - 1)])  0.79 us
    ppermute x1, starting transfers between devices, shards(): farthest = [lax.ppermute(unit, 'seq', [(0, wanted)])] if direct else []  0.66 us
  transfers between devices with their start and end apart: 12, of which 5 were waited for; matrix products, arithmetic and copies ran while one was open for 0% of the time, Pallas kernels for 30%

profile of v3, /device:TPU:19, one launch (start us, length us, event | category | flops | bytes accessed | tf_op | source)
XLA Modules:
  0.0 28.8 jit_solution(1973013107638687618)
XLA Ops:
  0.7 0.1 pad_add_fusion.scalar_ref
  0.7 1.7 %shard_map.131 = (bf16[128,512]{1,0:T(8,128)(2,1)S(1)}, f32[8,128]{1,0:T(8,128)S(1)}, f32[8,128]{1,0:T(8,128)S(1)}, s32[1,128]{1,0:T(1,128)S(1)}, bf16[128,1024]...) custom-call(s32[4]{0:T(128)S(1)} %pad_add_fusion.scalar_ref, ...), custom_call_target="tpu_custom_call" | custom-call | flops 1677721600 | bytes 664592 | tf_op jit(solution)/shard_map/pallas_call | solution.py:299
  2.5 0.7 %collective-permute-start.1 = (bf16[4,128,128]{2,1,0:T(8,128)(2,1)S(1)}, bf16[4,128,128]{2,1,0:T(8,128)(2,1)S(1)}, u32[]{:S(2)}, u32[]{:S(2)}) collective-permute-start(bf16[4,128,128]{2,1,0:T(8,128)(2,1)S(1)} %get-tuple-element.34), channel_id=1, source_target_pairs={{0,4},{1,5},{2,6},{3,7},{16,20},{17,21},{18,22},{19,23}} | collective-permute-start | bytes 393224 | tf_op jit(solution)/shard_map/ppermute | solution.py:374
  3.1 0.7 %collective-permute-start = (bf16[4,128,128]{2,1,0:T(8,128)(2,1)S(1)}, bf16[4,128,128]{2,1,0:T(8,128)(2,1)S(1)}, u32[]{:S(2)}, u32[]{:S(2)}) collective-permute-start(bf16[4,128,128]{2,1,0:T(8,128)(2,1)S(1)} %get-tuple-element.33), channel_id=1, source_target_pairs={{0,4},{1,5},{2,6},{3,7},{16,20},{17,21},{18,22},{19,23}} | collective-permute-start | bytes 393224 | tf_op jit(solution)/shard_map/ppermute | solution.py:374
  3.8 0.6 %shard_map.132 = (bf16[8,128,128]{2,1,0:T(8,128)(2,1)S(1)}, bf16[8,128,128]{2,1,0:T(8,128)(2,1)S(1)}, f32[8,128,128]{2,1,0:T(8,128)S(1)}, bf16[8,128,128]{2,1,0:T(8,128)(2,1)S(1)}) custom-call(s32[4]{0:T(128)S(1)} %pad_add_fusion.scalar_ref, bf16[128,512]{1,0:T(8,128)(2,1)S(1)} %get-tuple-element.35.refs_0_.k_ref, ...), custom_call_target="tpu_custom_call", output_to_operand_aliasing={{0}: (6, {})} | custom-call | flops 1677721600 | bytes 664080 | tf_op jit(solution)/shard_map/pallas_call | solution.py:299
  4.4 3.2 %collective-permute-start.5 = (bf16[256,128]{1,0:T(8,128)(2,1)S(1)}, bf16[256,128]{1,0:T(8,128)(2,1)S(1)}, u32[]{:S(2)}, u32[]{:S(2)}) collective-permute-start(bf16[256,128]{1,0:T(8,128)(2,1)S(1)} %get-tuple-element.56), channel_id=1, source_target_pairs={{0,4},{4,8},{8,12},{1,5},{5,9},{9,13},{2,6},{6,10},{10,14},{3,7},{... | collective-permute-start | bytes 196616 | tf_op jit(solution)/shard_map/ppermute | solution.py:404
  7.6 0.7 %collective-permute-start.9 = (bf16[256,128]{1,0:T(8,128)(2,1)S(1)}, bf16[256,128]{1,0:T(8,128)(2,1)S(1)}, u32[]{:S(2)}, u32[]{:S(2)}) collective-permute-start(bf16[256,128]{1,0:T(8,128)(2,1)S(1)} %get-tuple-element.56), channel_id=1, source_target_pairs={{0,12},{1,13},{2,14},{3,15},{16,28},{17,29},{18,30},{19,31}} | collective-permute-start | bytes 196616 | tf_op jit(solution)/shard_map/ppermute | solution.py:406
  8.3 0.0 collective-permute-done.1.s_ref.refs_0_
  8.3 0.2 shard_map.133
  8.5 1.3 %collective-permute-start.3 = (bf16[4,128,128]{2,1,0:T(8,128)(2,1)S(1)}, bf16[4,128,128]{2,1,0:T(8,128)(2,1)S(1)}, u32[]{:S(2)}, u32[]{:S(2)}) collective-permute-start(bf16[4,128,128]{2,1,0:T(8,128)(2,1)S(1)} %shard_map.133), channel_id=1, source_target_pairs={{4,8},{5,9},{6,10},{7,11},{20,24},{21,25},{22,26},{23,27}} | collective-permute-start | bytes 393224 | tf_op jit(solution)/shard_map/ppermute | solution.py:374
  9.8 0.0 collective-permute-done.s_ref.refs_0_
  9.8 0.2 shard_map.134
  10.0 1.3 %collective-permute-start.2 = (bf16[4,128,128]{2,1,0:T(8,128)(2,1)S(1)}, bf16[4,128,128]{2,1,0:T(8,128)(2,1)S(1)}, u32[]{:S(2)}, u32[]{:S(2)}) collective-permute-start(bf16[4,128,128]{2,1,0:T(8,128)(2,1)S(1)} %shard_map.134), channel_id=1, source_target_pairs={{4,8},{5,9},{6,10},{7,11},{20,24},{21,25},{22,26},{23,27}} | collective-permute-start | bytes 393224 | tf_op jit(solution)/shard_map/ppermute | solution.py:374
  11.3 0.8 %collective-permute-done.5.refs_0_ = bf16[256,128]{1,0:T(8,128)(2,1)S(1)} collective-permute-done((bf16[256,128]{1,0:T(8,128)(2,1)S(1)}, bf16[256,128]{1,0:T(8,128)(2,1)S(1)}, u32[]{:S(2)}, u32[]{:S(2)}) %collective-permute-start.5) | collective-permute-done | bytes 65568 | tf_op jit(solution)/shard_map/ppermute | solution.py:404
  12.1 1.9 %collective-permute-start.7 = (bf16[256,128]{1,0:T(8,128)(2,1)S(1)}, bf16[256,128]{1,0:T(8,128)(2,1)S(1)}, u32[]{:S(2)}, u32[]{:S(2)}) collective-permute-start(bf16[256,128]{1,0:T(8,128)(2,1)S(1)} %collective-permute-done.5.refs_0_), channel_id=1, source_target_pairs={{4,8},{8,12},{5,9},{9,13},{6,10},{10,14},{7,11},{11,15},{20,24},{2... | collective-permute-start | bytes 196616 | tf_op jit(solution)/shard_map/ppermute | solution.py:411
  14.0 3.2 %shard_map.135 = (bf16[8,128,128]{2,1,0:T(8,128)(2,1)S(1)}, bf16[8,128,128]{2,1,0:T(8,128)(2,1)S(1)}, f32[8,128,128]{2,1,0:T(8,128)S(1)}, bf16[8,128,128]{2,1,0:T(8,128)(2,1)S(1)}) custom-call(s32[4]{0:T(128)S(1)} %pad_add_fusion.scalar_ref, ...), custom_call_target="tpu_custom_call", output_to_operand_aliasing={{0}: (6, {}), {1}: (7, {}), {2}: (8, {}), {3}: (9, {})} | custom-call | flops 1677721600 | bytes 1712656 | tf_op jit(solution)/shard_map/pallas_call | solution.py:299
  17.2 0.1 collective-permute-done.3.s_ref.refs_1_
  17.3 0.0 copy-start.4
  17.3 0.0 copy-start.5
  17.3 0.2 shard_map.136
  17.5 1.3 %collective-permute-start.11 = (bf16[4,128,128]{2,1,0:T(8,128)(2,1)S(1)}, bf16[4,128,128]{2,1,0:T(8,128)(2,1)S(1)}, u32[]{:S(2)}, u32[]{:S(2)}) collective-permute-start(bf16[4,128,128]{2,1,0:T(8,128)(2,1)S(1)} %shard_map.136), channel_id=1, source_target_pairs={{8,12},{9,13},{10,14},{11,15},{24,28},{25,29},{26,30},{27,31}} | collective-permute-start | bytes 393224 | tf_op jit(solution)/shard_map/ppermute | solution.py:374
  18.8 0.0 copy-done.4
  18.8 0.0 copy-done.5
  18.9 1.7 %shard_map.137 = (f32[8,128,128]{2,1,0:T(8,128)S(1)}, bf16[8,128,128]{2,1,0:T(8,128)(2,1)S(1)}, f32[8,128,128]{2,1,0:T(8,128)S(1)}) custom-call(s32[4]{0:T(128)S(1)} %pad_add_fusion.scalar_ref, s32[1,128]{1,0:T(1,128)S(1)} %get-tuple-element.38.refs_3_.doc_ref, f32[8,128]{1,0:T(8,128)S(1)} %get-tuple-element.37.refs_2_.beta_ref, ...), custom_call_target="tpu_custom_call" | custom-call | flops 1677721600 | bytes 1057808 | tf_op jit(solution)/shard_map/pallas_call | solution.py:299
  20.6 0.0 collective-permute-done.2.s_ref.refs_1_
  20.6 0.0 copy-start
  20.6 0.0 copy-start.1
  20.6 0.0 copy-start.2
  20.6 0.0 copy-start.3
  20.6 0.2 shard_map.138
  20.8 1.3 %collective-permute-start.4 = (bf16[4,128,128]{2,1,0:T(8,128)(2,1)S(1)}, bf16[4,128,128]{2,1,0:T(8,128)(2,1)S(1)}, u32[]{:S(2)}, u32[]{:S(2)}) collective-permute-start(bf16[4,128,128]{2,1,0:T(8,128)(2,1)S(1)} %shard_map.138), channel_id=1, source_target_pairs={{8,12},{9,13},{10,14},{11,15},{24,28},{25,29},{26,30},{27,31}} | collective-permute-start | bytes 393224 | tf_op jit(solution)/shard_map/ppermute | solution.py:374
  22.1 0.0 collective-permute-done.9.refs_4_
  22.1 1.8 %collective-permute-start.10 = (bf16[256,128]{1,0:T(8,128)(2,1)S(1)}, bf16[256,128]{1,0:T(8,128)(2,1)S(1)}, u32[]{:S(2)}, u32[]{:S(2)}) collective-permute-start(bf16[256,128]{1,0:T(8,128)(2,1)S(1)} %collective-permute-done.9.refs_4_), channel_id=1, source_target_pairs={{0,1},{1,0},{2,3},{3,2},{4,5},{5,4},{6,7},{7,6},{8,9},{9,8},{10,11... | collective-permute-start | bytes 196616 | tf_op jit(solution)/shard_map/ppermute | solution.py:396
  24.0 0.0 collective-permute-done.7.refs_2_
  24.0 0.1 collective-permute-start.8
  24.1 0.4 %collective-permute-start.6 = (bf16[256,128]{1,0:T(8,128)(2,1)S(1)}, bf16[256,128]{1,0:T(8,128)(2,1)S(1)}, u32[]{:S(2)}, u32[]{:S(2)}) collective-permute-start(bf16[256,128]{1,0:T(8,128)(2,1)S(1)} %collective-permute-done.5.refs_0_), channel_id=1, source_target_pairs={{0,1},{1,0},{2,3},{3,2},{4,5},{5,4},{6,7},{7,6},{8,9},{9,8},{10,11... | collective-permute-start | bytes 196616 | tf_op jit(solution)/shard_map/ppermute | solution.py:396
  24.5 0.4 %collective-permute-done.10.refs_5_ = bf16[256,128]{1,0:T(8,128)(2,1)S(1)} collective-permute-done((bf16[256,128]{1,0:T(8,128)(2,1)S(1)}, bf16[256,128]{1,0:T(8,128)(2,1)S(1)}, u32[]{:S(2)}, u32[]{:S(2)}) %collective-permute-start.10) | collective-permute-done | bytes 65568 | tf_op jit(solution)/shard_map/ppermute | solution.py:396
  24.9 0.4 %collective-permute-done.8.refs_3_ = bf16[256,128]{1,0:T(8,128)(2,1)S(1)} collective-permute-done((bf16[256,128]{1,0:T(8,128)(2,1)S(1)}, bf16[256,128]{1,0:T(8,128)(2,1)S(1)}, u32[]{:S(2)}, u32[]{:S(2)}) %collective-permute-start.8) | collective-permute-done | bytes 65568 | tf_op jit(solution)/shard_map/ppermute | solution.py:396
  25.2 0.2 collective-permute-done.6.refs_1_
  25.4 0.0 copy-done
  25.4 0.0 copy-done.1
  25.4 0.0 copy-done.2
  25.4 0.0 copy-done.3
  25.4 2.0 %shard_map.139 = bf16[128,1024]{1,0:T(8,128)(2,1)} custom-call(s32[4]{0:T(128)S(1)} %pad_add_fusion.scalar_ref, s32[1,128]{1,0:T(1,128)S(1)} %get-tuple-element.38.refs_3_.doc_ref, bf16[128,1024]{1,0:T(8,128)(2,1)S(1)} %copy-done, bf16[128,1024]{1,0:T(8,128)(2,1)S(1)} %copy-done.1, bf16[128,512]{1,0:T(8,128)(2,1)S(1)} %copy-done.2, ...), custom_call_target="tpu_custom_call" | custom-call | flops 268435456 | bytes 1180176 | tf_op jit(solution)/shard_map/pallas_call | solution.py:299
  27.5 0.0 collective-permute-done.11.refs_2_
  27.5 0.3 %shard_map.140.refs_6_ = bf16[128,512]{1,0:T(8,128)(2,1)S(1)} custom-call(bf16[4,128,128]{2,1,0:T(8,128)(2,1)S(1)} %collective-permute-done.1.s_ref.refs_0_, bf16[4,128,128]{2,1,0:T(8,128)(2,1)S(1)} %collective-permute-done.3.s_ref.refs_1_, bf16[4,128,128]{2,1,0:T(8,128)(2,1)S(1)} %collective-permute-done.11.refs_2_, ...), custom_call_target="tpu_custom_call" | custom-call | flops 16777216 | bytes 1703936 | tf_op jit(solution)/shard_map/pallas_call | solution.py:299
  27.8 0.0 collective-permute-done.4.refs_2_
  27.8 1.0 %shard_map.141 = bf16[128,1024]{1,0:T(8,128)(2,1)} custom-call(bf16[4,128,128]{2,1,0:T(8,128)(2,1)S(1)} %collective-permute-done.s_ref.refs_0_, bf16[4,128,128]{2,1,0:T(8,128)(2,1)S(1)} %collective-permute-done.2.s_ref.refs_1_, bf16[4,128,128]{2,1,0:T(8,128)(2,1)S(1)} %collective-permute-done.4.refs_2_, f32[8,128,128]{2,1,0:T(8,128)S(1)} %get-tuple-element.61.refs_3_, ...), custom_call_target="tpu_custom_call" | custom-call | flops 16777216 | bytes 1835008 | tf_op jit(solution)/shard_map/pallas_call | solution.py:299
Async XLA Ops:
  2.5 5.8 %collective-permute-start.1 = (bf16[4,128,128]{2,1,0:T(8,128)(2,1)S(1)}, bf16[4,128,128]{2,1,0:T(8,128)(2,1)S(1)}, u32[]{:S(2)}, u32[]{:S(2)}) collective-permute-start(bf16[4,128,128]{2,1,0:T(8,128)(2,1)S(1)} %get-tuple-element.34), channel_id=1, source_target_pairs={{0,4},{1,5},{2,6},{3,7},{16,20},{17,21},{18,22},{19,23}} | collective-permute-start | bytes 393224 | tf_op jit(solution)/shard_map/ppermute | solution.py:374
  3.1 6.6 %collective-permute-start = (bf16[4,128,128]{2,1,0:T(8,128)(2,1)S(1)}, bf16[4,128,128]{2,1,0:T(8,128)(2,1)S(1)}, u32[]{:S(2)}, u32[]{:S(2)}) collective-permute-start(bf16[4,128,128]{2,1,0:T(8,128)(2,1)S(1)} %get-tuple-element.33), channel_id=1, source_target_pairs={{0,4},{1,5},{2,6},{3,7},{16,20},{17,21},{18,22},{19,23}} | collective-permute-start | bytes 393224 | tf_op jit(solution)/shard_map/ppermute | solution.py:374
  4.4 7.7 %collective-permute-start.5 = (bf16[256,128]{1,0:T(8,128)(2,1)S(1)}, bf16[256,128]{1,0:T(8,128)(2,1)S(1)}, u32[]{:S(2)}, u32[]{:S(2)}) collective-permute-start(bf16[256,128]{1,0:T(8,128)(2,1)S(1)} %get-tuple-element.56), channel_id=1, source_target_pairs={{0,4},{4,8},{8,12},{1,5},{5,9},{9,13},{2,6},{6,10},{10,14},{3,7},{... | collective-permute-start | bytes 196616 | tf_op jit(solution)/shard_map/ppermute | solution.py:404
  7.6 14.5 %collective-permute-start.9 = (bf16[256,128]{1,0:T(8,128)(2,1)S(1)}, bf16[256,128]{1,0:T(8,128)(2,1)S(1)}, u32[]{:S(2)}, u32[]{:S(2)}) collective-permute-start(bf16[256,128]{1,0:T(8,128)(2,1)S(1)} %get-tuple-element.56), channel_id=1, source_target_pairs={{0,12},{1,13},{2,14},{3,15},{16,28},{17,29},{18,30},{19,31}} | collective-permute-start | bytes 196616 | tf_op jit(solution)/shard_map/ppermute | solution.py:406
  8.5 8.9 %collective-permute-start.3 = (bf16[4,128,128]{2,1,0:T(8,128)(2,1)S(1)}, bf16[4,128,128]{2,1,0:T(8,128)(2,1)S(1)}, u32[]{:S(2)}, u32[]{:S(2)}) collective-permute-start(bf16[4,128,128]{2,1,0:T(8,128)(2,1)S(1)} %shard_map.133), channel_id=1, source_target_pairs={{4,8},{5,9},{6,10},{7,11},{20,24},{21,25},{22,26},{23,27}} | collective-permute-start | bytes 393224 | tf_op jit(solution)/shard_map/ppermute | solution.py:374
  10.0 10.6 %collective-permute-start.2 = (bf16[4,128,128]{2,1,0:T(8,128)(2,1)S(1)}, bf16[4,128,128]{2,1,0:T(8,128)(2,1)S(1)}, u32[]{:S(2)}, u32[]{:S(2)}) collective-permute-start(bf16[4,128,128]{2,1,0:T(8,128)(2,1)S(1)} %shard_map.134), channel_id=1, source_target_pairs={{4,8},{5,9},{6,10},{7,11},{20,24},{21,25},{22,26},{23,27}} | collective-permute-start | bytes 393224 | tf_op jit(solution)/shard_map/ppermute | solution.py:374
  12.1 11.9 %collective-permute-start.7 = (bf16[256,128]{1,0:T(8,128)(2,1)S(1)}, bf16[256,128]{1,0:T(8,128)(2,1)S(1)}, u32[]{:S(2)}, u32[]{:S(2)}) collective-permute-start(bf16[256,128]{1,0:T(8,128)(2,1)S(1)} %collective-permute-done.5.refs_0_), channel_id=1, source_target_pairs={{4,8},{8,12},{5,9},{9,13},{6,10},{10,14},{7,11},{11,15},{20,24},{2... | collective-permute-start | bytes 196616 | tf_op jit(solution)/shard_map/ppermute | solution.py:411
  17.3 1.5 %copy-start.4 = (bf16[128,1024]{1,0:T(8,128)(2,1)S(1)}, bf16[128,1024]{1,0:T(8,128)(2,1)}, u32[]{:S(2)}) copy-start(bf16[128,1024]{1,0:T(8,128)(2,1)} %z_ref.1) | copy-start | bytes 786436
  17.3 1.5 %copy-start.5 = (bf16[128,512]{1,0:T(8,128)(2,1)S(1)}, bf16[128,512]{1,0:T(8,128)(2,1)}, u32[]{:S(2)}) copy-start(bf16[128,512]{1,0:T(8,128)(2,1)} %q_ref.2) | copy-start | bytes 393220
  17.5 9.9 %collective-permute-start.11 = (bf16[4,128,128]{2,1,0:T(8,128)(2,1)S(1)}, bf16[4,128,128]{2,1,0:T(8,128)(2,1)S(1)}, u32[]{:S(2)}, u32[]{:S(2)}) collective-permute-start(bf16[4,128,128]{2,1,0:T(8,128)(2,1)S(1)} %shard_map.136), channel_id=1, source_target_pairs={{8,12},{9,13},{10,14},{11,15},{24,28},{25,29},{26,30},{27,31}} | collective-permute-start | bytes 393224 | tf_op jit(solution)/shard_map/ppermute | solution.py:374
  20.6 4.8 %copy-start = (bf16[128,1024]{1,0:T(8,128)(2,1)S(1)}, bf16[128,1024]{1,0:T(8,128)(2,1)}, u32[]{:S(2)}) copy-start(bf16[128,1024]{1,0:T(8,128)(2,1)} %q_ref.3) | copy-start | bytes 786436
  20.6 4.8 %copy-start.1 = (bf16[128,1024]{1,0:T(8,128)(2,1)S(1)}, bf16[128,1024]{1,0:T(8,128)(2,1)}, u32[]{:S(2)}) copy-start(bf16[128,1024]{1,0:T(8,128)(2,1)} %gate_ref.1) | copy-start | bytes 786436
  20.6 4.8 %copy-start.2 = (bf16[128,512]{1,0:T(8,128)(2,1)S(1)}, bf16[128,512]{1,0:T(8,128)(2,1)}, u32[]{:S(2)}) copy-start(bf16[128,512]{1,0:T(8,128)(2,1)} %k_ref.1) | copy-start | bytes 393220
  20.6 4.8 %copy-start.3 = (bf16[128,512]{1,0:T(8,128)(2,1)S(1)}, bf16[128,512]{1,0:T(8,128)(2,1)}, u32[]{:S(2)}) copy-start(bf16[128,512]{1,0:T(8,128)(2,1)} %v_ref.1) | copy-start | bytes 393220
  20.8 7.0 %collective-permute-start.4 = (bf16[4,128,128]{2,1,0:T(8,128)(2,1)S(1)}, bf16[4,128,128]{2,1,0:T(8,128)(2,1)S(1)}, u32[]{:S(2)}, u32[]{:S(2)}) collective-permute-start(bf16[4,128,128]{2,1,0:T(8,128)(2,1)S(1)} %shard_map.138), channel_id=1, source_target_pairs={{8,12},{9,13},{10,14},{11,15},{24,28},{25,29},{26,30},{27,31}} | collective-permute-start | bytes 393224 | tf_op jit(solution)/shard_map/ppermute | solution.py:374
  22.1 2.7 %collective-permute-start.10 = (bf16[256,128]{1,0:T(8,128)(2,1)S(1)}, bf16[256,128]{1,0:T(8,128)(2,1)S(1)}, u32[]{:S(2)}, u32[]{:S(2)}) collective-permute-start(bf16[256,128]{1,0:T(8,128)(2,1)S(1)} %collective-permute-done.9.refs_4_), channel_id=1, source_target_pairs={{0,1},{1,0},{2,3},{3,2},{4,5},{5,4},{6,7},{7,6},{8,9},{9,8},{10,11... | collective-permute-start | bytes 196616 | tf_op jit(solution)/shard_map/ppermute | solution.py:396
  24.0 1.3 %collective-permute-start.8 = (bf16[256,128]{1,0:T(8,128)(2,1)S(1)}, bf16[256,128]{1,0:T(8,128)(2,1)S(1)}, u32[]{:S(2)}, u32[]{:S(2)}) collective-permute-start(bf16[256,128]{1,0:T(8,128)(2,1)S(1)} %collective-permute-done.7.refs_2_), channel_id=1, source_target_pairs={{0,1},{1,0},{2,3},{3,2},{4,5},{5,4},{6,7},{7,6},{8,9},{9,8},{10,11... | collective-permute-start | bytes 196616 | tf_op jit(solution)/shard_map/ppermute | solution.py:396
  24.1 1.3 %collective-permute-start.6 = (bf16[256,128]{1,0:T(8,128)(2,1)S(1)}, bf16[256,128]{1,0:T(8,128)(2,1)S(1)}, u32[]{:S(2)}, u32[]{:S(2)}) collective-permute-start(bf16[256,128]{1,0:T(8,128)(2,1)S(1)} %collective-permute-done.5.refs_0_), channel_id=1, source_target_pairs={{0,1},{1,0},{2,3},{3,2},{4,5},{5,4},{6,7},{7,6},{8,9},{9,8},{10,11... | collective-permute-start | bytes 196616 | tf_op jit(solution)/shard_map/ppermute | solution.py:396

commit v4 on v3

--- a/solution.py
+++ b/solution.py
@@ -119,30 +119,30 @@
 
 
 def opening_kernel(scalar_ref, *refs):
-    sources, (ka_hbm, va_hbm) = refs[:6], refs[6:8]
-    inputs, (unit_ref, u_ref), send_refs, sems = refs[8:14], refs[14:16], refs[16:-1], refs[-1]
+    sources, u_ref, send_refs = refs[:5], refs[5], refs[6:-6]
+    inputs, sems = refs[-6:-1], refs[-1]
+
+    @pl.when(scalar_ref[0] == 0)
+    def _():
+        copies = [pltpu.make_async_copy(a, b, sems.at[i]) for i, (a, b) in enumerate(zip(sources, inputs))]
+        for copy in copies:
+            copy.start()
+        for copy in copies:
+            copy.wait()
+        state_terms(scalar_ref, inputs, u_ref, send_refs=send_refs)
+
+
+def second_kernel(scalar_ref, *refs):
+    inputs, (ka_ref, va_ref, gain_ref, _) = refs[:5], refs[5:9]
+    u_ref, w_ref, a_ref, m_ref, unit_ref, kept_ref = refs[9:]
+    kept_ref[...] = gain_ref[...]
+    length = u_ref.shape[1]
     groups = HD_A // DK
     rows = unit_ref.shape[0] // (2 * groups)
-    column = pl.multiple_of(scalar_ref[1], HD_A)
     begin = pl.multiple_of(scalar_ref[2], rows)
-    pairs = list(zip(sources, inputs))
     for at in range(2 * groups):
-        source = (ka_hbm, va_hbm)[at // groups].at[pl.ds(begin, rows), pl.ds(column + at % groups * DK, DK)]
-        pairs.append((source, unit_ref.at[pl.ds(at * rows, rows)]))
-    copies = [pltpu.make_async_copy(a, b, sems.at[i]) for i, (a, b) in enumerate(pairs)]
-    for copy in copies:
-        copy.start()
-    for copy in copies:
-        copy.wait()
-
-    @pl.when(scalar_ref[0] == 0)
-    def _():
-        state_terms(scalar_ref, inputs[:5], u_ref, send_refs=send_refs)
-
-
-def second_kernel(scalar_ref, *refs):
-    inputs, (_, u_ref, w_ref, a_ref, m_ref) = refs[:5], refs[5:]
-    length = u_ref.shape[1]
+        lanes = pl.ds(pl.multiple_of(scalar_ref[1] + at % groups * DK, DK), DK)
+        unit_ref[at * rows : (at + 1) * rows] = (ka_ref, va_ref)[at // groups][pl.ds(begin, rows), lanes]
 
     @pl.when(scalar_ref[0] == 0)
     def _():
@@ -355,20 +355,15 @@
     work = 100 * heads * length * DK * DV
     piece = heads // pieces
     groups = HD_A // DK
-    opened = call(
+    inputs, gain_in = sources[:5], sources[5]
+    fresh, *leaving = call(
         opening_kernel,
-        (
-            *[shape(a.shape, a.dtype) for a in sources],
-            shape((2 * groups * rows, DK), BF16),
-            terms[0],
-            *[shape((piece, DK, DV), BF16)] * pieces,
-        ),
-        (scalars, *sources, k_attn, v_attn),
+        (terms[0], *[shape((piece, DK, DV), BF16)] * pieces),
+        (scalars, *inputs),
         work,
-        outside=len(sources) + 2,
-        scratch=[pltpu.SemaphoreType.DMA((len(sources) + 2 * groups,))],
-    )
-    inputs, (gain_in, unit, fresh), leaving = opened[:5], opened[5:8], opened[8:]
+        outside=len(inputs),
+        scratch=[*[pltpu.VMEM(a.shape, a.dtype) for a in inputs], pltpu.SemaphoreType.DMA((len(inputs),))],
+    )
 
     def hand_on(hop, pieces_out):
         return [lax.ppermute(s, "seq", [(hop, hop + 1)]) for s in pieces_out]
@@ -397,10 +392,13 @@
 
     wanted = min(devices // 2 + 1, devices - 1)
     arrived = [hand_on(0, leaving)]
-    fresh, erased, added, carry = call(
-        second_kernel, terms, (scalars, *inputs, fresh), work, aliases={6: 0}
-    )
-    unit = after(unit, fresh)
+    fresh, erased, added, carry, unit, gain_in = call(
+        second_kernel,
+        (*terms, shape((2 * groups * rows, DK), BF16), shape(gain_in.shape, F32)),
+        (scalars, *inputs, k_attn, v_attn, gain_in, fresh),
+        work,
+        aliases={9: 0},
+    )
     units = [lax.ppermute(unit, "seq", [(i, i + 1) for i in range(devices - 1)])]
     direct = wanted == devices - 1 and wanted > 1
     farthest = [lax.ppermute(unit, "seq", [(0, wanted)])] if direct else []
@@ -435,8 +433,10 @@
         return mixing[:1]
 
     mixing = []
+    queries(fresh)
     for hop in range(2, devices - 1):
-        leaving = combined(arrived[-1], carry, added, queries if hop == 2 else None)
+        got = [after(arrived[-1][0], mixing[0]), *arrived[-1][1:]] if hop == 2 else arrived[-1]
+        leaving = combined(got, carry, added)
         arrived.append(hand_on(hop, leaving))
     local_out, reach, gain = mixing
 

time: 29.1 us -> 28.1 us (0.966)
  the two profiles are of different devices: /device:TPU:19 before, /device:TPU:26 now
where the time goes in v4:
time: 28.1 us; the launch traced here: 27.8 us
  Pallas kernels  10.2 us (36%)
  starting transfers between devices  9.85 us (35%)
  waiting for transfers between devices  6.07 us (22%)
  between operations  1.01 us (4%)
  local copies, waits for them, and re-layouts  0.65 us (2%)
    pallas_call x11, Pallas kernels, call(): pl.pallas_call(kernel, out_shape=out_shape, in_specs=specs, out_specs=jax...  10.2 us
    ppermute x6, starting transfers between devices, hand_on(): return [lax.ppermute(s, 'seq', [(hop, hop + 1)]) for s in pieces_out]  5.39 us
    ppermute x6, waiting for transfers between devices, hand_on(): return [lax.ppermute(s, 'seq', [(hop, hop + 1)]) for s in pieces_out]  3.42 us
    ppermute x1, waiting for transfers between devices, shards(): lax.ppermute(block, 'seq', [(i, i + 1) for i in range(distance - 1, devic...  1.74 us
    ppermute x1, starting transfers between devices, shards(): farthest = [lax.ppermute(unit, 'seq', [(0, wanted)])] if direct else []  1.29 us
    ppermute x1, starting transfers between devices, shards(): lax.ppermute(unit, 'seq', [(i, i + 1) for i in range(devices - 1)])  1.29 us
    ppermute x1, starting transfers between devices, shards(): lax.ppermute(block, 'seq', [(i, i + 1) for i in range(distance - 1, devic...  1.29 us
    ppermute x3, waiting for transfers between devices, swapped(): return lax.ppermute(got, 'head', pairs)  0.9 us
  transfers between devices with their start and end apart: 12, of which 5 were waited for; matrix products, arithmetic and copies ran while one was open for 0% of the time, Pallas kernels for 31%

profile of v4, /device:TPU:26, one launch (start us, length us, event | category | flops | bytes accessed | tf_op | source)
XLA Modules:
  0.0 27.8 jit_solution(15115536952663389659)
XLA Ops:
  0.7 0.1 pad_add_fusion.scalar_ref
  0.8 0.0 copy-start.10
  0.8 0.6 %shard_map.131 = (bf16[8,128,128]{2,1,0:T(8,128)(2,1)S(1)}, bf16[4,128,128]{2,1,0:T(8,128)(2,1)S(1)}, bf16[4,128,128]{2,1,0:T(8,128)(2,1)S(1)}) custom-call(s32[4]{0:T(128)S(1)} %pad_add_fusion.scalar_ref, bf16[128,512]{1,0:T(8,128)(2,1)} %k_ref.2, f32[8,128]{1,0:T(8,128)} %gate_ref.2, f32[8,128]{1,0:T(8,128)} %beta_ref.1, s32[1,128]{1,0:T(1,128)} %bitcast.6, ...), custom_call_target="tpu_custom_call" | custom-call | flops 1677721600 | bytes 401936 | tf_op jit(solution)/shard_map/pallas_call | solution.py:299
  1.4 0.0 copy-start.9
  1.4 0.7 %collective-permute-start.1 = (bf16[4,128,128]{2,1,0:T(8,128)(2,1)S(1)}, bf16[4,128,128]{2,1,0:T(8,128)(2,1)S(1)}, u32[]{:S(2)}, u32[]{:S(2)}) collective-permute-start(bf16[4,128,128]{2,1,0:T(8,128)(2,1)S(1)} %get-tuple-element.28), channel_id=1, source_target_pairs={{0,4},{1,5},{2,6},{3,7},{16,20},{17,21},{18,22},{19,23}} | collective-permute-start | bytes 393224 | tf_op jit(solution)/shard_map/ppermute | solution.py:369
  2.1 0.7 %collective-permute-start = (bf16[4,128,128]{2,1,0:T(8,128)(2,1)S(1)}, bf16[4,128,128]{2,1,0:T(8,128)(2,1)S(1)}, u32[]{:S(2)}, u32[]{:S(2)}) collective-permute-start(bf16[4,128,128]{2,1,0:T(8,128)(2,1)S(1)} %get-tuple-element.27), channel_id=1, source_target_pairs={{0,4},{1,5},{2,6},{3,7},{16,20},{17,21},{18,22},{19,23}} | collective-permute-start | bytes 393224 | tf_op jit(solution)/shard_map/ppermute | solution.py:369
  2.7 0.0 copy-start.4
  2.8 0.0 copy-start.11
  2.8 0.6 %copy-done.4 = s32[128]{0:T(128)S(1)} copy-done((s32[128]{0:T(128)S(1)}, s32[128]{0:T(128)}, u32[]{:S(2)}) %copy-start.4) | copy-done | bytes 536
  3.4 0.0 copy-done.11
  3.4 0.6 %shard_map.132 = (bf16[8,128,128]{2,1,0:T(8,128)(2,1)S(1)}, bf16[8,128,128]{2,1,0:T(8,128)(2,1)S(1)}, f32[8,128,128]{2,1,0:T(8,128)S(1)}, bf16[8,128,128]{2,1,0:...) custom-call(s32[4]{0:T(128)S(1)} %pad_add_fusion.scalar_ref, ...), custom_call_target="tpu_custom_call", output_to_operand_aliasing={{0}: (9, {})} | custom-call | flops 1677721600 | bytes 926736 | tf_op jit(solution)/shard_map/pallas_call | solution.py:299
  4.0 1.3 %collective-permute-start.9 = (bf16[256,128]{1,0:T(8,128)(2,1)S(1)}, bf16[256,128]{1,0:T(8,128)(2,1)S(1)}, u32[]{:S(2)}, u32[]{:S(2)}) collective-permute-start(bf16[256,128]{1,0:T(8,128)(2,1)S(1)} %get-tuple-element.44), channel_id=1, source_target_pairs={{0,12},{1,13},{2,14},{3,15},{16,28},{17,29},{18,30},{19,31}} | collective-permute-start | bytes 196616 | tf_op jit(solution)/shard_map/ppermute | solution.py:404
  5.3 1.3 %collective-permute-start.5 = (bf16[256,128]{1,0:T(8,128)(2,1)S(1)}, bf16[256,128]{1,0:T(8,128)(2,1)S(1)}, u32[]{:S(2)}, u32[]{:S(2)}) collective-permute-start(bf16[256,128]{1,0:T(8,128)(2,1)S(1)} %get-tuple-element.44), channel_id=1, source_target_pairs={{0,4},{4,8},{8,12},{1,5},{5,9},{9,13},{2,6},{6,10},{10,14},{3,7},{... | collective-permute-start | bytes 196616 | tf_op jit(solution)/shard_map/ppermute | solution.py:402
  6.6 0.0 collective-permute-done.1.s_ref.refs_0_
  6.6 0.2 shard_map.133
  6.8 0.7 %collective-permute-start.3 = (bf16[4,128,128]{2,1,0:T(8,128)(2,1)S(1)}, bf16[4,128,128]{2,1,0:T(8,128)(2,1)S(1)}, u32[]{:S(2)}, u32[]{:S(2)}) collective-permute-start(bf16[4,128,128]{2,1,0:T(8,128)(2,1)S(1)} %shard_map.133), channel_id=1, source_target_pairs={{4,8},{5,9},{6,10},{7,11},{20,24},{21,25},{22,26},{23,27}} | collective-permute-start | bytes 393224 | tf_op jit(solution)/shard_map/ppermute | solution.py:369
  7.5 0.0 collective-permute-done.s_ref.refs_0_
  7.5 0.2 shard_map.134
  7.7 0.7 %collective-permute-start.2 = (bf16[4,128,128]{2,1,0:T(8,128)(2,1)S(1)}, bf16[4,128,128]{2,1,0:T(8,128)(2,1)S(1)}, u32[]{:S(2)}, u32[]{:S(2)}) collective-permute-start(bf16[4,128,128]{2,1,0:T(8,128)(2,1)S(1)} %shard_map.134), channel_id=1, source_target_pairs={{4,8},{5,9},{6,10},{7,11},{20,24},{21,25},{22,26},{23,27}} | collective-permute-start | bytes 393224 | tf_op jit(solution)/shard_map/ppermute | solution.py:369
  8.3 0.0 copy-start.6
  8.3 0.0 copy-start.8
  8.4 3.2 %shard_map.135 = (bf16[8,128,128]{2,1,0:T(8,128)(2,1)S(1)}, bf16[8,128,128]{2,1,0:T(8,128)(2,1)S(1)}, f32[8,128,128]{2,1,0:T(8,128)S(1)}, bf16[8,128,128]{2,1,0:T(8,128)(2,1)S(1)}) custom-call(s32[4]{0:T(128)S(1)} %pad_add_fusion.scalar_ref, bf16[128,512]{1,0:T(8,128)(2,1)S(1)} %copy-done.7, ...), custom_call_target="tpu_custom_call", output_to_operand_aliasing={{0}: (6, {}), {1}: (7, {}), {2}: (8, {}), {3}: (9, {})} | custom-call | flops 1677721600 | bytes 1712656 | tf_op jit(solution)/shard_map/pallas_call | solution.py:299
  11.6 0.0 collective-permute-done.5.refs_0_
  11.6 1.3 %collective-permute-start.7 = (bf16[256,128]{1,0:T(8,128)(2,1)S(1)}, bf16[256,128]{1,0:T(8,128)(2,1)S(1)}, u32[]{:S(2)}, u32[]{:S(2)}) collective-permute-start(bf16[256,128]{1,0:T(8,128)(2,1)S(1)} %collective-permute-done.5.refs_0_), channel_id=1, source_target_pairs={{4,8},{8,12},{5,9},{9,13},{6,10},{10,14},{7,11},{11,15},{20,24},{2... | collective-permute-start | bytes 196616 | tf_op jit(solution)/shard_map/ppermute | solution.py:409
  12.9 0.0 copy-done.6
  12.9 0.0 copy-done.8
  12.9 1.7 %shard_map.136 = (f32[8,128,128]{2,1,0:T(8,128)S(1)}, bf16[8,128,128]{2,1,0:T(8,128)(2,1)S(1)}, f32[8,128,128]{2,1,0:T(8,128)S(1)}) custom-call(s32[4]{0:T(128)S(1)} %pad_add_fusion.scalar_ref, s32[1,128]{1,0:T(1,128)S(1)} %bitcast.9, f32[8,128]{1,0:T(8,128)S(1)} %copy-done.10, f32[8,128]{1,0:T(8,128)S(1)} %copy-done.9, bf16[128,512]{1,0:T(8,128)(2,1)S(1)} %copy-done.8, ...), custom_call_target="tpu_custom_call" | custom-call | flops 1677721600 | bytes 1057808 | tf_op jit(solution)/shard_map/pallas_call | solution.py:299
  14.7 0.0 collective-permute-done.3.s_ref.refs_1_
  14.7 0.2 shard_map.137
  14.9 0.0 copy-start
  14.9 0.0 copy-start.1
  14.9 1.4 %collective-permute-start.11 = (bf16[4,128,128]{2,1,0:T(8,128)(2,1)S(1)}, bf16[4,128,128]{2,1,0:T(8,128)(2,1)S(1)}, u32[]{:S(2)}, u32[]{:S(2)}) collective-permute-start(bf16[4,128,128]{2,1,0:T(8,128)(2,1)S(1)} %shard_map.137), channel_id=1, source_target_pairs={{8,12},{9,13},{10,14},{11,15},{24,28},{25,29},{26,30},{27,31}} | collective-permute-start | bytes 393224 | tf_op jit(solution)/shard_map/ppermute | solution.py:369
  16.3 0.0 collective-permute-done.2.s_ref.refs_1_
  16.3 0.2 shard_map.138
  16.5 1.3 %collective-permute-start.4 = (bf16[4,128,128]{2,1,0:T(8,128)(2,1)S(1)}, bf16[4,128,128]{2,1,0:T(8,128)(2,1)S(1)}, u32[]{:S(2)}, u32[]{:S(2)}) collective-permute-start(bf16[4,128,128]{2,1,0:T(8,128)(2,1)S(1)} %shard_map.138), channel_id=1, source_target_pairs={{8,12},{9,13},{10,14},{11,15},{24,28},{25,29},{26,30},{27,31}} | collective-permute-start | bytes 393224 | tf_op jit(solution)/shard_map/ppermute | solution.py:369
  17.8 0.0 collective-permute-done.9.refs_4_
  17.8 0.1 collective-permute-start.10
  17.9 1.7 %collective-permute-done.7.refs_2_ = bf16[256,128]{1,0:T(8,128)(2,1)S(1)} collective-permute-done((bf16[256,128]{1,0:T(8,128)(2,1)S(1)}, bf16[256,128]{1,0:T(8,128)(2,1)S(1)}, u32[]{:S(2)}, u32[]{:S(2)}) %collective-permute-start.7) | collective-permute-done | bytes 65568 | tf_op jit(solution)/shard_map/ppermute | solution.py:409
  19.7 0.0 collective-permute-start.8
  19.7 0.5 %collective-permute-start.6 = (bf16[256,128]{1,0:T(8,128)(2,1)S(1)}, bf16[256,128]{1,0:T(8,128)(2,1)S(1)}, u32[]{:S(2)}, u32[]{:S(2)}) collective-permute-start(bf16[256,128]{1,0:T(8,128)(2,1)S(1)} %collective-permute-done.5.refs_0_), channel_id=1, source_target_pairs={{0,1},{1,0},{2,3},{3,2},{4,5},{5,4},{6,7},{7,6},{8,9},{9,8},{10,11... | collective-permute-start | bytes 196616 | tf_op jit(solution)/shard_map/ppermute | solution.py:391
  20.2 0.0 collective-permute-done.10.refs_5_
  20.2 0.7 %collective-permute-done.8.refs_3_ = bf16[256,128]{1,0:T(8,128)(2,1)S(1)} collective-permute-done((bf16[256,128]{1,0:T(8,128)(2,1)S(1)}, bf16[256,128]{1,0:T(8,128)(2,1)S(1)}, u32[]{:S(2)}, u32[]{:S(2)}) %collective-permute-start.8) | collective-permute-done | bytes 65568 | tf_op jit(solution)/shard_map/ppermute | solution.py:391
  20.9 0.2 collective-permute-done.6.refs_1_
  21.1 2.0 %shard_map.139 = bf16[128,1024]{1,0:T(8,128)(2,1)} custom-call(s32[4]{0:T(128)S(1)} %pad_add_fusion.scalar_ref, s32[1,128]{1,0:T(1,128)S(1)} %bitcast.10, bf16[128,1024]{1,0:T(8,128)(2,1)S(1)} %copy-done, bf16[128,1024]{1,0:T(8,128)(2,1)S(1)} %copy-done.1, bf16[128,512]{1,0:T(8,128)(2,1)S(1)} %copy-done.2, bf16[128,512]{1,0:T(8,128)(2,1)S(1)} %copy-done.3, ...), custom_call_target="tpu_custom_call" | custom-call | flops 268435456 | bytes 1180176 | tf_op jit(solution)/shard_map/pallas_call | solution.py:299
  23.1 2.1 %collective-permute-done.11.refs_2_ = bf16[4,128,128]{2,1,0:T(8,128)(2,1)S(1)} collective-permute-done((bf16[4,128,128]{2,1,0:T(8,128)(2,1)S(1)}, bf16[4,128,128]{2,1,0:T(8,128)(2,1)S(1)}, u32[]{:S(2)}, u32[]{:S(2)}) %collective-permute-start.11) | collective-permute-done | bytes 131104 | tf_op jit(solution)/shard_map/ppermute | solution.py:369
  25.2 0.3 %shard_map.140.refs_6_ = bf16[128,512]{1,0:T(8,128)(2,1)S(1)} custom-call(bf16[4,128,128]{2,1,0:T(8,128)(2,1)S(1)} %collective-permute-done.1.s_ref.refs_0_, bf16[4,128,128]{2,1,0:T(8,128)(2,1)S(1)} %collective-permute-done.3.s_ref.refs_1_, bf16[4,128,128]{2,1,0:T(8,128)(2,1)S(1)} %collective-permute-done.11.refs_2_, ...), custom_call_target="tpu_custom_call" | custom-call | flops 16777216 | bytes 1703936 | tf_op jit(solution)/shard_map/pallas_call | solution.py:299
  25.5 1.3 %collective-permute-done.4.refs_2_ = bf16[4,128,128]{2,1,0:T(8,128)(2,1)S(1)} collective-permute-done((bf16[4,128,128]{2,1,0:T(8,128)(2,1)S(1)}, bf16[4,128,128]{2,1,0:T(8,128)(2,1)S(1)}, u32[]{:S(2)}, u32[]{:S(2)}) %collective-permute-start.4) | collective-permute-done | bytes 131104 | tf_op jit(solution)/shard_map/ppermute | solution.py:369
  26.8 1.0 %shard_map.141 = bf16[128,1024]{1,0:T(8,128)(2,1)} custom-call(bf16[4,128,128]{2,1,0:T(8,128)(2,1)S(1)} %collective-permute-done.s_ref.refs_0_, bf16[4,128,128]{2,1,0:T(8,128)(2,1)S(1)} %collective-permute-done.2.s_ref.refs_1_, bf16[4,128,128]{2,1,0:T(8,128)(2,1)S(1)} %collective-permute-done.4.refs_2_, f32[8,128,128]{2,1,0:T(8,128)S(1)} %get-tuple-element.49.refs_3_, ...), custom_call_target="tpu_custom_call" | custom-call | flops 16777216 | bytes 1835008 | tf_op jit(solution)/shard_map/pallas_call | solution.py:299
  (12 shorter events, 0.0 us)
Async XLA Ops:
  0.7 2.0 %copy-start.2 = (bf16[128,512]{1,0:T(8,128)(2,1)S(1)}, bf16[128,512]{1,0:T(8,128)(2,1)}, u32[]{:S(2)}) copy-start(bf16[128,512]{1,0:T(8,128)(2,1)} %k_ref.3) | copy-start | bytes 393220
  0.7 2.0 %copy-start.3 = (bf16[128,512]{1,0:T(8,128)(2,1)S(1)}, bf16[128,512]{1,0:T(8,128)(2,1)}, u32[]{:S(2)}) copy-start(bf16[128,512]{1,0:T(8,128)(2,1)} %v_ref.1) | copy-start | bytes 393220
  0.7 2.0 %copy-start.5 = (bf16[128,1024]{1,0:T(8,128)(2,1)S(1)}, bf16[128,1024]{1,0:T(8,128)(2,1)}, u32[]{:S(2)}) copy-start(bf16[128,1024]{1,0:T(8,128)(2,1)} %refs_4_.5) | copy-start | bytes 786436
  0.7 2.0 %copy-start.7 = (bf16[128,512]{1,0:T(8,128)(2,1)S(1)}, bf16[128,512]{1,0:T(8,128)(2,1)}, u32[]{:S(2)}) copy-start(bf16[128,512]{1,0:T(8,128)(2,1)} %k_ref.2) | copy-start | bytes 393220
  0.8 2.0 %copy-start.10 = (f32[8,128]{1,0:T(8,128)S(1)}, f32[8,128]{1,0:T(8,128)}, u32[]{:S(2)}) copy-start(f32[8,128]{1,0:T(8,128)} %beta_ref.1) | copy-start | bytes 12292
  1.4 1.4 %copy-start.9 = (f32[8,128]{1,0:T(8,128)S(1)}, f32[8,128]{1,0:T(8,128)}, u32[]{:S(2)}) copy-start(f32[8,128]{1,0:T(8,128)} %gate_ref.2) | copy-start | bytes 12292
  1.4 5.2 %collective-permute-start.1 = (bf16[4,128,128]{2,1,0:T(8,128)(2,1)S(1)}, bf16[4,128,128]{2,1,0:T(8,128)(2,1)S(1)}, u32[]{:S(2)}, u32[]{:S(2)}) collective-permute-start(bf16[4,128,128]{2,1,0:T(8,128)(2,1)S(1)} %get-tuple-element.28), channel_id=1, source_target_pairs={{0,4},{1,5},{2,6},{3,7},{16,20},{17,21},{18,22},{19,23}} | collective-permute-start | bytes 393224 | tf_op jit(solution)/shard_map/ppermute | solution.py:369
  2.1 5.4 %collective-permute-start = (bf16[4,128,128]{2,1,0:T(8,128)(2,1)S(1)}, bf16[4,128,128]{2,1,0:T(8,128)(2,1)S(1)}, u32[]{:S(2)}, u32[]{:S(2)}) collective-permute-start(bf16[4,128,128]{2,1,0:T(8,128)(2,1)S(1)} %get-tuple-element.27), channel_id=1, source_target_pairs={{0,4},{1,5},{2,6},{3,7},{16,20},{17,21},{18,22},{19,23}} | collective-permute-start | bytes 393224 | tf_op jit(solution)/shard_map/ppermute | solution.py:369
  2.7 0.7 %copy-start.4 = (s32[128]{0:T(128)S(1)}, s32[128]{0:T(128)}, u32[]{:S(2)}) copy-start(s32[128]{0:T(128)} %param.12) | copy-start | bytes 1540
  2.8 0.7 %copy-start.11 = (f32[128]{0:T(128)S(1)}, f32[128]{0:T(128)}, u32[]{:S(2)}) copy-start(f32[128]{0:T(128)} %param.19) | copy-start | bytes 1540
  4.0 13.8 %collective-permute-start.9 = (bf16[256,128]{1,0:T(8,128)(2,1)S(1)}, bf16[256,128]{1,0:T(8,128)(2,1)S(1)}, u32[]{:S(2)}, u32[]{:S(2)}) collective-permute-start(bf16[256,128]{1,0:T(8,128)(2,1)S(1)} %get-tuple-element.44), channel_id=1, source_target_pairs={{0,12},{1,13},{2,14},{3,15},{16,28},{17,29},{18,30},{19,31}} | collective-permute-start | bytes 196616 | tf_op jit(solution)/shard_map/ppermute | solution.py:404
  5.3 6.3 %collective-permute-start.5 = (bf16[256,128]{1,0:T(8,128)(2,1)S(1)}, bf16[256,128]{1,0:T(8,128)(2,1)S(1)}, u32[]{:S(2)}, u32[]{:S(2)}) collective-permute-start(bf16[256,128]{1,0:T(8,128)(2,1)S(1)} %get-tuple-element.44), channel_id=1, source_target_pairs={{0,4},{4,8},{8,12},{1,5},{5,9},{9,13},{2,6},{6,10},{10,14},{3,7},{... | collective-permute-start | bytes 196616 | tf_op jit(solution)/shard_map/ppermute | solution.py:402
  6.8 7.9 %collective-permute-start.3 = (bf16[4,128,128]{2,1,0:T(8,128)(2,1)S(1)}, bf16[4,128,128]{2,1,0:T(8,128)(2,1)S(1)}, u32[]{:S(2)}, u32[]{:S(2)}) collective-permute-start(bf16[4,128,128]{2,1,0:T(8,128)(2,1)S(1)} %shard_map.133), channel_id=1, source_target_pairs={{4,8},{5,9},{6,10},{7,11},{20,24},{21,25},{22,26},{23,27}} | collective-permute-start | bytes 393224 | tf_op jit(solution)/shard_map/ppermute | solution.py:369
  7.7 8.7 %collective-permute-start.2 = (bf16[4,128,128]{2,1,0:T(8,128)(2,1)S(1)}, bf16[4,128,128]{2,1,0:T(8,128)(2,1)S(1)}, u32[]{:S(2)}, u32[]{:S(2)}) collective-permute-start(bf16[4,128,128]{2,1,0:T(8,128)(2,1)S(1)} %shard_map.134), channel_id=1, source_target_pairs={{4,8},{5,9},{6,10},{7,11},{20,24},{21,25},{22,26},{23,27}} | collective-permute-start | bytes 393224 | tf_op jit(solution)/shard_map/ppermute | solution.py:369
  8.3 4.6 %copy-start.6 = (bf16[128,1024]{1,0:T(8,128)(2,1)S(1)}, bf16[128,1024]{1,0:T(8,128)(2,1)}, u32[]{:S(2)}) copy-start(bf16[128,1024]{1,0:T(8,128)(2,1)} %z_ref.1) | copy-start | bytes 786436
  8.3 4.6 %copy-start.8 = (bf16[128,512]{1,0:T(8,128)(2,1)S(1)}, bf16[128,512]{1,0:T(8,128)(2,1)}, u32[]{:S(2)}) copy-start(bf16[128,512]{1,0:T(8,128)(2,1)} %q_ref.2) | copy-start | bytes 393220
  11.6 8.0 %collective-permute-start.7 = (bf16[256,128]{1,0:T(8,128)(2,1)S(1)}, bf16[256,128]{1,0:T(8,128)(2,1)S(1)}, u32[]{:S(2)}, u32[]{:S(2)}) collective-permute-start(bf16[256,128]{1,0:T(8,128)(2,1)S(1)} %collective-permute-done.5.refs_0_), channel_id=1, source_target_pairs={{4,8},{8,12},{5,9},{9,13},{6,10},{10,14},{7,11},{11,15},{20,24},{2... | collective-permute-start | bytes 196616 | tf_op jit(solution)/shard_map/ppermute | solution.py:409
  14.9 6.2 %copy-start = (bf16[128,1024]{1,0:T(8,128)(2,1)S(1)}, bf16[128,1024]{1,0:T(8,128)(2,1)}, u32[]{:S(2)}) copy-start(bf16[128,1024]{1,0:T(8,128)(2,1)} %q_ref.3) | copy-start | bytes 786436
  14.9 6.2 %copy-start.1 = (bf16[128,1024]{1,0:T(8,128)(2,1)S(1)}, bf16[128,1024]{1,0:T(8,128)(2,1)}, u32[]{:S(2)}) copy-start(bf16[128,1024]{1,0:T(8,128)(2,1)} %gate_ref.3) | copy-start | bytes 786436
  14.9 10.3 %collective-permute-start.11 = (bf16[4,128,128]{2,1,0:T(8,128)(2,1)S(1)}, bf16[4,128,128]{2,1,0:T(8,128)(2,1)S(1)}, u32[]{:S(2)}, u32[]{:S(2)}) collective-permute-start(bf16[4,128,128]{2,1,0:T(8,128)(2,1)S(1)} %shard_map.137), channel_id=1, source_target_pairs={{8,12},{9,13},{10,14},{11,15},{24,28},{25,29},{26,30},{27,31}} | collective-permute-start | bytes 393224 | tf_op jit(solution)/shard_map/ppermute | solution.py:369
  16.5 10.3 %collective-permute-start.4 = (bf16[4,128,128]{2,1,0:T(8,128)(2,1)S(1)}, bf16[4,128,128]{2,1,0:T(8,128)(2,1)S(1)}, u32[]{:S(2)}, u32[]{:S(2)}) collective-permute-start(bf16[4,128,128]{2,1,0:T(8,128)(2,1)S(1)} %shard_map.138), channel_id=1, source_target_pairs={{8,12},{9,13},{10,14},{11,15},{24,28},{25,29},{26,30},{27,31}} | collective-permute-start | bytes 393224 | tf_op jit(solution)/shard_map/ppermute | solution.py:369
  17.8 2.3 %collective-permute-start.10 = (bf16[256,128]{1,0:T(8,128)(2,1)S(1)}, bf16[256,128]{1,0:T(8,128)(2,1)S(1)}, u32[]{:S(2)}, u32[]{:S(2)}) collective-permute-start(bf16[256,128]{1,0:T(8,128)(2,1)S(1)} %collective-permute-done.9.refs_4_), channel_id=1, source_target_pairs={{0,1},{1,0},{2,3},{3,2},{4,5},{5,4},{6,7},{7,6},{8,9},{9,8},{10,11... | collective-permute-start | bytes 196616 | tf_op jit(solution)/shard_map/ppermute | solution.py:391
  19.7 1.3 %collective-permute-start.8 = (bf16[256,128]{1,0:T(8,128)(2,1)S(1)}, bf16[256,128]{1,0:T(8,128)(2,1)S(1)}, u32[]{:S(2)}, u32[]{:S(2)}) collective-permute-start(bf16[256,128]{1,0:T(8,128)(2,1)S(1)} %collective-permute-done.7.refs_2_), channel_id=1, source_target_pairs={{0,1},{1,0},{2,3},{3,2},{4,5},{5,4},{6,7},{7,6},{8,9},{9,8},{10,11... | collective-permute-start | bytes 196616 | tf_op jit(solution)/shard_map/ppermute | solution.py:391
  19.7 1.4 %collective-permute-start.6 = (bf16[256,128]{1,0:T(8,128)(2,1)S(1)}, bf16[256,128]{1,0:T(8,128)(2,1)S(1)}, u32[]{:S(2)}, u32[]{:S(2)}) collective-permute-start(bf16[256,128]{1,0:T(8,128)(2,1)S(1)} %collective-permute-done.5.refs_0_), channel_id=1, source_target_pairs={{0,1},{1,0},{2,3},{3,2},{4,5},{5,4},{6,7},{7,6},{8,9},{9,8},{10,11... | collective-permute-start | bytes 196616 | tf_op jit(solution)/shard_map/ppermute | solution.py:391

commit v5 on v4

--- a/solution.py
+++ b/solution.py
@@ -54,6 +54,10 @@
     row = lax.broadcasted_iota(jnp.int32, (length, length), 0)
     col = lax.broadcasted_iota(jnp.int32, (length, length), 1)
     return row, col
+
+
+def upper_rows(square, size):
+    return jnp.concatenate([square[i : i + size] for i in range(size, square.shape[0], 2 * size)], axis=0)
 
 
 def state_terms(scalar_ref, inputs, u_ref, w_ref=None, a_ref=None, m_ref=None, send_refs=()):
@@ -87,15 +91,47 @@
         weight = beta[h : h + 1, :] * inv[h // repeat]
         systems.append(decay * grams[h // repeat] * weight)
     differ = row ^ col
-    inverse = [jnp.where(row == col, 1.0, 0.0) - jnp.where(differ == 1, n, 0.0) for n in systems]
-    level = 1
+    diagonal = differ < 8
+    strip_row = lax.broadcasted_iota(jnp.int32, (8, length), 0)
+    strip_col = lax.broadcasted_iota(jnp.int32, (8, length), 1)
+    lead = strip_col // 8 * 8
+    unit = jnp.where(strip_row == strip_col - lead, 1.0, 0.0)
+    strips = []
+    for n in systems:
+        kept = jnp.where(diagonal, n, 0.0)
+        parts = [kept[at : at + 8] for at in range(0, length, 8)]
+        while len(parts) > 1:
+            parts = [x + y for x, y in zip(parts[::2], parts[1::2])]
+        strips.append(parts[0])
+    solved = [unit] * heads
+    for step in range(7):
+        picked = [jnp.take_along_axis(n, lead + step, axis=1) for n in strips]
+        solved = [x - p * x[step : step + 1] for x, p in zip(solved, picked)]
+    inverse = [jnp.where(diagonal, jnp.concatenate([x] * (length // 8), axis=0), 0.0) for x in solved]
+    level = 3
     while (1 << level) < length:
-        mask = (differ >> level) == 1
-        short = [x.astype(BF16) for x in inverse]
+        size = 1 << level
+        starts = range(size, length, 2 * size)
+        mask = (upper_rows(differ, size) >> level) == 1
+        kept = [jnp.where(mask, upper_rows(n, size), 0.0).astype(BF16) for n in systems]
+        inner = [dot(n, x.astype(BF16)) for n, x in zip(kept, inverse)]
+        spare = jnp.zeros((size, length), F32)
         inner = [
-            dot(jnp.where(mask, n, 0.0).astype(BF16), x).astype(BF16) for n, x in zip(systems, short)
+            jnp.concatenate([p for i in range(len(starts)) for p in (spare, y[i * size : (i + 1) * size])], axis=0)
+            for y in inner
         ]
-        inverse = [x - dot(s, y) for x, s, y in zip(inverse, short, inner)]
+        outer = [dot(upper_rows(x, size).astype(BF16), y.astype(BF16)) for x, y in zip(inverse, inner)]
+        inverse = [
+            jnp.concatenate(
+                [
+                    p
+                    for j, i in enumerate(starts)
+                    for p in (x[i - size : i], x[i : i + size] - o[j * size : (j + 1) * size])
+                ],
+                axis=0,
+            )
+            for x, o in zip(inverse, outer)
+        ]
         level += 1
     keys_t = [k.astype(F32).T for k in keys]
     for h in range(heads):
@@ -428,7 +464,7 @@
                 *(scalars, inputs[3], inputs[2], inputs[1], q_gdn, inputs[0], z_gdn, gain_in),
                 *(after(fresh, first), erased),
             ),
-            work,
+            3 * work,
         ))
         return mixing[:1]
 

time: 28.1 us -> 27.7 us (0.986)
  Pallas kernels: 10.2 us -> 9.72 us
    pallas_call x11, Pallas kernels: 10.2 us -> 9.72 us  [call(): pl.pallas_call(kernel, out_shape=out_shape, in_specs=specs, out_specs=jax...]
    ppermute x1, waiting for transfers between devices: 0.01 us -> 0.29 us  [shards(): lax.ppermute(unit, 'seq', [(i, i + 1) for i in range(devices - 1)])]
  transfers between devices with their start and end apart: 12 -> 12, of which waited for: 5 -> 6; matrix products, arithmetic and copies ran while one was open for 0% -> 0% of each run, Pallas kernels for 31% -> 30%
where the time goes in v5:
time: 27.7 us; the launch traced here: 27.4 us
  starting transfers between devices  9.84 us (36%)
  Pallas kernels  9.72 us (35%)
  waiting for transfers between devices  6.08 us (22%)
  between operations  1 us (4%)
  local copies, waits for them, and re-layouts  0.65 us (2%)
    pallas_call x11, Pallas kernels, call(): pl.pallas_call(kernel, out_shape=out_shape, in_specs=specs, out_specs=jax...  9.72 us
    ppermute x6, starting transfers between devices, hand_on(): return [lax.ppermute(s, 'seq', [(hop, hop + 1)]) for s in pieces_out]  5.39 us
    ppermute x6, waiting for transfers between devices, hand_on(): return [lax.ppermute(s, 'seq', [(hop, hop + 1)]) for s in pieces_out]  3.42 us
    ppermute x1, waiting for transfers between devices, shards(): lax.ppermute(block, 'seq', [(i, i + 1) for i in range(distance - 1, devic...  1.47 us
    ppermute x1, starting transfers between devices, shards(): farthest = [lax.ppermute(unit, 'seq', [(0, wanted)])] if direct else []  1.29 us
    ppermute x1, starting transfers between devices, shards(): lax.ppermute(unit, 'seq', [(i, i + 1) for i in range(devices - 1)])  1.29 us
    ppermute x1, starting transfers between devices, shards(): lax.ppermute(block, 'seq', [(i, i + 1) for i in range(distance - 1, devic...  1.28 us
    ppermute x3, waiting for transfers between devices, swapped(): return lax.ppermute(got, 'head', pairs)  0.9 us
  transfers between devices with their start and end apart: 12, of which 6 were waited for; matrix products, arithmetic and copies ran while one was open for 0% of the time, Pallas kernels for 30%

profile of v5, /device:TPU:26, one launch (start us, length us, event | category | flops | bytes accessed | tf_op | source)
XLA Modules:
  0.0 27.4 jit_solution(821081917357243854)
XLA Ops:
  0.7 0.1 pad_add_fusion.scalar_ref
  0.8 0.0 copy-start.10
  0.8 0.6 %shard_map.131 = (bf16[8,128,128]{2,1,0:T(8,128)(2,1)S(1)}, bf16[4,128,128]{2,1,0:T(8,128)(2,1)S(1)}, bf16[4,128,128]{2,1,0:T(8,128)(2,1)S(1)}) custom-call(s32[4]{0:T(128)S(1)} %pad_add_fusion.scalar_ref, bf16[128,512]{1,0:T(8,128)(2,1)} %k_ref.2, f32[8,128]{1,0:T(8,128)} %gate_ref.2, f32[8,128]{1,0:T(8,128)} %beta_ref.1, s32[1,128]{1,0:T(1,128)} %bitcast.6, ...), custom_call_target="tpu_custom_call" | custom-call | flops 1677721600 | bytes 401936 | tf_op jit(solution)/shard_map/pallas_call | solution.py:335
  1.4 0.0 copy-start.9
  1.4 0.7 %collective-permute-start.1 = (bf16[4,128,128]{2,1,0:T(8,128)(2,1)S(1)}, bf16[4,128,128]{2,1,0:T(8,128)(2,1)S(1)}, u32[]{:S(2)}, u32[]{:S(2)}) collective-permute-start(bf16[4,128,128]{2,1,0:T(8,128)(2,1)S(1)} %get-tuple-element.28), channel_id=1, source_target_pairs={{0,4},{1,5},{2,6},{3,7},{16,20},{17,21},{18,22},{19,23}} | collective-permute-start | bytes 393224 | tf_op jit(solution)/shard_map/ppermute | solution.py:405
  2.1 0.7 %collective-permute-start = (bf16[4,128,128]{2,1,0:T(8,128)(2,1)S(1)}, bf16[4,128,128]{2,1,0:T(8,128)(2,1)S(1)}, u32[]{:S(2)}, u32[]{:S(2)}) collective-permute-start(bf16[4,128,128]{2,1,0:T(8,128)(2,1)S(1)} %get-tuple-element.27), channel_id=1, source_target_pairs={{0,4},{1,5},{2,6},{3,7},{16,20},{17,21},{18,22},{19,23}} | collective-permute-start | bytes 393224 | tf_op jit(solution)/shard_map/ppermute | solution.py:405
  2.7 0.0 copy-start.4
  2.8 0.0 copy-start.11
  2.8 0.0 copy-done.2
  2.8 0.6 %copy-done.4 = s32[128]{0:T(128)S(1)} copy-done((s32[128]{0:T(128)S(1)}, s32[128]{0:T(128)}, u32[]{:S(2)}) %copy-start.4) | copy-done | bytes 536
  3.4 0.0 copy-done.11
  3.4 0.6 %shard_map.132 = (bf16[8,128,128]{2,1,0:T(8,128)(2,1)S(1)}, bf16[8,128,128]{2,1,0:T(8,128)(2,1)S(1)}, f32[8,128,128]{2,1,0:T(8,128)S(1)}, bf16[8,128,128]{2,1,0:...) custom-call(s32[4]{0:T(128)S(1)} %pad_add_fusion.scalar_ref, ...), custom_call_target="tpu_custom_call", output_to_operand_aliasing={{0}: (9, {})} | custom-call | flops 1677721600 | bytes 926736 | tf_op jit(solution)/shard_map/pallas_call | solution.py:335
  4.0 1.3 %collective-permute-start.9 = (bf16[256,128]{1,0:T(8,128)(2,1)S(1)}, bf16[256,128]{1,0:T(8,128)(2,1)S(1)}, u32[]{:S(2)}, u32[]{:S(2)}) collective-permute-start(bf16[256,128]{1,0:T(8,128)(2,1)S(1)} %get-tuple-element.44), channel_id=1, source_target_pairs={{0,12},{1,13},{2,14},{3,15},{16,28},{17,29},{18,30},{19,31}} | collective-permute-start | bytes 196616 | tf_op jit(solution)/shard_map/ppermute | solution.py:440
  5.3 1.3 %collective-permute-start.5 = (bf16[256,128]{1,0:T(8,128)(2,1)S(1)}, bf16[256,128]{1,0:T(8,128)(2,1)S(1)}, u32[]{:S(2)}, u32[]{:S(2)}) collective-permute-start(bf16[256,128]{1,0:T(8,128)(2,1)S(1)} %get-tuple-element.44), channel_id=1, source_target_pairs={{0,4},{4,8},{8,12},{1,5},{5,9},{9,13},{2,6},{6,10},{10,14},{3,7},{... | collective-permute-start | bytes 196616 | tf_op jit(solution)/shard_map/ppermute | solution.py:438
  6.6 0.0 collective-permute-done.1.s_ref.refs_0_
  6.6 0.2 shard_map.133
  6.8 0.7 %collective-permute-start.3 = (bf16[4,128,128]{2,1,0:T(8,128)(2,1)S(1)}, bf16[4,128,128]{2,1,0:T(8,128)(2,1)S(1)}, u32[]{:S(2)}, u32[]{:S(2)}) collective-permute-start(bf16[4,128,128]{2,1,0:T(8,128)(2,1)S(1)} %shard_map.133), channel_id=1, source_target_pairs={{4,8},{5,9},{6,10},{7,11},{20,24},{21,25},{22,26},{23,27}} | collective-permute-start | bytes 393224 | tf_op jit(solution)/shard_map/ppermute | solution.py:405
  7.5 0.0 collective-permute-done.s_ref.refs_0_
  7.5 0.2 shard_map.134
  7.7 0.7 %collective-permute-start.2 = (bf16[4,128,128]{2,1,0:T(8,128)(2,1)S(1)}, bf16[4,128,128]{2,1,0:T(8,128)(2,1)S(1)}, u32[]{:S(2)}, u32[]{:S(2)}) collective-permute-start(bf16[4,128,128]{2,1,0:T(8,128)(2,1)S(1)} %shard_map.134), channel_id=1, source_target_pairs={{4,8},{5,9},{6,10},{7,11},{20,24},{21,25},{22,26},{23,27}} | collective-permute-start | bytes 393224 | tf_op jit(solution)/shard_map/ppermute | solution.py:405
  8.3 0.0 copy-start.6
  8.3 0.0 copy-start.8
  8.4 2.8 %shard_map.135 = (bf16[8,128,128]{2,1,0:T(8,128)(2,1)S(1)}, bf16[8,128,128]{2,1,0:T(8,128)(2,1)S(1)}, f32[8,128,128]{2,1,0:T(8,128)S(1)}, bf16[8,128,128]{2,1,0:T(8,128)(2,1)S(1)}) custom-call(s32[4]{0:T(128)S(1)} %pad_add_fusion.scalar_ref, bf16[128,512]{1,0:T(8,128)(2,1)S(1)} %copy-done.7, ...), custom_call_target="tpu_custom_call", output_to_operand_aliasing={{0}: (6, {}), {1}: (7, {}), {2}: (8, {}), {3}: (9, {})} | custom-call | flops 1677721600 | bytes 1712656 | tf_op jit(solution)/shard_map/pallas_call | solution.py:335
  11.2 0.3 %collective-permute-done.5.refs_0_ = bf16[256,128]{1,0:T(8,128)(2,1)S(1)} collective-permute-done((bf16[256,128]{1,0:T(8,128)(2,1)S(1)}, bf16[256,128]{1,0:T(8,128)(2,1)S(1)}, u32[]{:S(2)}, u32[]{:S(2)}) %collective-permute-start.5) | collective-permute-done | bytes 65568 | tf_op jit(solution)/shard_map/ppermute | solution.py:438
  11.4 1.3 %collective-permute-start.7 = (bf16[256,128]{1,0:T(8,128)(2,1)S(1)}, bf16[256,128]{1,0:T(8,128)(2,1)S(1)}, u32[]{:S(2)}, u32[]{:S(2)}) collective-permute-start(bf16[256,128]{1,0:T(8,128)(2,1)S(1)} %collective-permute-done.5.refs_0_), channel_id=1, source_target_pairs={{4,8},{8,12},{5,9},{9,13},{6,10},{10,14},{7,11},{11,15},{20,24},{2... | collective-permute-start | bytes 196616 | tf_op jit(solution)/shard_map/ppermute | solution.py:445
  12.8 1.7 %shard_map.136 = (f32[8,128,128]{2,1,0:T(8,128)S(1)}, bf16[8,128,128]{2,1,0:T(8,128)(2,1)S(1)}, f32[8,128,128]{2,1,0:T(8,128)S(1)}) custom-call(s32[4]{0:T(128)S(1)} %pad_add_fusion.scalar_ref, s32[1,128]{1,0:T(1,128)S(1)} %bitcast.9, f32[8,128]{1,0:T(8,128)S(1)} %copy-done.10, f32[8,128]{1,0:T(8,128)S(1)} %copy-done.9, bf16[128,512]{1,0:T(8,128)(2,1)S(1)} %copy-done.8, ...), custom_call_target="tpu_custom_call" | custom-call | flops 5033164800 | bytes 1057808 | tf_op jit(solution)/shard_map/pallas_call | solution.py:335
  14.5 0.0 collective-permute-done.3.s_ref.refs_1_
  14.5 0.2 shard_map.137
  14.7 0.0 copy-start
  14.7 0.0 copy-start.1
  14.7 1.4 %collective-permute-start.11 = (bf16[4,128,128]{2,1,0:T(8,128)(2,1)S(1)}, bf16[4,128,128]{2,1,0:T(8,128)(2,1)S(1)}, u32[]{:S(2)}, u32[]{:S(2)}) collective-permute-start(bf16[4,128,128]{2,1,0:T(8,128)(2,1)S(1)} %shard_map.137), channel_id=1, source_target_pairs={{8,12},{9,13},{10,14},{11,15},{24,28},{25,29},{26,30},{27,31}} | collective-permute-start | bytes 393224 | tf_op jit(solution)/shard_map/ppermute | solution.py:405
  16.2 0.0 collective-permute-done.2.s_ref.refs_1_
  16.2 0.2 shard_map.138
  16.3 1.3 %collective-permute-start.4 = (bf16[4,128,128]{2,1,0:T(8,128)(2,1)S(1)}, bf16[4,128,128]{2,1,0:T(8,128)(2,1)S(1)}, u32[]{:S(2)}, u32[]{:S(2)}) collective-permute-start(bf16[4,128,128]{2,1,0:T(8,128)(2,1)S(1)} %shard_map.138), channel_id=1, source_target_pairs={{8,12},{9,13},{10,14},{11,15},{24,28},{25,29},{26,30},{27,31}} | collective-permute-start | bytes 393224 | tf_op jit(solution)/shard_map/ppermute | solution.py:405
  17.6 0.0 collective-permute-done.9.refs_4_
  17.7 0.1 collective-permute-start.10
  17.7 1.5 %collective-permute-done.7.refs_2_ = bf16[256,128]{1,0:T(8,128)(2,1)S(1)} collective-permute-done((bf16[256,128]{1,0:T(8,128)(2,1)S(1)}, bf16[256,128]{1,0:T(8,128)(2,1)S(1)}, u32[]{:S(2)}, u32[]{:S(2)}) %collective-permute-start.7) | collective-permute-done | bytes 65568 | tf_op jit(solution)/shard_map/ppermute | solution.py:445
  19.2 0.0 collective-permute-start.8
  19.2 0.5 %collective-permute-start.6 = (bf16[256,128]{1,0:T(8,128)(2,1)S(1)}, bf16[256,128]{1,0:T(8,128)(2,1)S(1)}, u32[]{:S(2)}, u32[]{:S(2)}) collective-permute-start(bf16[256,128]{1,0:T(8,128)(2,1)S(1)} %collective-permute-done.5.refs_0_), channel_id=1, source_target_pairs={{0,1},{1,0},{2,3},{3,2},{4,5},{5,4},{6,7},{7,6},{8,9},{9,8},{10,11... | collective-permute-start | bytes 196616 | tf_op jit(solution)/shard_map/ppermute | solution.py:427
  19.7 0.0 collective-permute-done.10.refs_5_
  19.7 0.7 %collective-permute-done.8.refs_3_ = bf16[256,128]{1,0:T(8,128)(2,1)S(1)} collective-permute-done((bf16[256,128]{1,0:T(8,128)(2,1)S(1)}, bf16[256,128]{1,0:T(8,128)(2,1)S(1)}, u32[]{:S(2)}, u32[]{:S(2)}) %collective-permute-start.8) | collective-permute-done | bytes 65568 | tf_op jit(solution)/shard_map/ppermute | solution.py:427
  20.5 0.2 collective-permute-done.6.refs_1_
  20.6 0.0 copy-done.1
  20.6 2.0 %shard_map.139 = bf16[128,1024]{1,0:T(8,128)(2,1)} custom-call(s32[4]{0:T(128)S(1)} %pad_add_fusion.scalar_ref, s32[1,128]{1,0:T(1,128)S(1)} %bitcast.10, bf16[128,1024]{1,0:T(8,128)(2,1)S(1)} %copy-done, bf16[128,1024]{1,0:T(8,128)(2,1)S(1)} %copy-done.1, bf16[128,512]{1,0:T(8,128)(2,1)S(1)} %copy-done.2, bf16[128,512]{1,0:T(8,128)(2,1)S(1)} %copy-done.3, ...), custom_call_target="tpu_custom_call" | custom-call | flops 268435456 | bytes 1180176 | tf_op jit(solution)/shard_map/pallas_call | solution.py:335
  22.7 2.1 %collective-permute-done.11.refs_2_ = bf16[4,128,128]{2,1,0:T(8,128)(2,1)S(1)} collective-permute-done((bf16[4,128,128]{2,1,0:T(8,128)(2,1)S(1)}, bf16[4,128,128]{2,1,0:T(8,128)(2,1)S(1)}, u32[]{:S(2)}, u32[]{:S(2)}) %collective-permute-start.11) | collective-permute-done | bytes 131104 | tf_op jit(solution)/shard_map/ppermute | solution.py:405
  24.7 0.3 %shard_map.140.refs_6_ = bf16[128,512]{1,0:T(8,128)(2,1)S(1)} custom-call(bf16[4,128,128]{2,1,0:T(8,128)(2,1)S(1)} %collective-permute-done.1.s_ref.refs_0_, bf16[4,128,128]{2,1,0:T(8,128)(2,1)S(1)} %collective-permute-done.3.s_ref.refs_1_, bf16[4,128,128]{2,1,0:T(8,128)(2,1)S(1)} %collective-permute-done.11.refs_2_, ...), custom_call_target="tpu_custom_call" | custom-call | flops 16777216 | bytes 1703936 | tf_op jit(solution)/shard_map/pallas_call | solution.py:335
  25.1 1.3 %collective-permute-done.4.refs_2_ = bf16[4,128,128]{2,1,0:T(8,128)(2,1)S(1)} collective-permute-done((bf16[4,128,128]{2,1,0:T(8,128)(2,1)S(1)}, bf16[4,128,128]{2,1,0:T(8,128)(2,1)S(1)}, u32[]{:S(2)}, u32[]{:S(2)}) %collective-permute-start.4) | collective-permute-done | bytes 131104 | tf_op jit(solution)/shard_map/ppermute | solution.py:405
  26.4 1.0 %shard_map.141 = bf16[128,1024]{1,0:T(8,128)(2,1)} custom-call(bf16[4,128,128]{2,1,0:T(8,128)(2,1)S(1)} %collective-permute-done.s_ref.refs_0_, bf16[4,128,128]{2,1,0:T(8,128)(2,1)S(1)} %collective-permute-done.2.s_ref.refs_1_, bf16[4,128,128]{2,1,0:T(8,128)(2,1)S(1)} %collective-permute-done.4.refs_2_, f32[8,128,128]{2,1,0:T(8,128)S(1)} %get-tuple-element.49.refs_3_, ...), custom_call_target="tpu_custom_call" | custom-call | flops 16777216 | bytes 1835008 | tf_op jit(solution)/shard_map/pallas_call | solution.py:335
  (12 shorter events, 0.0 us)
Async XLA Ops:
  0.7 2.0 %copy-start.2 = (bf16[128,512]{1,0:T(8,128)(2,1)S(1)}, bf16[128,512]{1,0:T(8,128)(2,1)}, u32[]{:S(2)}) copy-start(bf16[128,512]{1,0:T(8,128)(2,1)} %k_ref.3) | copy-start | bytes 393220
  0.7 2.0 %copy-start.3 = (bf16[128,512]{1,0:T(8,128)(2,1)S(1)}, bf16[128,512]{1,0:T(8,128)(2,1)}, u32[]{:S(2)}) copy-start(bf16[128,512]{1,0:T(8,128)(2,1)} %v_ref.1) | copy-start | bytes 393220
  0.7 2.0 %copy-start.5 = (bf16[128,1024]{1,0:T(8,128)(2,1)S(1)}, bf16[128,1024]{1,0:T(8,128)(2,1)}, u32[]{:S(2)}) copy-start(bf16[128,1024]{1,0:T(8,128)(2,1)} %refs_4_.5) | copy-start | bytes 786436
  0.7 2.0 %copy-start.7 = (bf16[128,512]{1,0:T(8,128)(2,1)S(1)}, bf16[128,512]{1,0:T(8,128)(2,1)}, u32[]{:S(2)}) copy-start(bf16[128,512]{1,0:T(8,128)(2,1)} %k_ref.2) | copy-start | bytes 393220
  0.8 2.0 %copy-start.10 = (f32[8,128]{1,0:T(8,128)S(1)}, f32[8,128]{1,0:T(8,128)}, u32[]{:S(2)}) copy-start(f32[8,128]{1,0:T(8,128)} %beta_ref.1) | copy-start | bytes 12292
  1.4 1.4 %copy-start.9 = (f32[8,128]{1,0:T(8,128)S(1)}, f32[8,128]{1,0:T(8,128)}, u32[]{:S(2)}) copy-start(f32[8,128]{1,0:T(8,128)} %gate_ref.2) | copy-start | bytes 12292
  1.4 5.2 %collective-permute-start.1 = (bf16[4,128,128]{2,1,0:T(8,128)(2,1)S(1)}, bf16[4,128,128]{2,1,0:T(8,128)(2,1)S(1)}, u32[]{:S(2)}, u32[]{:S(2)}) collective-permute-start(bf16[4,128,128]{2,1,0:T(8,128)(2,1)S(1)} %get-tuple-element.28), channel_id=1, source_target_pairs={{0,4},{1,5},{2,6},{3,7},{16,20},{17,21},{18,22},{19,23}} | collective-permute-start | bytes 393224 | tf_op jit(solution)/shard_map/ppermute | solution.py:405
  2.1 5.4 %collective-permute-start = (bf16[4,128,128]{2,1,0:T(8,128)(2,1)S(1)}, bf16[4,128,128]{2,1,0:T(8,128)(2,1)S(1)}, u32[]{:S(2)}, u32[]{:S(2)}) collective-permute-start(bf16[4,128,128]{2,1,0:T(8,128)(2,1)S(1)} %get-tuple-element.27), channel_id=1, source_target_pairs={{0,4},{1,5},{2,6},{3,7},{16,20},{17,21},{18,22},{19,23}} | collective-permute-start | bytes 393224 | tf_op jit(solution)/shard_map/ppermute | solution.py:405
  2.7 0.7 %copy-start.4 = (s32[128]{0:T(128)S(1)}, s32[128]{0:T(128)}, u32[]{:S(2)}) copy-start(s32[128]{0:T(128)} %param.12) | copy-start | bytes 1540
  2.8 0.7 %copy-start.11 = (f32[128]{0:T(128)S(1)}, f32[128]{0:T(128)}, u32[]{:S(2)}) copy-start(f32[128]{0:T(128)} %param.19) | copy-start | bytes 1540
  4.0 13.7 %collective-permute-start.9 = (bf16[256,128]{1,0:T(8,128)(2,1)S(1)}, bf16[256,128]{1,0:T(8,128)(2,1)S(1)}, u32[]{:S(2)}, u32[]{:S(2)}) collective-permute-start(bf16[256,128]{1,0:T(8,128)(2,1)S(1)} %get-tuple-element.44), channel_id=1, source_target_pairs={{0,12},{1,13},{2,14},{3,15},{16,28},{17,29},{18,30},{19,31}} | collective-permute-start | bytes 196616 | tf_op jit(solution)/shard_map/ppermute | solution.py:440
  5.3 6.2 %collective-permute-start.5 = (bf16[256,128]{1,0:T(8,128)(2,1)S(1)}, bf16[256,128]{1,0:T(8,128)(2,1)S(1)}, u32[]{:S(2)}, u32[]{:S(2)}) collective-permute-start(bf16[256,128]{1,0:T(8,128)(2,1)S(1)} %get-tuple-element.44), channel_id=1, source_target_pairs={{0,4},{4,8},{8,12},{1,5},{5,9},{9,13},{2,6},{6,10},{10,14},{3,7},{... | collective-permute-start | bytes 196616 | tf_op jit(solution)/shard_map/ppermute | solution.py:438
  6.8 7.7 %collective-permute-start.3 = (bf16[4,128,128]{2,1,0:T(8,128)(2,1)S(1)}, bf16[4,128,128]{2,1,0:T(8,128)(2,1)S(1)}, u32[]{:S(2)}, u32[]{:S(2)}) collective-permute-start(bf16[4,128,128]{2,1,0:T(8,128)(2,1)S(1)} %shard_map.133), channel_id=1, source_target_pairs={{4,8},{5,9},{6,10},{7,11},{20,24},{21,25},{22,26},{23,27}} | collective-permute-start | bytes 393224 | tf_op jit(solution)/shard_map/ppermute | solution.py:405
  7.7 8.5 %collective-permute-start.2 = (bf16[4,128,128]{2,1,0:T(8,128)(2,1)S(1)}, bf16[4,128,128]{2,1,0:T(8,128)(2,1)S(1)}, u32[]{:S(2)}, u32[]{:S(2)}) collective-permute-start(bf16[4,128,128]{2,1,0:T(8,128)(2,1)S(1)} %shard_map.134), channel_id=1, source_target_pairs={{4,8},{5,9},{6,10},{7,11},{20,24},{21,25},{22,26},{23,27}} | collective-permute-start | bytes 393224 | tf_op jit(solution)/shard_map/ppermute | solution.py:405
  8.3 4.4 %copy-start.6 = (bf16[128,1024]{1,0:T(8,128)(2,1)S(1)}, bf16[128,1024]{1,0:T(8,128)(2,1)}, u32[]{:S(2)}) copy-start(bf16[128,1024]{1,0:T(8,128)(2,1)} %z_ref.1) | copy-start | bytes 786436
  8.3 4.4 %copy-start.8 = (bf16[128,512]{1,0:T(8,128)(2,1)S(1)}, bf16[128,512]{1,0:T(8,128)(2,1)}, u32[]{:S(2)}) copy-start(bf16[128,512]{1,0:T(8,128)(2,1)} %q_ref.2) | copy-start | bytes 393220
  11.4 7.8 %collective-permute-start.7 = (bf16[256,128]{1,0:T(8,128)(2,1)S(1)}, bf16[256,128]{1,0:T(8,128)(2,1)S(1)}, u32[]{:S(2)}, u32[]{:S(2)}) collective-permute-start(bf16[256,128]{1,0:T(8,128)(2,1)S(1)} %collective-permute-done.5.refs_0_), channel_id=1, source_target_pairs={{4,8},{8,12},{5,9},{9,13},{6,10},{10,14},{7,11},{11,15},{20,24},{2... | collective-permute-start | bytes 196616 | tf_op jit(solution)/shard_map/ppermute | solution.py:445
  14.7 5.9 %copy-start = (bf16[128,1024]{1,0:T(8,128)(2,1)S(1)}, bf16[128,1024]{1,0:T(8,128)(2,1)}, u32[]{:S(2)}) copy-start(bf16[128,1024]{1,0:T(8,128)(2,1)} %q_ref.3) | copy-start | bytes 786436
  14.7 5.9 %copy-start.1 = (bf16[128,1024]{1,0:T(8,128)(2,1)S(1)}, bf16[128,1024]{1,0:T(8,128)(2,1)}, u32[]{:S(2)}) copy-start(bf16[128,1024]{1,0:T(8,128)(2,1)} %gate_ref.3) | copy-start | bytes 786436
  14.7 10.0 %collective-permute-start.11 = (bf16[4,128,128]{2,1,0:T(8,128)(2,1)S(1)}, bf16[4,128,128]{2,1,0:T(8,128)(2,1)S(1)}, u32[]{:S(2)}, u32[]{:S(2)}) collective-permute-start(bf16[4,128,128]{2,1,0:T(8,128)(2,1)S(1)} %shard_map.137), channel_id=1, source_target_pairs={{8,12},{9,13},{10,14},{11,15},{24,28},{25,29},{26,30},{27,31}} | collective-permute-start | bytes 393224 | tf_op jit(solution)/shard_map/ppermute | solution.py:405
  16.3 10.0 %collective-permute-start.4 = (bf16[4,128,128]{2,1,0:T(8,128)(2,1)S(1)}, bf16[4,128,128]{2,1,0:T(8,128)(2,1)S(1)}, u32[]{:S(2)}, u32[]{:S(2)}) collective-permute-start(bf16[4,128,128]{2,1,0:T(8,128)(2,1)S(1)} %shard_map.138), channel_id=1, source_target_pairs={{8,12},{9,13},{10,14},{11,15},{24,28},{25,29},{26,30},{27,31}} | collective-permute-start | bytes 393224 | tf_op jit(solution)/shard_map/ppermute | solution.py:405
  17.7 2.1 %collective-permute-start.10 = (bf16[256,128]{1,0:T(8,128)(2,1)S(1)}, bf16[256,128]{1,0:T(8,128)(2,1)S(1)}, u32[]{:S(2)}, u32[]{:S(2)}) collective-permute-start(bf16[256,128]{1,0:T(8,128)(2,1)S(1)} %collective-permute-done.9.refs_4_), channel_id=1, source_target_pairs={{0,1},{1,0},{2,3},{3,2},{4,5},{5,4},{6,7},{7,6},{8,9},{9,8},{10,11... | collective-permute-start | bytes 196616 | tf_op jit(solution)/shard_map/ppermute | solution.py:427
  19.2 1.3 %collective-permute-start.8 = (bf16[256,128]{1,0:T(8,128)(2,1)S(1)}, bf16[256,128]{1,0:T(8,128)(2,1)S(1)}, u32[]{:S(2)}, u32[]{:S(2)}) collective-permute-start(bf16[256,128]{1,0:T(8,128)(2,1)S(1)} %collective-permute-done.7.refs_2_), channel_id=1, source_target_pairs={{0,1},{1,0},{2,3},{3,2},{4,5},{5,4},{6,7},{7,6},{8,9},{9,8},{10,11... | collective-permute-start | bytes 196616 | tf_op jit(solution)/shard_map/ppermute | solution.py:427
  19.2 1.4 %collective-permute-start.6 = (bf16[256,128]{1,0:T(8,128)(2,1)S(1)}, bf16[256,128]{1,0:T(8,128)(2,1)S(1)}, u32[]{:S(2)}, u32[]{:S(2)}) collective-permute-start(bf16[256,128]{1,0:T(8,128)(2,1)S(1)} %collective-permute-done.5.refs_0_), channel_id=1, source_target_pairs={{0,1},{1,0},{2,3},{3,2},{4,5},{5,4},{6,7},{7,6},{8,9},{9,8},{10,11... | collective-permute-start | bytes 196616 | tf_op jit(solution)/shard_map/ppermute | solution.py:427

commit v6 on v5

--- a/solution.py
+++ b/solution.py
@@ -259,9 +259,10 @@
 
 
 def output_kernel(begin, hops, *refs):
-    states, terms, ready = refs[:hops], refs[hops : hops + 3], refs[hops + 3 : -3]
-    out_hbm, held_ref, sems = refs[-3:]
-    copies = []
+    states, terms, attn_ref, ready = refs[:hops], refs[hops : hops + 3], refs[hops + 3], refs[hops + 4 : -4]
+    out_hbm, attn_hbm, held_ref, sems = refs[-4:]
+    copies = [pltpu.make_async_copy(attn_ref, attn_hbm, sems.at[len(ready) + 1])]
+    copies[0].start()
     spot = 0
     for at, part in enumerate((*ready, held_ref)):
         if part is held_ref:
@@ -275,7 +276,7 @@
 
 
 def attention_kernel(window, layout, scalar_ref, doc_ref, q_ref, gate_ref, k_ref, v_ref, *refs):
-    units, (out_hbm, held_ref, sems) = refs[:-3], refs[-3:]
+    units, out_ref = refs[:-1], refs[-1]
     length = q_ref.shape[0]
     heads = q_ref.shape[1] // HD_A
     groups = HD_A // DK
@@ -298,7 +299,6 @@
     keys = jnp.concatenate(keys, axis=0)
     values = jnp.concatenate(values, axis=0)
     step = 2
-    copies = []
     for first in range(0, heads, step):
         names = range(first, min(first + step, heads))
         queries = jnp.concatenate([q_ref[:, h * HD_A : (h + 1) * HD_A] for h in names], axis=0)
@@ -312,12 +312,7 @@
             part = slice(h * HD_A, (h + 1) * HD_A)
             rows = slice(at * length, (at + 1) * length)
             gate = 1.0 + jnp.exp(-gate_ref[:, part].astype(F32))
-            held_ref[:, part] = (mixed[rows] / (total[rows] * gate)).astype(BF16)
-            copy = pltpu.make_async_copy(held_ref.at[:, part], out_hbm.at[:, part], sems.at[h])
-            copy.start()
-            copies.append(copy)
-    for copy in copies:
-        copy.wait()
+            out_ref[:, part] = (mixed[rows] / (total[rows] * gate)).astype(BF16)
 
 
 def call(kernel, out_shape, operands, flops, scalars=1, outside=0, scratch=(), aliases=None, held=pltpu.VMEM):
@@ -437,14 +432,9 @@
     )
     units = [lax.ppermute(unit, "seq", [(i, i + 1) for i in range(devices - 1)])]
     direct = wanted == devices - 1 and wanted > 1
-    farthest = [lax.ppermute(unit, "seq", [(0, wanted)])] if direct else []
     leaving = combined(arrived[-1], carry, added)
     arrived.append(hand_on(1, leaving))
-    block = after(units[0], leaving[-1])
-    for distance in range(2, wanted + 1 - direct):
-        block = lax.ppermute(block, "seq", [(i, i + 1) for i in range(distance - 1, devices - 1)])
-        units.append(block)
-    units += farthest
+    farthest = [lax.ppermute(after(unit, leaving[-1]), "seq", [(0, wanted)])] if direct else []
     fresh, erased, added, carry = call(
         later_kernel,
         terms,
@@ -452,6 +442,11 @@
         work,
         aliases={6: 0, 7: 1, 8: 2, 9: 3},
     )
+    block = after(units[0], fresh)
+    for distance in range(2, wanted + 1 - direct):
+        block = lax.ppermute(block, "seq", [(i, i + 1) for i in range(distance - 1, devices - 1)])
+        units.append(block)
+    units += farthest
     def queries(first):
         mixing.extend(call(
             query_kernel,
@@ -464,7 +459,7 @@
                 *(scalars, inputs[3], inputs[2], inputs[1], q_gdn, inputs[0], z_gdn, gain_in),
                 *(after(fresh, first), erased),
             ),
-            3 * work,
+            work,
         ))
         return mixing[:1]
 
@@ -486,8 +481,6 @@
         shape(q_attn.shape, BF16),
         (scalars, inputs[3], q_attn, gate_attn, k_attn, v_attn, *sections),
         4 * local_heads * length * length * (wanted + 1) * HD_A,
-        scratch=[pltpu.VMEM(q_attn.shape, BF16), pltpu.SemaphoreType.DMA((local_heads,))],
-        held=pltpu.HBM,
     )
     ready = []
     for at in range(pieces):
@@ -504,16 +497,15 @@
                     0,
                 )
             )
-    gdn_out = call(
+    return call(
         functools.partial(output_kernel, at * piece, len(states)),
-        shape(v_gdn.shape, BF16),
-        (*operands, *ready),
+        (shape(v_gdn.shape, BF16), shape(q_attn.shape, BF16)),
+        (*operands, attn_out, *ready),
         cost,
         0,
-        scratch=[pltpu.VMEM((length, piece * DV), BF16), pltpu.SemaphoreType.DMA((pieces,))],
+        scratch=[pltpu.VMEM((length, piece * DV), BF16), pltpu.SemaphoreType.DMA((pieces + 1,))],
         held=pltpu.HBM,
     )
-    return (gdn_out, attn_out)
 
 
 def solution(mesh):

time: 27.7 us -> 27.1 us (0.978)
  Pallas kernels: 9.72 us -> 9.05 us
    pallas_call x11, Pallas kernels: 9.72 us -> 9.05 us  [call(): pl.pallas_call(kernel, out_shape=out_shape, in_specs=specs, out_specs=jax...]
    ppermute x1, waiting for transfers between devices: 0.01 us -> 0.53 us  [shards(): lax.ppermute(after(unit, leaving[-1]), 'seq', [(0, wanted)])]
    ppermute x1, waiting for transfers between devices: 1.47 us -> 1 us  [shards(): lax.ppermute(block, 'seq', [(i, i + 1) for i in range(distance - 1, devic...]
    ppermute x6, waiting for transfers between devices: 3.42 us -> 3.77 us  [hand_on(): return [lax.ppermute(s, 'seq', [(hop, hop + 1)]) for s in pieces_out]]
    ppermute x1, waiting for transfers between devices: 0.29 us -> 0.01 us  [shards(): lax.ppermute(unit, 'seq', [(i, i + 1) for i in range(devices - 1)])]
  transfers between devices with their start and end apart: 12 -> 12, of which waited for: 6 -> 6; matrix products, arithmetic and copies ran while one was open for 0% -> 0% of each run, Pallas kernels for 30% -> 28%
where the time goes in v6:
time: 27.1 us; the launch traced here: 26.7 us
  starting transfers between devices  9.78 us (36%)
  Pallas kernels  9.05 us (33%)
  waiting for transfers between devices  6.2 us (23%)
  between operations  0.99 us (4%)
  local copies, waits for them, and re-layouts  0.65 us (2%)
    pallas_call x11, Pallas kernels, call(): pl.pallas_call(kernel, out_shape=out_shape, in_specs=specs, out_specs=jax...  9.05 us
    ppermute x6, starting transfers between devices, hand_on(): return [lax.ppermute(s, 'seq', [(hop, hop + 1)]) for s in pieces_out]  5.39 us
    ppermute x6, waiting for transfers between devices, hand_on(): return [lax.ppermute(s, 'seq', [(hop, hop + 1)]) for s in pieces_out]  3.77 us
    ppermute x1, starting transfers between devices, shards(): lax.ppermute(unit, 'seq', [(i, i + 1) for i in range(devices - 1)])  1.29 us
    ppermute x1, starting transfers between devices, shards(): lax.ppermute(after(unit, leaving[-1]), 'seq', [(0, wanted)])  1.29 us
    ppermute x1, starting transfers between devices, shards(): lax.ppermute(block, 'seq', [(i, i + 1) for i in range(distance - 1, devic...  1.29 us
    ppermute x1, waiting for transfers between devices, shards(): lax.ppermute(block, 'seq', [(i, i + 1) for i in range(distance - 1, devic...  1 us
    ppermute x3, waiting for transfers between devices, swapped(): return lax.ppermute(got, 'head', pairs)  0.9 us
  transfers between devices with their start and end apart: 12, of which 6 were waited for; matrix products, arithmetic and copies ran while one was open for 0% of the time, Pallas kernels for 28%

profile of v6, /device:TPU:26, one launch (start us, length us, event | category | flops | bytes accessed | tf_op | source)
XLA Modules:
  0.0 26.7 jit_solution(15314483512555294976)
XLA Ops:
  0.7 0.1 pad_add_fusion.scalar_ref
  0.8 0.0 copy-start.10
  0.8 0.6 %shard_map.131 = (bf16[8,128,128]{2,1,0:T(8,128)(2,1)S(1)}, bf16[4,128,128]{2,1,0:T(8,128)(2,1)S(1)}, bf16[4,128,128]{2,1,0:T(8,128)(2,1)S(1)}) custom-call(s32[4]{0:T(128)S(1)} %pad_add_fusion.scalar_ref, bf16[128,512]{1,0:T(8,128)(2,1)} %k_ref.2, f32[8,128]{1,0:T(8,128)} %gate_ref.2, f32[8,128]{1,0:T(8,128)} %beta_ref.1, s32[1,128]{1,0:T(1,128)} %bitcast.6, ...), custom_call_target="tpu_custom_call" | custom-call | flops 1677721600 | bytes 401936 | tf_op jit(solution)/shard_map/pallas_call | solution.py:330
  1.4 0.0 copy-start.9
  1.4 0.7 %collective-permute-start.1 = (bf16[4,128,128]{2,1,0:T(8,128)(2,1)S(1)}, bf16[4,128,128]{2,1,0:T(8,128)(2,1)S(1)}, u32[]{:S(2)}, u32[]{:S(2)}) collective-permute-start(bf16[4,128,128]{2,1,0:T(8,128)(2,1)S(1)} %get-tuple-element.30), channel_id=1, source_target_pairs={{0,4},{1,5},{2,6},{3,7},{16,20},{17,21},{18,22},{19,23}} | collective-permute-start | bytes 393224 | tf_op jit(solution)/shard_map/ppermute | solution.py:400
  2.1 0.7 %collective-permute-start = (bf16[4,128,128]{2,1,0:T(8,128)(2,1)S(1)}, bf16[4,128,128]{2,1,0:T(8,128)(2,1)S(1)}, u32[]{:S(2)}, u32[]{:S(2)}) collective-permute-start(bf16[4,128,128]{2,1,0:T(8,128)(2,1)S(1)} %get-tuple-element.29), channel_id=1, source_target_pairs={{0,4},{1,5},{2,6},{3,7},{16,20},{17,21},{18,22},{19,23}} | collective-permute-start | bytes 393224 | tf_op jit(solution)/shard_map/ppermute | solution.py:400
  2.7 0.0 copy-start.4
  2.8 0.0 copy-start.11
  2.8 0.0 copy-done.2
  2.8 0.0 copy-done.3
  2.8 0.6 %copy-done.4 = s32[128]{0:T(128)S(1)} copy-done((s32[128]{0:T(128)S(1)}, s32[128]{0:T(128)}, u32[]{:S(2)}) %copy-start.4) | copy-done | bytes 536
  3.4 0.0 copy-done.11
  3.4 0.6 %shard_map.132 = (bf16[8,128,128]{2,1,0:T(8,128)(2,1)S(1)}, bf16[8,128,128]{2,1,0:T(8,128)(2,1)S(1)}, f32[8,128,128]{2,1,0:T(8,128)S(1)}, bf16[8,128,128]{2,1,0:...) custom-call(s32[4]{0:T(128)S(1)} %pad_add_fusion.scalar_ref, ...), custom_call_target="tpu_custom_call", output_to_operand_aliasing={{0}: (9, {})} | custom-call | flops 1677721600 | bytes 926736 | tf_op jit(solution)/shard_map/pallas_call | solution.py:330
  4.0 1.3 %collective-permute-start.5 = (bf16[256,128]{1,0:T(8,128)(2,1)S(1)}, bf16[256,128]{1,0:T(8,128)(2,1)S(1)}, u32[]{:S(2)}, u32[]{:S(2)}) collective-permute-start(bf16[256,128]{1,0:T(8,128)(2,1)S(1)} %get-tuple-element.51), channel_id=1, source_target_pairs={{0,4},{4,8},{8,12},{1,5},{5,9},{9,13},{2,6},{6,10},{10,14},{3,7},{... | collective-permute-start | bytes 196616 | tf_op jit(solution)/shard_map/ppermute | solution.py:433
  5.3 0.0 collective-permute-done.1.s_ref.refs_0_
  5.3 0.2 shard_map.133
  5.5 0.7 %collective-permute-start.3 = (bf16[4,128,128]{2,1,0:T(8,128)(2,1)S(1)}, bf16[4,128,128]{2,1,0:T(8,128)(2,1)S(1)}, u32[]{:S(2)}, u32[]{:S(2)}) collective-permute-start(bf16[4,128,128]{2,1,0:T(8,128)(2,1)S(1)} %shard_map.133), channel_id=1, source_target_pairs={{4,8},{5,9},{6,10},{7,11},{20,24},{21,25},{22,26},{23,27}} | collective-permute-start | bytes 393224 | tf_op jit(solution)/shard_map/ppermute | solution.py:400
  6.2 0.0 collective-permute-done.s_ref.refs_0_
  6.2 0.2 shard_map.134
  6.4 0.7 %collective-permute-start.2 = (bf16[4,128,128]{2,1,0:T(8,128)(2,1)S(1)}, bf16[4,128,128]{2,1,0:T(8,128)(2,1)S(1)}, u32[]{:S(2)}, u32[]{:S(2)}) collective-permute-start(bf16[4,128,128]{2,1,0:T(8,128)(2,1)S(1)} %shard_map.134), channel_id=1, source_target_pairs={{4,8},{5,9},{6,10},{7,11},{20,24},{21,25},{22,26},{23,27}} | collective-permute-start | bytes 393224 | tf_op jit(solution)/shard_map/ppermute | solution.py:400
  7.0 0.0 copy-start.6
  7.0 0.0 copy-start.8
  7.1 2.8 %shard_map.135 = (bf16[8,128,128]{2,1,0:T(8,128)(2,1)S(1)}, bf16[8,128,128]{2,1,0:T(8,128)(2,1)S(1)}, f32[8,128,128]{2,1,0:T(8,128)S(1)}, bf16[8,128,128]{2,1,0:T(8,128)(2,1)S(1)}) custom-call(s32[4]{0:T(128)S(1)} %pad_add_fusion.scalar_ref, bf16[128,512]{1,0:T(8,128)(2,1)S(1)} %copy-done.7, ...), custom_call_target="tpu_custom_call", output_to_operand_aliasing={{0}: (6, {}), {1}: (7, {}), {2}: (8, {}), {3}: (9, {})} | custom-call | flops 1677721600 | bytes 1712656 | tf_op jit(solution)/shard_map/pallas_call | solution.py:330
  9.8 1.3 %collective-permute-start.9 = (bf16[256,128]{1,0:T(8,128)(2,1)S(1)}, bf16[256,128]{1,0:T(8,128)(2,1)S(1)}, u32[]{:S(2)}, u32[]{:S(2)}) collective-permute-start(bf16[256,128]{1,0:T(8,128)(2,1)S(1)} %get-tuple-element.51), channel_id=1, source_target_pairs={{0,12},{1,13},{2,14},{3,15},{16,28},{17,29},{18,30},{19,31}} | collective-permute-start | bytes 196616 | tf_op jit(solution)/shard_map/ppermute | solution.py:437
  11.1 0.0 collective-permute-done.5.refs_0_
  11.2 1.3 %collective-permute-start.7 = (bf16[256,128]{1,0:T(8,128)(2,1)S(1)}, bf16[256,128]{1,0:T(8,128)(2,1)S(1)}, u32[]{:S(2)}, u32[]{:S(2)}) collective-permute-start(bf16[256,128]{1,0:T(8,128)(2,1)S(1)} %collective-permute-done.5.refs_0_), channel_id=1, source_target_pairs={{4,8},{8,12},{5,9},{9,13},{6,10},{10,14},{7,11},{11,15},{20,24},{2... | collective-permute-start | bytes 196616 | tf_op jit(solution)/shard_map/ppermute | solution.py:447
  12.5 1.7 %shard_map.136 = (f32[8,128,128]{2,1,0:T(8,128)S(1)}, bf16[8,128,128]{2,1,0:T(8,128)(2,1)S(1)}, f32[8,128,128]{2,1,0:T(8,128)S(1)}) custom-call(s32[4]{0:T(128)S(1)} %pad_add_fusion.scalar_ref, s32[1,128]{1,0:T(1,128)S(1)} %bitcast.9, f32[8,128]{1,0:T(8,128)S(1)} %copy-done.10, f32[8,128]{1,0:T(8,128)S(1)} %copy-done.9, bf16[128,512]{1,0:T(8,128)(2,1)S(1)} %copy-done.8, ...), custom_call_target="tpu_custom_call" | custom-call | flops 1677721600 | bytes 1057808 | tf_op jit(solution)/shard_map/pallas_call | solution.py:330
  14.2 0.0 collective-permute-done.3.s_ref.refs_1_
  14.2 0.2 shard_map.137
  14.4 0.0 copy-start
  14.4 0.0 copy-start.1
  14.4 1.4 %collective-permute-start.11 = (bf16[4,128,128]{2,1,0:T(8,128)(2,1)S(1)}, bf16[4,128,128]{2,1,0:T(8,128)(2,1)S(1)}, u32[]{:S(2)}, u32[]{:S(2)}) collective-permute-start(bf16[4,128,128]{2,1,0:T(8,128)(2,1)S(1)} %shard_map.137), channel_id=1, source_target_pairs={{8,12},{9,13},{10,14},{11,15},{24,28},{25,29},{26,30},{27,31}} | collective-permute-start | bytes 393224 | tf_op jit(solution)/shard_map/ppermute | solution.py:400
  15.9 0.0 collective-permute-done.2.s_ref.refs_1_
  15.9 0.2 shard_map.138
  16.1 1.3 %collective-permute-start.4 = (bf16[4,128,128]{2,1,0:T(8,128)(2,1)S(1)}, bf16[4,128,128]{2,1,0:T(8,128)(2,1)S(1)}, u32[]{:S(2)}, u32[]{:S(2)}) collective-permute-start(bf16[4,128,128]{2,1,0:T(8,128)(2,1)S(1)} %shard_map.138), channel_id=1, source_target_pairs={{8,12},{9,13},{10,14},{11,15},{24,28},{25,29},{26,30},{27,31}} | collective-permute-start | bytes 393224 | tf_op jit(solution)/shard_map/ppermute | solution.py:400
  17.4 0.5 %collective-permute-done.9.refs_4_ = bf16[256,128]{1,0:T(8,128)(2,1)S(1)} collective-permute-done((bf16[256,128]{1,0:T(8,128)(2,1)S(1)}, bf16[256,128]{1,0:T(8,128)(2,1)S(1)}, u32[]{:S(2)}, u32[]{:S(2)}) %collective-permute-start.9) | collective-permute-done | bytes 65568 | tf_op jit(solution)/shard_map/ppermute | solution.py:437
  17.9 0.0 collective-permute-start.10
  17.9 1.0 %collective-permute-done.7.refs_2_ = bf16[256,128]{1,0:T(8,128)(2,1)S(1)} collective-permute-done((bf16[256,128]{1,0:T(8,128)(2,1)S(1)}, bf16[256,128]{1,0:T(8,128)(2,1)S(1)}, u32[]{:S(2)}, u32[]{:S(2)}) %collective-permute-start.7) | collective-permute-done | bytes 65568 | tf_op jit(solution)/shard_map/ppermute | solution.py:447
  18.9 0.0 collective-permute-start.8
  18.9 0.5 %collective-permute-start.6 = (bf16[256,128]{1,0:T(8,128)(2,1)S(1)}, bf16[256,128]{1,0:T(8,128)(2,1)S(1)}, u32[]{:S(2)}, u32[]{:S(2)}) collective-permute-start(bf16[256,128]{1,0:T(8,128)(2,1)S(1)} %collective-permute-done.5.refs_0_), channel_id=1, source_target_pairs={{0,1},{1,0},{2,3},{3,2},{4,5},{5,4},{6,7},{7,6},{8,9},{9,8},{10,11... | collective-permute-start | bytes 196616 | tf_op jit(solution)/shard_map/ppermute | solution.py:422
  19.4 0.0 collective-permute-done.10.refs_5_
  19.4 0.7 %collective-permute-done.8.refs_3_ = bf16[256,128]{1,0:T(8,128)(2,1)S(1)} collective-permute-done((bf16[256,128]{1,0:T(8,128)(2,1)S(1)}, bf16[256,128]{1,0:T(8,128)(2,1)S(1)}, u32[]{:S(2)}, u32[]{:S(2)}) %collective-permute-start.8) | collective-permute-done | bytes 65568 | tf_op jit(solution)/shard_map/ppermute | solution.py:422
  20.1 0.2 collective-permute-done.6.refs_1_
  20.3 1.4 %shard_map.139.refs_6_ = bf16[128,1024]{1,0:T(8,128)(2,1)S(1)} custom-call(s32[4]{0:T(128)S(1)} %pad_add_fusion.scalar_ref, s32[1,128]{1,0:T(1,128)S(1)} %bitcast.10, bf16[128,1024]{1,0:T(8,128)(2,1)S(1)} %copy-done, bf16[128,1024]{1,0:T(8,128)(2,1)S(1)} %copy-done.1, bf16[128,512]{1,0:T(8,128)(2,1)S(1)} %copy-done.2, bf16[128,512]{1,0:T(8,128)(2,1)S(1)} %copy-done.3, ...), custom_call_target="tpu_custom_call" | custom-call | flops 268435456 | bytes 1180176 | tf_op jit(solution)/shard_map/pallas_call | solution.py:330
  21.7 2.4 %collective-permute-done.11.refs_2_ = bf16[4,128,128]{2,1,0:T(8,128)(2,1)S(1)} collective-permute-done((bf16[4,128,128]{2,1,0:T(8,128)(2,1)S(1)}, bf16[4,128,128]{2,1,0:T(8,128)(2,1)S(1)}, u32[]{:S(2)}, u32[]{:S(2)}) %collective-permute-start.11) | collective-permute-done | bytes 131104 | tf_op jit(solution)/shard_map/ppermute | solution.py:400
  24.1 0.3 %shard_map.140.refs_7_ = bf16[128,512]{1,0:T(8,128)(2,1)S(1)} custom-call(bf16[4,128,128]{2,1,0:T(8,128)(2,1)S(1)} %collective-permute-done.1.s_ref.refs_0_, bf16[4,128,128]{2,1,0:T(8,128)(2,1)S(1)} %collective-permute-done.3.s_ref.refs_1_, bf16[4,128,128]{2,1,0:T(8,128)(2,1)S(1)} %collective-permute-done.11.refs_2_, ...), custom_call_target="tpu_custom_call" | custom-call | flops 16777216 | bytes 1703936 | tf_op jit(solution)/shard_map/pallas_call | solution.py:330
  24.4 1.3 %collective-permute-done.4.refs_2_ = bf16[4,128,128]{2,1,0:T(8,128)(2,1)S(1)} collective-permute-done((bf16[4,128,128]{2,1,0:T(8,128)(2,1)S(1)}, bf16[4,128,128]{2,1,0:T(8,128)(2,1)S(1)}, u32[]{:S(2)}, u32[]{:S(2)}) %collective-permute-start.4) | collective-permute-done | bytes 131104 | tf_op jit(solution)/shard_map/ppermute | solution.py:400
  25.8 1.0 %shard_map.141 = (bf16[128,1024]{1,0:T(8,128)(2,1)}, bf16[128,1024]{1,0:T(8,128)(2,1)}) custom-call(bf16[4,128,128]{2,1,0:T(8,128)(2,1)S(1)} %collective-permute-done.s_ref.refs_0_, bf16[4,128,128]{2,1,0:T(8,128)(2,1)S(1)} %collective-permute-done.2.s_ref.refs_1_, bf16[4,128,128]{2,1,0:T(8,128)(2,1)S(1)} %collective-permute-done.4.refs_2_, ...), custom_call_target="tpu_custom_call" | custom-call | flops 16777216 | bytes 2097152 | tf_op jit(solution)/shard_map/pallas_call | solution.py:330
  (12 shorter events, 0.0 us)
Async XLA Ops:
  0.7 2.0 %copy-start.2 = (bf16[128,512]{1,0:T(8,128)(2,1)S(1)}, bf16[128,512]{1,0:T(8,128)(2,1)}, u32[]{:S(2)}) copy-start(bf16[128,512]{1,0:T(8,128)(2,1)} %k_ref.3) | copy-start | bytes 393220
  0.7 2.0 %copy-start.3 = (bf16[128,512]{1,0:T(8,128)(2,1)S(1)}, bf16[128,512]{1,0:T(8,128)(2,1)}, u32[]{:S(2)}) copy-start(bf16[128,512]{1,0:T(8,128)(2,1)} %v_ref.1) | copy-start | bytes 393220
  0.7 2.0 %copy-start.5 = (bf16[128,1024]{1,0:T(8,128)(2,1)S(1)}, bf16[128,1024]{1,0:T(8,128)(2,1)}, u32[]{:S(2)}) copy-start(bf16[128,1024]{1,0:T(8,128)(2,1)} %refs_4_.5) | copy-start | bytes 786436
  0.7 2.0 %copy-start.7 = (bf16[128,512]{1,0:T(8,128)(2,1)S(1)}, bf16[128,512]{1,0:T(8,128)(2,1)}, u32[]{:S(2)}) copy-start(bf16[128,512]{1,0:T(8,128)(2,1)} %k_ref.2) | copy-start | bytes 393220
  0.8 2.0 %copy-start.10 = (f32[8,128]{1,0:T(8,128)S(1)}, f32[8,128]{1,0:T(8,128)}, u32[]{:S(2)}) copy-start(f32[8,128]{1,0:T(8,128)} %beta_ref.1) | copy-start | bytes 12292
  1.4 1.4 %copy-start.9 = (f32[8,128]{1,0:T(8,128)S(1)}, f32[8,128]{1,0:T(8,128)}, u32[]{:S(2)}) copy-start(f32[8,128]{1,0:T(8,128)} %gate_ref.2) | copy-start | bytes 12292
  1.4 3.9 %collective-permute-start.1 = (bf16[4,128,128]{2,1,0:T(8,128)(2,1)S(1)}, bf16[4,128,128]{2,1,0:T(8,128)(2,1)S(1)}, u32[]{:S(2)}, u32[]{:S(2)}) collective-permute-start(bf16[4,128,128]{2,1,0:T(8,128)(2,1)S(1)} %get-tuple-element.30), channel_id=1, source_target_pairs={{0,4},{1,5},{2,6},{3,7},{16,20},{17,21},{18,22},{19,23}} | collective-permute-start | bytes 393224 | tf_op jit(solution)/shard_map/ppermute | solution.py:400
  2.1 4.1 %collective-permute-start = (bf16[4,128,128]{2,1,0:T(8,128)(2,1)S(1)}, bf16[4,128,128]{2,1,0:T(8,128)(2,1)S(1)}, u32[]{:S(2)}, u32[]{:S(2)}) collective-permute-start(bf16[4,128,128]{2,1,0:T(8,128)(2,1)S(1)} %get-tuple-element.29), channel_id=1, source_target_pairs={{0,4},{1,5},{2,6},{3,7},{16,20},{17,21},{18,22},{19,23}} | collective-permute-start | bytes 393224 | tf_op jit(solution)/shard_map/ppermute | solution.py:400
  2.7 0.7 %copy-start.4 = (s32[128]{0:T(128)S(1)}, s32[128]{0:T(128)}, u32[]{:S(2)}) copy-start(s32[128]{0:T(128)} %param.12) | copy-start | bytes 1540
  2.8 0.7 %copy-start.11 = (f32[128]{0:T(128)S(1)}, f32[128]{0:T(128)}, u32[]{:S(2)}) copy-start(f32[128]{0:T(128)} %param.19) | copy-start | bytes 1540
  4.0 7.2 %collective-permute-start.5 = (bf16[256,128]{1,0:T(8,128)(2,1)S(1)}, bf16[256,128]{1,0:T(8,128)(2,1)S(1)}, u32[]{:S(2)}, u32[]{:S(2)}) collective-permute-start(bf16[256,128]{1,0:T(8,128)(2,1)S(1)} %get-tuple-element.51), channel_id=1, source_target_pairs={{0,4},{4,8},{8,12},{1,5},{5,9},{9,13},{2,6},{6,10},{10,14},{3,7},{... | collective-permute-start | bytes 196616 | tf_op jit(solution)/shard_map/ppermute | solution.py:433
  5.5 8.7 %collective-permute-start.3 = (bf16[4,128,128]{2,1,0:T(8,128)(2,1)S(1)}, bf16[4,128,128]{2,1,0:T(8,128)(2,1)S(1)}, u32[]{:S(2)}, u32[]{:S(2)}) collective-permute-start(bf16[4,128,128]{2,1,0:T(8,128)(2,1)S(1)} %shard_map.133), channel_id=1, source_target_pairs={{4,8},{5,9},{6,10},{7,11},{20,24},{21,25},{22,26},{23,27}} | collective-permute-start | bytes 393224 | tf_op jit(solution)/shard_map/ppermute | solution.py:400
  6.4 9.5 %collective-permute-start.2 = (bf16[4,128,128]{2,1,0:T(8,128)(2,1)S(1)}, bf16[4,128,128]{2,1,0:T(8,128)(2,1)S(1)}, u32[]{:S(2)}, u32[]{:S(2)}) collective-permute-start(bf16[4,128,128]{2,1,0:T(8,128)(2,1)S(1)} %shard_map.134), channel_id=1, source_target_pairs={{4,8},{5,9},{6,10},{7,11},{20,24},{21,25},{22,26},{23,27}} | collective-permute-start | bytes 393224 | tf_op jit(solution)/shard_map/ppermute | solution.py:400
  7.0 5.4 %copy-start.6 = (bf16[128,1024]{1,0:T(8,128)(2,1)S(1)}, bf16[128,1024]{1,0:T(8,128)(2,1)}, u32[]{:S(2)}) copy-start(bf16[128,1024]{1,0:T(8,128)(2,1)} %z_ref.1) | copy-start | bytes 786436
  7.0 5.4 %copy-start.8 = (bf16[128,512]{1,0:T(8,128)(2,1)S(1)}, bf16[128,512]{1,0:T(8,128)(2,1)}, u32[]{:S(2)}) copy-start(bf16[128,512]{1,0:T(8,128)(2,1)} %q_ref.2) | copy-start | bytes 393220
  9.8 8.0 %collective-permute-start.9 = (bf16[256,128]{1,0:T(8,128)(2,1)S(1)}, bf16[256,128]{1,0:T(8,128)(2,1)S(1)}, u32[]{:S(2)}, u32[]{:S(2)}) collective-permute-start(bf16[256,128]{1,0:T(8,128)(2,1)S(1)} %get-tuple-element.51), channel_id=1, source_target_pairs={{0,12},{1,13},{2,14},{3,15},{16,28},{17,29},{18,30},{19,31}} | collective-permute-start | bytes 196616 | tf_op jit(solution)/shard_map/ppermute | solution.py:437
  11.2 7.7 %collective-permute-start.7 = (bf16[256,128]{1,0:T(8,128)(2,1)S(1)}, bf16[256,128]{1,0:T(8,128)(2,1)S(1)}, u32[]{:S(2)}, u32[]{:S(2)}) collective-permute-start(bf16[256,128]{1,0:T(8,128)(2,1)S(1)} %collective-permute-done.5.refs_0_), channel_id=1, source_target_pairs={{4,8},{8,12},{5,9},{9,13},{6,10},{10,14},{7,11},{11,15},{20,24},{2... | collective-permute-start | bytes 196616 | tf_op jit(solution)/shard_map/ppermute | solution.py:447
  14.4 5.9 %copy-start = (bf16[128,1024]{1,0:T(8,128)(2,1)S(1)}, bf16[128,1024]{1,0:T(8,128)(2,1)}, u32[]{:S(2)}) copy-start(bf16[128,1024]{1,0:T(8,128)(2,1)} %q_ref.3) | copy-start | bytes 786436
  14.4 5.9 %copy-start.1 = (bf16[128,1024]{1,0:T(8,128)(2,1)S(1)}, bf16[128,1024]{1,0:T(8,128)(2,1)}, u32[]{:S(2)}) copy-start(bf16[128,1024]{1,0:T(8,128)(2,1)} %gate_ref.3) | copy-start | bytes 786436
  14.4 9.7 %collective-permute-start.11 = (bf16[4,128,128]{2,1,0:T(8,128)(2,1)S(1)}, bf16[4,128,128]{2,1,0:T(8,128)(2,1)S(1)}, u32[]{:S(2)}, u32[]{:S(2)}) collective-permute-start(bf16[4,128,128]{2,1,0:T(8,128)(2,1)S(1)} %shard_map.137), channel_id=1, source_target_pairs={{8,12},{9,13},{10,14},{11,15},{24,28},{25,29},{26,30},{27,31}} | collective-permute-start | bytes 393224 | tf_op jit(solution)/shard_map/ppermute | solution.py:400
  16.1 9.7 %collective-permute-start.4 = (bf16[4,128,128]{2,1,0:T(8,128)(2,1)S(1)}, bf16[4,128,128]{2,1,0:T(8,128)(2,1)S(1)}, u32[]{:S(2)}, u32[]{:S(2)}) collective-permute-start(bf16[4,128,128]{2,1,0:T(8,128)(2,1)S(1)} %shard_map.138), channel_id=1, source_target_pairs={{8,12},{9,13},{10,14},{11,15},{24,28},{25,29},{26,30},{27,31}} | collective-permute-start | bytes 393224 | tf_op jit(solution)/shard_map/ppermute | solution.py:400
  17.9 1.5 %collective-permute-start.10 = (bf16[256,128]{1,0:T(8,128)(2,1)S(1)}, bf16[256,128]{1,0:T(8,128)(2,1)S(1)}, u32[]{:S(2)}, u32[]{:S(2)}) collective-permute-start(bf16[256,128]{1,0:T(8,128)(2,1)S(1)} %collective-permute-done.9.refs_4_), channel_id=1, source_target_pairs={{0,1},{1,0},{2,3},{3,2},{4,5},{5,4},{6,7},{7,6},{8,9},{9,8},{10,11... | collective-permute-start | bytes 196616 | tf_op jit(solution)/shard_map/ppermute | solution.py:422
  18.9 1.3 %collective-permute-start.8 = (bf16[256,128]{1,0:T(8,128)(2,1)S(1)}, bf16[256,128]{1,0:T(8,128)(2,1)S(1)}, u32[]{:S(2)}, u32[]{:S(2)}) collective-permute-start(bf16[256,128]{1,0:T(8,128)(2,1)S(1)} %collective-permute-done.7.refs_2_), channel_id=1, source_target_pairs={{0,1},{1,0},{2,3},{3,2},{4,5},{5,4},{6,7},{7,6},{8,9},{9,8},{10,11... | collective-permute-start | bytes 196616 | tf_op jit(solution)/shard_map/ppermute | solution.py:422
  18.9 1.4 %collective-permute-start.6 = (bf16[256,128]{1,0:T(8,128)(2,1)S(1)}, bf16[256,128]{1,0:T(8,128)(2,1)S(1)}, u32[]{:S(2)}, u32[]{:S(2)}) collective-permute-start(bf16[256,128]{1,0:T(8,128)(2,1)S(1)} %collective-permute-done.5.refs_0_), channel_id=1, source_target_pairs={{0,1},{1,0},{2,3},{3,2},{4,5},{5,4},{6,7},{7,6},{8,9},{9,8},{10,11... | collective-permute-start | bytes 196616 | tf_op jit(solution)/shard_map/ppermute | solution.py:422

commit v7 on v6

--- a/solution.py
+++ b/solution.py
@@ -60,7 +60,7 @@
     return jnp.concatenate([square[i : i + size] for i in range(size, square.shape[0], 2 * size)], axis=0)
 
 
-def state_terms(scalar_ref, inputs, u_ref, w_ref=None, a_ref=None, m_ref=None, send_refs=()):
+def state_terms(scalar_ref, inputs, u_ref, w_ref=None, a_ref=None, m_ref=None, send_refs=(), late=()):
     k_ref, gate_ref, beta_ref, doc_ref, v_ref = inputs
     doc = doc_ref[...]
     anchor = scalar_ref[0]
@@ -134,6 +134,8 @@
         ]
         level += 1
     keys_t = [k.astype(F32).T for k in keys]
+    for copy in late:
+        copy.wait()
     for h in range(heads):
         g = h // repeat
         run = running[h : h + 1, :]
@@ -163,9 +165,9 @@
         copies = [pltpu.make_async_copy(a, b, sems.at[i]) for i, (a, b) in enumerate(zip(sources, inputs))]
         for copy in copies:
             copy.start()
-        for copy in copies:
+        for copy in copies[:-1]:
             copy.wait()
-        state_terms(scalar_ref, inputs, u_ref, send_refs=send_refs)
+        state_terms(scalar_ref, inputs, u_ref, send_refs=send_refs, late=copies[-1:])
 
 
 def second_kernel(scalar_ref, *refs):

time: 27.1 us -> 27.1 us (level)
  no operation moved by 1% of the time
where the time goes in v7:
time: 27.1 us; the launch traced here: 26.7 us
  starting transfers between devices  9.78 us (36%)
  Pallas kernels  9.05 us (33%)
  waiting for transfers between devices  6.2 us (23%)
  between operations  0.99 us (4%)
  local copies, waits for them, and re-layouts  0.65 us (2%)
    pallas_call x11, Pallas kernels, call(): pl.pallas_call(kernel, out_shape=out_shape, in_specs=specs, out_specs=jax...  9.05 us
    ppermute x6, starting transfers between devices, hand_on(): return [lax.ppermute(s, 'seq', [(hop, hop + 1)]) for s in pieces_out]  5.39 us
    ppermute x6, waiting for transfers between devices, hand_on(): return [lax.ppermute(s, 'seq', [(hop, hop + 1)]) for s in pieces_out]  3.78 us
    ppermute x1, starting transfers between devices, shards(): lax.ppermute(unit, 'seq', [(i, i + 1) for i in range(devices - 1)])  1.29 us
    ppermute x1, starting transfers between devices, shards(): lax.ppermute(after(unit, leaving[-1]), 'seq', [(0, wanted)])  1.29 us
    ppermute x1, starting transfers between devices, shards(): lax.ppermute(block, 'seq', [(i, i + 1) for i in range(distance - 1, devic...  1.29 us
    ppermute x1, waiting for transfers between devices, shards(): lax.ppermute(block, 'seq', [(i, i + 1) for i in range(distance - 1, devic...  0.99 us
    ppermute x3, waiting for transfers between devices, swapped(): return lax.ppermute(got, 'head', pairs)  0.9 us
  transfers between devices with their start and end apart: 12, of which 6 were waited for; matrix products, arithmetic and copies ran while one was open for 0% of the time, Pallas kernels for 28%

profile of v7, /device:TPU:26, one launch (start us, length us, event | category | flops | bytes accessed | tf_op | source)
XLA Modules:
  0.0 26.7 jit_solution(8249309179370889490)
XLA Ops:
  0.7 0.1 pad_add_fusion.scalar_ref
  0.8 0.0 copy-start.10
  0.8 0.6 %shard_map.131 = (bf16[8,128,128]{2,1,0:T(8,128)(2,1)S(1)}, bf16[4,128,128]{2,1,0:T(8,128)(2,1)S(1)}, bf16[4,128,128]{2,1,0:T(8,128)(2,1)S(1)}) custom-call(s32[4]{0:T(128)S(1)} %pad_add_fusion.scalar_ref, bf16[128,512]{1,0:T(8,128)(2,1)} %k_ref.2, f32[8,128]{1,0:T(8,128)} %gate_ref.2, f32[8,128]{1,0:T(8,128)} %beta_ref.1, s32[1,128]{1,0:T(1,128)} %bitcast.6, ...), custom_call_target="tpu_custom_call" | custom-call | flops 1677721600 | bytes 401936 | tf_op jit(solution)/shard_map/pallas_call | solution.py:332
  1.4 0.0 copy-start.9
  1.4 0.7 %collective-permute-start.1 = (bf16[4,128,128]{2,1,0:T(8,128)(2,1)S(1)}, bf16[4,128,128]{2,1,0:T(8,128)(2,1)S(1)}, u32[]{:S(2)}, u32[]{:S(2)}) collective-permute-start(bf16[4,128,128]{2,1,0:T(8,128)(2,1)S(1)} %get-tuple-element.30), channel_id=1, source_target_pairs={{0,4},{1,5},{2,6},{3,7},{16,20},{17,21},{18,22},{19,23}} | collective-permute-start | bytes 393224 | tf_op jit(solution)/shard_map/ppermute | solution.py:402
  2.1 0.7 %collective-permute-start = (bf16[4,128,128]{2,1,0:T(8,128)(2,1)S(1)}, bf16[4,128,128]{2,1,0:T(8,128)(2,1)S(1)}, u32[]{:S(2)}, u32[]{:S(2)}) collective-permute-start(bf16[4,128,128]{2,1,0:T(8,128)(2,1)S(1)} %get-tuple-element.29), channel_id=1, source_target_pairs={{0,4},{1,5},{2,6},{3,7},{16,20},{17,21},{18,22},{19,23}} | collective-permute-start | bytes 393224 | tf_op jit(solution)/shard_map/ppermute | solution.py:402
  2.7 0.0 copy-start.4
  2.8 0.0 copy-start.11
  2.8 0.0 copy-done.2
  2.8 0.6 %copy-done.4 = s32[128]{0:T(128)S(1)} copy-done((s32[128]{0:T(128)S(1)}, s32[128]{0:T(128)}, u32[]{:S(2)}) %copy-start.4) | copy-done | bytes 536
  3.4 0.0 copy-done.11
  3.4 0.6 %shard_map.132 = (bf16[8,128,128]{2,1,0:T(8,128)(2,1)S(1)}, bf16[8,128,128]{2,1,0:T(8,128)(2,1)S(1)}, f32[8,128,128]{2,1,0:T(8,128)S(1)}, bf16[8,128,128]{2,1,0:...) custom-call(s32[4]{0:T(128)S(1)} %pad_add_fusion.scalar_ref, ...), custom_call_target="tpu_custom_call", output_to_operand_aliasing={{0}: (9, {})} | custom-call | flops 1677721600 | bytes 926736 | tf_op jit(solution)/shard_map/pallas_call | solution.py:332
  4.0 1.3 %collective-permute-start.5 = (bf16[256,128]{1,0:T(8,128)(2,1)S(1)}, bf16[256,128]{1,0:T(8,128)(2,1)S(1)}, u32[]{:S(2)}, u32[]{:S(2)}) collective-permute-start(bf16[256,128]{1,0:T(8,128)(2,1)S(1)} %get-tuple-element.51), channel_id=1, source_target_pairs={{0,4},{4,8},{8,12},{1,5},{5,9},{9,13},{2,6},{6,10},{10,14},{3,7},{... | collective-permute-start | bytes 196616 | tf_op jit(solution)/shard_map/ppermute | solution.py:435
  5.3 0.0 collective-permute-done.1.s_ref.refs_0_
  5.3 0.2 shard_map.133
  5.5 0.7 %collective-permute-start.3 = (bf16[4,128,128]{2,1,0:T(8,128)(2,1)S(1)}, bf16[4,128,128]{2,1,0:T(8,128)(2,1)S(1)}, u32[]{:S(2)}, u32[]{:S(2)}) collective-permute-start(bf16[4,128,128]{2,1,0:T(8,128)(2,1)S(1)} %shard_map.133), channel_id=1, source_target_pairs={{4,8},{5,9},{6,10},{7,11},{20,24},{21,25},{22,26},{23,27}} | collective-permute-start | bytes 393224 | tf_op jit(solution)/shard_map/ppermute | solution.py:402
  6.2 0.0 collective-permute-done.s_ref.refs_0_
  6.2 0.2 shard_map.134
  6.4 0.7 %collective-permute-start.2 = (bf16[4,128,128]{2,1,0:T(8,128)(2,1)S(1)}, bf16[4,128,128]{2,1,0:T(8,128)(2,1)S(1)}, u32[]{:S(2)}, u32[]{:S(2)}) collective-permute-start(bf16[4,128,128]{2,1,0:T(8,128)(2,1)S(1)} %shard_map.134), channel_id=1, source_target_pairs={{4,8},{5,9},{6,10},{7,11},{20,24},{21,25},{22,26},{23,27}} | collective-permute-start | bytes 393224 | tf_op jit(solution)/shard_map/ppermute | solution.py:402
  7.0 0.0 copy-start.6
  7.0 0.0 copy-start.8
  7.1 2.8 %shard_map.135 = (bf16[8,128,128]{2,1,0:T(8,128)(2,1)S(1)}, bf16[8,128,128]{2,1,0:T(8,128)(2,1)S(1)}, f32[8,128,128]{2,1,0:T(8,128)S(1)}, bf16[8,128,128]{2,1,0:T(8,128)(2,1)S(1)}) custom-call(s32[4]{0:T(128)S(1)} %pad_add_fusion.scalar_ref, bf16[128,512]{1,0:T(8,128)(2,1)S(1)} %copy-done.7, ...), custom_call_target="tpu_custom_call", output_to_operand_aliasing={{0}: (6, {}), {1}: (7, {}), {2}: (8, {}), {3}: (9, {})} | custom-call | flops 1677721600 | bytes 1712656 | tf_op jit(solution)/shard_map/pallas_call | solution.py:332
  9.8 1.3 %collective-permute-start.9 = (bf16[256,128]{1,0:T(8,128)(2,1)S(1)}, bf16[256,128]{1,0:T(8,128)(2,1)S(1)}, u32[]{:S(2)}, u32[]{:S(2)}) collective-permute-start(bf16[256,128]{1,0:T(8,128)(2,1)S(1)} %get-tuple-element.51), channel_id=1, source_target_pairs={{0,12},{1,13},{2,14},{3,15},{16,28},{17,29},{18,30},{19,31}} | collective-permute-start | bytes 196616 | tf_op jit(solution)/shard_map/ppermute | solution.py:439
  11.1 0.0 collective-permute-done.5.refs_0_
  11.2 1.3 %collective-permute-start.7 = (bf16[256,128]{1,0:T(8,128)(2,1)S(1)}, bf16[256,128]{1,0:T(8,128)(2,1)S(1)}, u32[]{:S(2)}, u32[]{:S(2)}) collective-permute-start(bf16[256,128]{1,0:T(8,128)(2,1)S(1)} %collective-permute-done.5.refs_0_), channel_id=1, source_target_pairs={{4,8},{8,12},{5,9},{9,13},{6,10},{10,14},{7,11},{11,15},{20,24},{2... | collective-permute-start | bytes 196616 | tf_op jit(solution)/shard_map/ppermute | solution.py:449
  12.5 1.7 %shard_map.136 = (f32[8,128,128]{2,1,0:T(8,128)S(1)}, bf16[8,128,128]{2,1,0:T(8,128)(2,1)S(1)}, f32[8,128,128]{2,1,0:T(8,128)S(1)}) custom-call(s32[4]{0:T(128)S(1)} %pad_add_fusion.scalar_ref, s32[1,128]{1,0:T(1,128)S(1)} %bitcast.9, f32[8,128]{1,0:T(8,128)S(1)} %copy-done.10, f32[8,128]{1,0:T(8,128)S(1)} %copy-done.9, bf16[128,512]{1,0:T(8,128)(2,1)S(1)} %copy-done.8, ...), custom_call_target="tpu_custom_call" | custom-call | flops 1677721600 | bytes 1057808 | tf_op jit(solution)/shard_map/pallas_call | solution.py:332
  14.2 0.0 collective-permute-done.3.s_ref.refs_1_
  14.2 0.2 shard_map.137
  14.4 0.0 copy-start
  14.4 0.0 copy-start.1
  14.4 1.4 %collective-permute-start.11 = (bf16[4,128,128]{2,1,0:T(8,128)(2,1)S(1)}, bf16[4,128,128]{2,1,0:T(8,128)(2,1)S(1)}, u32[]{:S(2)}, u32[]{:S(2)}) collective-permute-start(bf16[4,128,128]{2,1,0:T(8,128)(2,1)S(1)} %shard_map.137), channel_id=1, source_target_pairs={{8,12},{9,13},{10,14},{11,15},{24,28},{25,29},{26,30},{27,31}} | collective-permute-start | bytes 393224 | tf_op jit(solution)/shard_map/ppermute | solution.py:402
  15.9 0.0 collective-permute-done.2.s_ref.refs_1_
  15.9 0.2 shard_map.138
  16.1 1.3 %collective-permute-start.4 = (bf16[4,128,128]{2,1,0:T(8,128)(2,1)S(1)}, bf16[4,128,128]{2,1,0:T(8,128)(2,1)S(1)}, u32[]{:S(2)}, u32[]{:S(2)}) collective-permute-start(bf16[4,128,128]{2,1,0:T(8,128)(2,1)S(1)} %shard_map.138), channel_id=1, source_target_pairs={{8,12},{9,13},{10,14},{11,15},{24,28},{25,29},{26,30},{27,31}} | collective-permute-start | bytes 393224 | tf_op jit(solution)/shard_map/ppermute | solution.py:402
  17.4 0.5 %collective-permute-done.9.refs_4_ = bf16[256,128]{1,0:T(8,128)(2,1)S(1)} collective-permute-done((bf16[256,128]{1,0:T(8,128)(2,1)S(1)}, bf16[256,128]{1,0:T(8,128)(2,1)S(1)}, u32[]{:S(2)}, u32[]{:S(2)}) %collective-permute-start.9) | collective-permute-done | bytes 65568 | tf_op jit(solution)/shard_map/ppermute | solution.py:439
  17.9 0.0 collective-permute-start.10
  17.9 1.0 %collective-permute-done.7.refs_2_ = bf16[256,128]{1,0:T(8,128)(2,1)S(1)} collective-permute-done((bf16[256,128]{1,0:T(8,128)(2,1)S(1)}, bf16[256,128]{1,0:T(8,128)(2,1)S(1)}, u32[]{:S(2)}, u32[]{:S(2)}) %collective-permute-start.7) | collective-permute-done | bytes 65568 | tf_op jit(solution)/shard_map/ppermute | solution.py:449
  18.9 0.0 collective-permute-start.8
  18.9 0.5 %collective-permute-start.6 = (bf16[256,128]{1,0:T(8,128)(2,1)S(1)}, bf16[256,128]{1,0:T(8,128)(2,1)S(1)}, u32[]{:S(2)}, u32[]{:S(2)}) collective-permute-start(bf16[256,128]{1,0:T(8,128)(2,1)S(1)} %collective-permute-done.5.refs_0_), channel_id=1, source_target_pairs={{0,1},{1,0},{2,3},{3,2},{4,5},{5,4},{6,7},{7,6},{8,9},{9,8},{10,11... | collective-permute-start | bytes 196616 | tf_op jit(solution)/shard_map/ppermute | solution.py:424
  19.4 0.0 collective-permute-done.10.refs_5_
  19.4 0.7 %collective-permute-done.8.refs_3_ = bf16[256,128]{1,0:T(8,128)(2,1)S(1)} collective-permute-done((bf16[256,128]{1,0:T(8,128)(2,1)S(1)}, bf16[256,128]{1,0:T(8,128)(2,1)S(1)}, u32[]{:S(2)}, u32[]{:S(2)}) %collective-permute-start.8) | collective-permute-done | bytes 65568 | tf_op jit(solution)/shard_map/ppermute | solution.py:424
  20.1 0.2 collective-permute-done.6.refs_1_
  20.3 0.0 copy-done.1
  20.3 1.4 %shard_map.139.refs_6_ = bf16[128,1024]{1,0:T(8,128)(2,1)S(1)} custom-call(s32[4]{0:T(128)S(1)} %pad_add_fusion.scalar_ref, s32[1,128]{1,0:T(1,128)S(1)} %bitcast.10, bf16[128,1024]{1,0:T(8,128)(2,1)S(1)} %copy-done, bf16[128,1024]{1,0:T(8,128)(2,1)S(1)} %copy-done.1, bf16[128,512]{1,0:T(8,128)(2,1)S(1)} %copy-done.2, bf16[128,512]{1,0:T(8,128)(2,1)S(1)} %copy-done.3, ...), custom_call_target="tpu_custom_call" | custom-call | flops 268435456 | bytes 1180176 | tf_op jit(solution)/shard_map/pallas_call | solution.py:332
  21.7 2.4 %collective-permute-done.11.refs_2_ = bf16[4,128,128]{2,1,0:T(8,128)(2,1)S(1)} collective-permute-done((bf16[4,128,128]{2,1,0:T(8,128)(2,1)S(1)}, bf16[4,128,128]{2,1,0:T(8,128)(2,1)S(1)}, u32[]{:S(2)}, u32[]{:S(2)}) %collective-permute-start.11) | collective-permute-done | bytes 131104 | tf_op jit(solution)/shard_map/ppermute | solution.py:402
  24.1 0.3 %shard_map.140.refs_7_ = bf16[128,512]{1,0:T(8,128)(2,1)S(1)} custom-call(bf16[4,128,128]{2,1,0:T(8,128)(2,1)S(1)} %collective-permute-done.1.s_ref.refs_0_, bf16[4,128,128]{2,1,0:T(8,128)(2,1)S(1)} %collective-permute-done.3.s_ref.refs_1_, bf16[4,128,128]{2,1,0:T(8,128)(2,1)S(1)} %collective-permute-done.11.refs_2_, ...), custom_call_target="tpu_custom_call" | custom-call | flops 16777216 | bytes 1703936 | tf_op jit(solution)/shard_map/pallas_call | solution.py:332
  24.4 1.3 %collective-permute-done.4.refs_2_ = bf16[4,128,128]{2,1,0:T(8,128)(2,1)S(1)} collective-permute-done((bf16[4,128,128]{2,1,0:T(8,128)(2,1)S(1)}, bf16[4,128,128]{2,1,0:T(8,128)(2,1)S(1)}, u32[]{:S(2)}, u32[]{:S(2)}) %collective-permute-start.4) | collective-permute-done | bytes 131104 | tf_op jit(solution)/shard_map/ppermute | solution.py:402
  25.8 1.0 %shard_map.141 = (bf16[128,1024]{1,0:T(8,128)(2,1)}, bf16[128,1024]{1,0:T(8,128)(2,1)}) custom-call(bf16[4,128,128]{2,1,0:T(8,128)(2,1)S(1)} %collective-permute-done.s_ref.refs_0_, bf16[4,128,128]{2,1,0:T(8,128)(2,1)S(1)} %collective-permute-done.2.s_ref.refs_1_, bf16[4,128,128]{2,1,0:T(8,128)(2,1)S(1)} %collective-permute-done.4.refs_2_, ...), custom_call_target="tpu_custom_call" | custom-call | flops 16777216 | bytes 2097152 | tf_op jit(solution)/shard_map/pallas_call | solution.py:332
  (12 shorter events, 0.0 us)
Async XLA Ops:
  0.7 2.0 %copy-start.2 = (bf16[128,512]{1,0:T(8,128)(2,1)S(1)}, bf16[128,512]{1,0:T(8,128)(2,1)}, u32[]{:S(2)}) copy-start(bf16[128,512]{1,0:T(8,128)(2,1)} %k_ref.3) | copy-start | bytes 393220
  0.7 2.0 %copy-start.3 = (bf16[128,512]{1,0:T(8,128)(2,1)S(1)}, bf16[128,512]{1,0:T(8,128)(2,1)}, u32[]{:S(2)}) copy-start(bf16[128,512]{1,0:T(8,128)(2,1)} %v_ref.1) | copy-start | bytes 393220
  0.7 2.0 %copy-start.5 = (bf16[128,1024]{1,0:T(8,128)(2,1)S(1)}, bf16[128,1024]{1,0:T(8,128)(2,1)}, u32[]{:S(2)}) copy-start(bf16[128,1024]{1,0:T(8,128)(2,1)} %refs_4_.5) | copy-start | bytes 786436
  0.7 2.0 %copy-start.7 = (bf16[128,512]{1,0:T(8,128)(2,1)S(1)}, bf16[128,512]{1,0:T(8,128)(2,1)}, u32[]{:S(2)}) copy-start(bf16[128,512]{1,0:T(8,128)(2,1)} %k_ref.2) | copy-start | bytes 393220
  0.8 2.0 %copy-start.10 = (f32[8,128]{1,0:T(8,128)S(1)}, f32[8,128]{1,0:T(8,128)}, u32[]{:S(2)}) copy-start(f32[8,128]{1,0:T(8,128)} %beta_ref.1) | copy-start | bytes 12292
  1.4 1.4 %copy-start.9 = (f32[8,128]{1,0:T(8,128)S(1)}, f32[8,128]{1,0:T(8,128)}, u32[]{:S(2)}) copy-start(f32[8,128]{1,0:T(8,128)} %gate_ref.2) | copy-start | bytes 12292
  1.4 3.9 %collective-permute-start.1 = (bf16[4,128,128]{2,1,0:T(8,128)(2,1)S(1)}, bf16[4,128,128]{2,1,0:T(8,128)(2,1)S(1)}, u32[]{:S(2)}, u32[]{:S(2)}) collective-permute-start(bf16[4,128,128]{2,1,0:T(8,128)(2,1)S(1)} %get-tuple-element.30), channel_id=1, source_target_pairs={{0,4},{1,5},{2,6},{3,7},{16,20},{17,21},{18,22},{19,23}} | collective-permute-start | bytes 393224 | tf_op jit(solution)/shard_map/ppermute | solution.py:402
  2.1 4.1 %collective-permute-start = (bf16[4,128,128]{2,1,0:T(8,128)(2,1)S(1)}, bf16[4,128,128]{2,1,0:T(8,128)(2,1)S(1)}, u32[]{:S(2)}, u32[]{:S(2)}) collective-permute-start(bf16[4,128,128]{2,1,0:T(8,128)(2,1)S(1)} %get-tuple-element.29), channel_id=1, source_target_pairs={{0,4},{1,5},{2,6},{3,7},{16,20},{17,21},{18,22},{19,23}} | collective-permute-start | bytes 393224 | tf_op jit(solution)/shard_map/ppermute | solution.py:402
  2.7 0.7 %copy-start.4 = (s32[128]{0:T(128)S(1)}, s32[128]{0:T(128)}, u32[]{:S(2)}) copy-start(s32[128]{0:T(128)} %param.12) | copy-start | bytes 1540
  2.8 0.7 %copy-start.11 = (f32[128]{0:T(128)S(1)}, f32[128]{0:T(128)}, u32[]{:S(2)}) copy-start(f32[128]{0:T(128)} %param.19) | copy-start | bytes 1540
  4.0 7.2 %collective-permute-start.5 = (bf16[256,128]{1,0:T(8,128)(2,1)S(1)}, bf16[256,128]{1,0:T(8,128)(2,1)S(1)}, u32[]{:S(2)}, u32[]{:S(2)}) collective-permute-start(bf16[256,128]{1,0:T(8,128)(2,1)S(1)} %get-tuple-element.51), channel_id=1, source_target_pairs={{0,4},{4,8},{8,12},{1,5},{5,9},{9,13},{2,6},{6,10},{10,14},{3,7},{... | collective-permute-start | bytes 196616 | tf_op jit(solution)/shard_map/ppermute | solution.py:435
  5.5 8.7 %collective-permute-start.3 = (bf16[4,128,128]{2,1,0:T(8,128)(2,1)S(1)}, bf16[4,128,128]{2,1,0:T(8,128)(2,1)S(1)}, u32[]{:S(2)}, u32[]{:S(2)}) collective-permute-start(bf16[4,128,128]{2,1,0:T(8,128)(2,1)S(1)} %shard_map.133), channel_id=1, source_target_pairs={{4,8},{5,9},{6,10},{7,11},{20,24},{21,25},{22,26},{23,27}} | collective-permute-start | bytes 393224 | tf_op jit(solution)/shard_map/ppermute | solution.py:402
  6.4 9.5 %collective-permute-start.2 = (bf16[4,128,128]{2,1,0:T(8,128)(2,1)S(1)}, bf16[4,128,128]{2,1,0:T(8,128)(2,1)S(1)}, u32[]{:S(2)}, u32[]{:S(2)}) collective-permute-start(bf16[4,128,128]{2,1,0:T(8,128)(2,1)S(1)} %shard_map.134), channel_id=1, source_target_pairs={{4,8},{5,9},{6,10},{7,11},{20,24},{21,25},{22,26},{23,27}} | collective-permute-start | bytes 393224 | tf_op jit(solution)/shard_map/ppermute | solution.py:402
  7.0 5.4 %copy-start.6 = (bf16[128,1024]{1,0:T(8,128)(2,1)S(1)}, bf16[128,1024]{1,0:T(8,128)(2,1)}, u32[]{:S(2)}) copy-start(bf16[128,1024]{1,0:T(8,128)(2,1)} %z_ref.1) | copy-start | bytes 786436
  7.0 5.4 %copy-start.8 = (bf16[128,512]{1,0:T(8,128)(2,1)S(1)}, bf16[128,512]{1,0:T(8,128)(2,1)}, u32[]{:S(2)}) copy-start(bf16[128,512]{1,0:T(8,128)(2,1)} %q_ref.2) | copy-start | bytes 393220
  9.8 8.0 %collective-permute-start.9 = (bf16[256,128]{1,0:T(8,128)(2,1)S(1)}, bf16[256,128]{1,0:T(8,128)(2,1)S(1)}, u32[]{:S(2)}, u32[]{:S(2)}) collective-permute-start(bf16[256,128]{1,0:T(8,128)(2,1)S(1)} %get-tuple-element.51), channel_id=1, source_target_pairs={{0,12},{1,13},{2,14},{3,15},{16,28},{17,29},{18,30},{19,31}} | collective-permute-start | bytes 196616 | tf_op jit(solution)/shard_map/ppermute | solution.py:439
  11.2 7.7 %collective-permute-start.7 = (bf16[256,128]{1,0:T(8,128)(2,1)S(1)}, bf16[256,128]{1,0:T(8,128)(2,1)S(1)}, u32[]{:S(2)}, u32[]{:S(2)}) collective-permute-start(bf16[256,128]{1,0:T(8,128)(2,1)S(1)} %collective-permute-done.5.refs_0_), channel_id=1, source_target_pairs={{4,8},{8,12},{5,9},{9,13},{6,10},{10,14},{7,11},{11,15},{20,24},{2... | collective-permute-start | bytes 196616 | tf_op jit(solution)/shard_map/ppermute | solution.py:449
  14.4 5.9 %copy-start = (bf16[128,1024]{1,0:T(8,128)(2,1)S(1)}, bf16[128,1024]{1,0:T(8,128)(2,1)}, u32[]{:S(2)}) copy-start(bf16[128,1024]{1,0:T(8,128)(2,1)} %q_ref.3) | copy-start | bytes 786436
  14.4 5.9 %copy-start.1 = (bf16[128,1024]{1,0:T(8,128)(2,1)S(1)}, bf16[128,1024]{1,0:T(8,128)(2,1)}, u32[]{:S(2)}) copy-start(bf16[128,1024]{1,0:T(8,128)(2,1)} %gate_ref.3) | copy-start | bytes 786436
  14.4 9.7 %collective-permute-start.11 = (bf16[4,128,128]{2,1,0:T(8,128)(2,1)S(1)}, bf16[4,128,128]{2,1,0:T(8,128)(2,1)S(1)}, u32[]{:S(2)}, u32[]{:S(2)}) collective-permute-start(bf16[4,128,128]{2,1,0:T(8,128)(2,1)S(1)} %shard_map.137), channel_id=1, source_target_pairs={{8,12},{9,13},{10,14},{11,15},{24,28},{25,29},{26,30},{27,31}} | collective-permute-start | bytes 393224 | tf_op jit(solution)/shard_map/ppermute | solution.py:402
  16.1 9.7 %collective-permute-start.4 = (bf16[4,128,128]{2,1,0:T(8,128)(2,1)S(1)}, bf16[4,128,128]{2,1,0:T(8,128)(2,1)S(1)}, u32[]{:S(2)}, u32[]{:S(2)}) collective-permute-start(bf16[4,128,128]{2,1,0:T(8,128)(2,1)S(1)} %shard_map.138), channel_id=1, source_target_pairs={{8,12},{9,13},{10,14},{11,15},{24,28},{25,29},{26,30},{27,31}} | collective-permute-start | bytes 393224 | tf_op jit(solution)/shard_map/ppermute | solution.py:402
  17.9 1.5 %collective-permute-start.10 = (bf16[256,128]{1,0:T(8,128)(2,1)S(1)}, bf16[256,128]{1,0:T(8,128)(2,1)S(1)}, u32[]{:S(2)}, u32[]{:S(2)}) collective-permute-start(bf16[256,128]{1,0:T(8,128)(2,1)S(1)} %collective-permute-done.9.refs_4_), channel_id=1, source_target_pairs={{0,1},{1,0},{2,3},{3,2},{4,5},{5,4},{6,7},{7,6},{8,9},{9,8},{10,11... | collective-permute-start | bytes 196616 | tf_op jit(solution)/shard_map/ppermute | solution.py:424
  18.9 1.3 %collective-permute-start.8 = (bf16[256,128]{1,0:T(8,128)(2,1)S(1)}, bf16[256,128]{1,0:T(8,128)(2,1)S(1)}, u32[]{:S(2)}, u32[]{:S(2)}) collective-permute-start(bf16[256,128]{1,0:T(8,128)(2,1)S(1)} %collective-permute-done.7.refs_2_), channel_id=1, source_target_pairs={{0,1},{1,0},{2,3},{3,2},{4,5},{5,4},{6,7},{7,6},{8,9},{9,8},{10,11... | collective-permute-start | bytes 196616 | tf_op jit(solution)/shard_map/ppermute | solution.py:424
  18.9 1.4 %collective-permute-start.6 = (bf16[256,128]{1,0:T(8,128)(2,1)S(1)}, bf16[256,128]{1,0:T(8,128)(2,1)S(1)}, u32[]{:S(2)}, u32[]{:S(2)}) collective-permute-start(bf16[256,128]{1,0:T(8,128)(2,1)S(1)} %collective-permute-done.5.refs_0_), channel_id=1, source_target_pairs={{0,1},{1,0},{2,3},{3,2},{4,5},{5,4},{6,7},{7,6},{8,9},{9,8},{10,11... | collective-permute-start | bytes 196616 | tf_op jit(solution)/shard_map/ppermute | solution.py:424
